TPU v7x, 32 devices: a whole 2x2x4 slice. The times are simulated.
32 devices in a mesh: fsdp: 8 (over z, y), frame: 4 (over x, core).
Axes of the slice: x: 2, y: 2, z: 4, core: 2. Of those that a mesh axis runs over, the one named last changes fastest.
Arguments:
- latents: bfloat16 [2, 8, 8, 128, 16], P(None, 'fsdp', 'frame'), may hold values from -6 to 6
- added_noise: bfloat16 [2, 8, 8, 128, 16], P(None, 'fsdp', 'frame'), may hold values from -6 to 6
- text_states: bfloat16 [2, 8, 64, 4096], P(None, 'fsdp'), may hold values from -1.75 to 1.75
- timesteps: int32 [2, 8], P(None, 'fsdp'), may hold values from 1 to 999
- token_counts: int32 [2, 8], P(None, 'fsdp'), may hold values from 26 to 128, as said below
- frame_counts: int32 [2, 8, 3], P(None, 'fsdp'), may hold values from 1 to 5, 8 in all within a row
- w_shared: float32 [1152, 12448], P('fsdp'), may hold values from -0.1875 to 0.1875
- w_spatial: float32 [1152, 18432], P('fsdp'), may hold values from -0.1875 to 0.1875
- w_temporal: float32 [1152, 13824], P('fsdp'), may hold values from -0.1875 to 0.1875
- shift_tables: float32 [1152, 14], P('fsdp'), may hold values from -3 to 3
- m_shared: float32 [1152, 12448], P('fsdp'), may hold values from -9.536743e-07 to 9.536743e-07
- m_spatial: float32 [1152, 18432], P('fsdp'), may hold values from -9.536743e-07 to 9.536743e-07
- m_temporal: float32 [1152, 13824], P('fsdp'), may hold values from -9.536743e-07 to 9.536743e-07
- m_tables: float32 [1152, 14], P('fsdp'), may hold values from -9.536743e-07 to 9.536743e-07
- v_shared: float32 [1152, 12448], P('fsdp'), may hold values from 1.941177e-15 to 7.764708e-15
- v_spatial: float32 [1152, 18432], P('fsdp'), may hold values from 1.941177e-15 to 7.764708e-15
- v_temporal: float32 [1152, 13824], P('fsdp'), may hold values from 1.941177e-15 to 7.764708e-15
- v_tables: float32 [1152, 14], P('fsdp'), may hold values from 1.941177e-15 to 7.764708e-15
Outputs:
- loss_sum: float32 [], replicated
- weight_total: float32 [], replicated
- grad_norm: float32 [], replicated
- matrix_norms: float32 [2, 18], replicated
- clipped_norms: float32 [18], replicated
- new_shared: float32 [1152, 12448], P('fsdp')
- new_spatial: float32 [1152, 18432], P('fsdp')
- new_temporal: float32 [1152, 13824], P('fsdp')
- new_tables: float32 [1152, 14], P('fsdp')
- first_shared: float32 [1152, 12448], P('fsdp')
- first_spatial: float32 [1152, 18432], P('fsdp')
- first_temporal: float32 [1152, 13824], P('fsdp')
- first_tables: float32 [1152, 14], P('fsdp')
- second_shared: float32 [1152, 12448], P('fsdp')
- second_spatial: float32 [1152, 18432], P('fsdp')
- second_temporal: float32 [1152, 13824], P('fsdp')
- second_tables: float32 [1152, 14], P('fsdp')
- copy_shared: bfloat16 [1152, 12448], P('fsdp')
- copy_spatial: bfloat16 [1152, 18432], P('fsdp')
- copy_temporal: bfloat16 [1152, 13824], P('fsdp')
- copy_tables: bfloat16 [1152, 14], P('fsdp')
Inputs may be any that keep to these rules, and one draw needn't show every extreme that they name: `token_counts`: valid patch tokens of each frame of a video; the rest of its 128 rows are padding. `frame_counts`: frames of the clips packed into a video, in order; they sum to 8.
All inputs are finite; a program needn't handle non-finite values.
Results may differ from a plain program's by a relative error of at most 0.0088.
Values may be sent and summed in bfloat16 or wider, within the bound.
No kernel may reach another device: no remote copies, remote signals or barrier semaphores. Data moves between devices by JAX's collectives and lax.ppermute only.
A program may use at most 768 MiB of HBM per device.

v0:
```python
import math

import jax
import jax.numpy as jnp
from jax import lax
from jax.sharding import PartitionSpec as P

D = 1152
HEADS = 16
HEAD_DIM = 72
FF = 4608
TXT_D = 4096
FREQ = 256
PCH = 16
STEP = 10


CLIP_NORM = 0.01
LEARN_RATE = 0.3
BETA_ONE = 0.9
BETA_TWO = 0.999
ADAM_EPS = 1e-06
DECAY_RATE = 0.01
SNR_GAMMA = 5.0
NORM_EPS = 1e-06


def for_sending(shard):
    return jax.tree.map(lambda a: a.astype(jnp.bfloat16) if a.dtype == jnp.float32 else a, shard)


def layer_norm(values):
    centered = values - jnp.mean(values, axis=-1, keepdims=True)
    return centered * lax.rsqrt(jnp.mean(centered * centered, axis=-1, keepdims=True) + NORM_EPS)


def modulate(residual, shift_by, scale_by):
    return layer_norm(residual) * (1.0 + scale_by) + shift_by


def gelu_tanh(values):
    return jax.nn.gelu(values, approximate=True)


def split_heads(values):
    return values.reshape(values.shape[:-1] + (HEADS, HEAD_DIM))


def join_heads(values):
    return values.reshape(values.shape[:-2] + (HEADS * HEAD_DIM,))


def shared_widths():
    return (PCH, FREQ, TXT_D, D, 6 * D, PCH)


def spatial_widths():
    return (3 * D, D, D, 2 * D, D, FF, FF)


def temporal_widths():
    return (3 * D, D, FF, FF)


def split_columns(weight, widths):
    pieces = []
    offset = 0
    for column_count in widths:
        pieces.append(weight[:, offset : offset + column_count])
        offset += column_count
    return pieces


def spread_columns(values, widths):
    return jnp.concatenate(
        [
            jnp.full((column_count,), values[position])
            for position, column_count in enumerate(widths)
        ]
    )


def matrix_squares(arrays):
    totals = []
    for array_one, widths in zip(
        arrays[:3], (shared_widths(), spatial_widths(), temporal_widths())
    ):
        for column_block in split_columns(array_one, widths):
            totals.append(jnp.sum(column_block * column_block))
    totals.append(jnp.sum(arrays[3] * arrays[3]))
    return jnp.stack(totals)


def linear(inputs, weight):
    return jnp.matmul(inputs.astype(jnp.bfloat16), weight, preferred_element_type=jnp.float32)


def linear_back(inputs, weight, grad_out):
    grad_low = grad_out.astype(jnp.bfloat16)
    grad_in = jnp.matmul(grad_low, weight.T, preferred_element_type=jnp.float32)
    rows_in = inputs.reshape(-1, inputs.shape[-1]).astype(jnp.bfloat16)
    grad_weight = jnp.dot(
        rows_in.T, grad_low.reshape(-1, grad_low.shape[-1]), preferred_element_type=jnp.float32
    )
    return (grad_in, grad_weight)


def attend_forward(query_heads, key_heads, value_heads, allowed):
    scores = jnp.einsum(
        "...qhd,...khd->...hqk", query_heads, key_heads, preferred_element_type=jnp.float32
    )
    scores = jnp.where(allowed, scores * (1.0 / math.sqrt(HEAD_DIM)), -1e30)
    soft_weights = jax.nn.softmax(scores, axis=-1)
    mixed_heads = jnp.einsum(
        "...hqk,...khd->...qhd",
        soft_weights.astype(jnp.bfloat16),
        value_heads,
        preferred_element_type=jnp.float32,
    )
    return (mixed_heads, soft_weights)


def attend_backward(query_heads, key_heads, value_heads, soft_weights, grad_mixed):
    grad_low = grad_mixed.astype(jnp.bfloat16)
    grad_soft = jnp.einsum(
        "...qhd,...khd->...hqk", grad_low, value_heads, preferred_element_type=jnp.float32
    )
    grad_values = jnp.einsum(
        "...hqk,...qhd->...khd",
        soft_weights.astype(jnp.bfloat16),
        grad_low,
        preferred_element_type=jnp.float32,
    )
    grad_scores = soft_weights * (
        grad_soft - jnp.sum(soft_weights * grad_soft, axis=-1, keepdims=True)
    )
    grad_scores = (grad_scores * (1.0 / math.sqrt(HEAD_DIM))).astype(jnp.bfloat16)
    grad_query = jnp.einsum(
        "...hqk,...khd->...qhd", grad_scores, key_heads, preferred_element_type=jnp.float32
    )
    grad_keys = jnp.einsum(
        "...hqk,...qhd->...khd", grad_scores, query_heads, preferred_element_type=jnp.float32
    )
    return (grad_query, grad_keys, grad_values)


def regather(shard):
    return lax.all_gather(shard.astype(jnp.bfloat16), "fsdp", axis=0, tiled=True)


def reduce_one(grad_full):
    share = lax.psum_scatter(grad_full, "fsdp", scatter_dimension=0, tiled=True)
    return lax.psum(share, "frame")


def block_forward(residual, six_rows, matrices, allowed, cross, temporal):
    gate_parts = [six_rows[:, position][:, None, None, :] for position in range(6)]
    normed = modulate(residual, gate_parts[0], gate_parts[1]).astype(jnp.bfloat16)
    packed = linear(normed, matrices[0]).astype(jnp.bfloat16)
    query_heads = split_heads(packed[..., :D])
    key_heads = split_heads(packed[..., D : 2 * D])
    value_heads = split_heads(packed[..., 2 * D :])
    if temporal:
        query_heads = jnp.swapaxes(query_heads, 1, 2)
        key_heads = jnp.swapaxes(key_heads, 1, 2)
        value_heads = jnp.swapaxes(value_heads, 1, 2)
        key_heads, value_heads = (
            lax.all_gather(for_sending(key_heads), "frame", axis=2, tiled=True).astype(
                key_heads.dtype
            ),
            lax.all_gather(for_sending(value_heads), "frame", axis=2, tiled=True).astype(
                value_heads.dtype
            ),
        )
    mixed_heads, soft_weights = attend_forward(query_heads, key_heads, value_heads, allowed)
    if temporal:
        mixed_heads = jnp.swapaxes(mixed_heads, 1, 2)
    mixed_heads = join_heads(mixed_heads).astype(jnp.bfloat16)
    projected = linear(mixed_heads, matrices[1])
    middle = residual + gate_parts[2] * projected
    kept_values = {
        "gate_parts": gate_parts,
        "residual": residual,
        "normed": normed,
        "query_heads": query_heads,
        "key_heads": key_heads,
        "value_heads": value_heads,
        "soft_weights": soft_weights,
        "mixed_heads": mixed_heads,
        "projected": projected,
    }
    if cross is not None:
        after_low = middle.astype(jnp.bfloat16)
        cross_query = split_heads(linear(after_low, cross[0]).astype(jnp.bfloat16))
        cross_mixed, cross_soft = attend_forward(cross_query, cross[2], cross[3], True)
        cross_mixed = join_heads(cross_mixed).astype(jnp.bfloat16)
        middle = middle + linear(cross_mixed, cross[1])
        kept_values.update(
            {
                "after_low": after_low,
                "cross_query": cross_query,
                "cross_soft": cross_soft,
                "cross_mixed": cross_mixed,
            }
        )
    normed_two = modulate(middle, gate_parts[3], gate_parts[4]).astype(jnp.bfloat16)
    up_values = linear(normed_two, matrices[2])
    active = gelu_tanh(up_values).astype(jnp.bfloat16)
    lowered = linear(active, matrices[3].T)
    kept_values.update(
        {
            "middle": middle,
            "normed_two": normed_two,
            "up_values": up_values,
            "active": active,
            "lowered": lowered,
        }
    )
    return (middle + gate_parts[5] * lowered, kept_values)


def block_backward(grad_out, kept_values, matrices, cross, temporal):
    gate_parts = kept_values["gate_parts"]
    grad_six = [None] * 6
    grad_six[5] = jnp.sum(grad_out * kept_values["lowered"], axis=(1, 2))
    grad_active, grad_down = linear_back(
        kept_values["active"], matrices[3].T, grad_out * gate_parts[5]
    )
    grad_up_values = jax.vjp(gelu_tanh, kept_values["up_values"])[1](grad_active)[0]
    grad_normed_two, grad_up = linear_back(kept_values["normed_two"], matrices[2], grad_up_values)
    grad_middle, grad_shift, grad_scale = jax.vjp(
        modulate, kept_values["middle"], gate_parts[3], gate_parts[4]
    )[1](grad_normed_two)
    grad_six[3] = grad_shift[:, 0, 0]
    grad_six[4] = grad_scale[:, 0, 0]
    grad_after = grad_out + grad_middle
    cross_grads = None
    if cross is not None:
        grad_cross_mixed, grad_cross_out = linear_back(
            kept_values["cross_mixed"], cross[1], grad_after
        )
        grad_cross_query, grad_cross_keys, grad_cross_values = attend_backward(
            kept_values["cross_query"],
            cross[2],
            cross[3],
            kept_values["cross_soft"],
            split_heads(grad_cross_mixed),
        )
        grad_after_part, grad_query_weight = linear_back(
            kept_values["after_low"], cross[0], join_heads(grad_cross_query)
        )
        grad_after = grad_after + grad_after_part
        grad_pair = jnp.concatenate(
            [
                join_heads(jnp.sum(grad_cross_keys, axis=1)),
                join_heads(jnp.sum(grad_cross_values, axis=1)),
            ],
            axis=-1,
        )
        cross_grads = (grad_query_weight, grad_cross_out, grad_pair)
    grad_six[2] = jnp.sum(grad_after * kept_values["projected"], axis=(1, 2))
    grad_mixed, grad_out_weight = linear_back(
        kept_values["mixed_heads"], matrices[1], grad_after * gate_parts[2]
    )
    grad_mixed = split_heads(grad_mixed)
    if temporal:
        grad_mixed = jnp.swapaxes(grad_mixed, 1, 2)
    grad_query, grad_keys, grad_values = attend_backward(
        kept_values["query_heads"],
        kept_values["key_heads"],
        kept_values["value_heads"],
        kept_values["soft_weights"],
        grad_mixed,
    )
    if temporal:
        grad_keys, grad_values = (
            lax.psum_scatter(
                grad_keys.astype(jnp.bfloat16), "frame", scatter_dimension=2, tiled=True
            ).astype(jnp.float32),
            lax.psum_scatter(
                grad_values.astype(jnp.bfloat16), "frame", scatter_dimension=2, tiled=True
            ).astype(jnp.float32),
        )
        grad_query = jnp.swapaxes(grad_query, 1, 2)
        grad_keys = jnp.swapaxes(grad_keys, 1, 2)
        grad_values = jnp.swapaxes(grad_values, 1, 2)
    grad_packed = jnp.concatenate(
        [join_heads(grad_query), join_heads(grad_keys), join_heads(grad_values)], axis=-1
    )
    grad_normed, grad_qkv = linear_back(kept_values["normed"], matrices[0], grad_packed)
    grad_residual, grad_shift, grad_scale = jax.vjp(
        modulate, kept_values["residual"], gate_parts[0], gate_parts[1]
    )[1](grad_normed)
    grad_six[0] = grad_shift[:, 0, 0]
    grad_six[1] = grad_scale[:, 0, 0]
    return (
        grad_after + grad_residual,
        jnp.stack(grad_six, axis=1),
        (grad_qkv, grad_out_weight, grad_up, grad_down.T),
        cross_grads,
    )


def local(
    latents,
    added_noise,
    text_states,
    timesteps,
    token_counts,
    frame_counts,
    w_shared,
    w_spatial,
    w_temporal,
    shift_tables,
    m_shared,
    m_spatial,
    m_temporal,
    m_tables,
    v_shared,
    v_spatial,
    v_temporal,
    v_tables,
):
    frames_local = latents.shape[2]
    frames_all = frames_local * lax.axis_size("frame")
    videos = latents.shape[0] * latents.shape[1]
    spatial_count = latents.shape[3]
    full_shared, full_spatial, full_temporal, full_tables = (
        lax.all_gather(w_shared.astype(jnp.bfloat16), "fsdp", axis=0, tiled=True),
        lax.all_gather(w_spatial.astype(jnp.bfloat16), "fsdp", axis=0, tiled=True),
        lax.all_gather(w_temporal.astype(jnp.bfloat16), "fsdp", axis=0, tiled=True),
        lax.all_gather(shift_tables.astype(jnp.bfloat16), "fsdp", axis=0, tiled=True),
    )
    shared_fwd = split_columns(full_shared, shared_widths())
    spatial_fwd = split_columns(full_spatial, spatial_widths())
    temporal_fwd = split_columns(full_temporal, temporal_widths())
    tables = full_tables.astype(jnp.float32)
    step_float = timesteps.reshape(videos).astype(jnp.float32)
    token_count = token_counts.reshape(videos)
    alpha_bar = jnp.cos((step_float / 1000.0 + 0.008) / 1.008 * (math.pi / 2)) ** 2
    snr_value = alpha_bar / (1.0 - alpha_bar)
    loss_weight = jnp.minimum(snr_value, SNR_GAMMA) / snr_value
    clean_latent = latents.reshape((videos,) + latents.shape[2:]).astype(jnp.float32)
    target = added_noise.reshape((videos,) + added_noise.shape[2:]).astype(jnp.float32)
    noisy = (
        jnp.sqrt(alpha_bar)[:, None, None, None] * clean_latent
        + jnp.sqrt(1.0 - alpha_bar)[:, None, None, None] * target
    ).astype(jnp.bfloat16)
    half_count = FREQ // 2
    frequency = jnp.exp(-math.log(10000.0) * jnp.arange(half_count, dtype=jnp.float32) / half_count)
    angles = step_float[:, None] * frequency[None, :]
    features = jnp.concatenate([jnp.cos(angles), jnp.sin(angles)], axis=-1).astype(jnp.bfloat16)
    frame_index = lax.axis_index("frame") * frames_local + jnp.arange(frames_local, dtype=jnp.int32)
    clip_ends = jnp.cumsum(frame_counts.reshape(videos, -1), axis=-1)
    segment_all = jnp.sum(
        (jnp.arange(frames_all, dtype=jnp.int32)[None, :, None] >= clip_ends[:, None, :]).astype(
            jnp.int32
        ),
        axis=-1,
    )
    segment_local = jnp.sum(
        (frame_index[None, :, None] >= clip_ends[:, None, :]).astype(jnp.int32), axis=-1
    )
    same_clip = (segment_local[:, :, None] == segment_all[:, None, :])[:, None, None]
    key_valid = jnp.arange(spatial_count)[None, :] < token_count[:, None]
    key_allowed = key_valid[:, None, None, None, :]
    hidden_pre = linear(features, shared_fwd[1].T)
    hidden_act = jax.nn.silu(hidden_pre).astype(jnp.bfloat16)
    embedding = linear(hidden_act, shared_fwd[3])
    embed_act = jax.nn.silu(embedding).astype(jnp.bfloat16)
    modulation = linear(embed_act, shared_fwd[4]).reshape(videos, 6, D)
    six_spatial = modulation + tables[:, 0:6].T[None]
    six_temporal = modulation + tables[:, 6:12].T[None]
    text_flat = text_states.reshape((videos,) + text_states.shape[2:])
    caption_pre = linear(text_flat, shared_fwd[2].T)
    caption = gelu_tanh(caption_pre).astype(jnp.bfloat16)
    cross_pair = linear(caption, spatial_fwd[3]).astype(jnp.bfloat16)
    pair_shape = (videos, frames_local, cross_pair.shape[1], HEADS, HEAD_DIM)
    cross_keys = jnp.broadcast_to(split_heads(cross_pair[..., :D])[:, None], pair_shape)
    cross_values = jnp.broadcast_to(split_heads(cross_pair[..., D:])[:, None], pair_shape)
    patches_in = linear(noisy, shared_fwd[0].T)
    first_out, first_kept = block_forward(
        patches_in,
        six_spatial,
        (spatial_fwd[0], spatial_fwd[1], spatial_fwd[5], spatial_fwd[6]),
        key_allowed,
        (spatial_fwd[2], spatial_fwd[4], cross_keys, cross_values),
        False,
    )
    second_out, second_kept = block_forward(
        first_out, six_temporal, tuple(temporal_fwd), same_clip, None, True
    )
    final_rows = embedding[:, None, :] + tables[:, 12:14].T[None]
    shift_final = final_rows[:, 0][:, None, None, :]
    scale_final = final_rows[:, 1][:, None, None, :]
    normed_final = modulate(second_out, shift_final, scale_final).astype(jnp.bfloat16)
    predicted = linear(normed_final, shared_fwd[5])
    pred_error = predicted - target
    keep_weight = key_valid.astype(jnp.float32)[:, None, :, None] * loss_weight[:, None, None, None]
    loss_part = jnp.sum(keep_weight * pred_error * pred_error) / PCH
    denom_part = jnp.sum(loss_weight * token_count.astype(jnp.float32)) * frames_local
    shared_back = split_columns(regather(w_shared), shared_widths())
    grad_pred = keep_weight * pred_error * (2.0 / PCH)
    grad_normed_final, grad_final_weight = linear_back(normed_final, shared_back[5], grad_pred)
    grad_second, grad_shift_final, grad_scale_final = jax.vjp(
        modulate, second_out, shift_final, scale_final
    )[1](grad_normed_final)
    temporal_back = split_columns(regather(w_temporal), temporal_widths())
    grad_first, grad_six_temporal, temporal_grads, unused = block_backward(
        grad_second, second_kept, tuple(temporal_back), None, True
    )
    temporal_share = reduce_one(jnp.concatenate(list(temporal_grads), axis=1))
    spatial_back = split_columns(regather(w_spatial), spatial_widths())
    grad_patches, grad_six_spatial, spatial_grads, cross_grads = block_backward(
        grad_first,
        first_kept,
        (spatial_back[0], spatial_back[1], spatial_back[5], spatial_back[6]),
        (spatial_back[2], spatial_back[4], cross_keys, cross_values),
        False,
    )
    grad_caption, grad_pair_weight = linear_back(caption, spatial_back[3], cross_grads[2])
    spatial_share = reduce_one(
        jnp.concatenate(
            [
                spatial_grads[0],
                spatial_grads[1],
                cross_grads[0],
                grad_pair_weight,
                cross_grads[1],
                spatial_grads[2],
                spatial_grads[3],
            ],
            axis=1,
        )
    )
    unused_in, grad_patch_weight = linear_back(noisy, shared_back[0].T, grad_patches)
    grad_caption_pre = jax.vjp(gelu_tanh, caption_pre)[1](grad_caption)[0]
    unused_text, grad_caption_weight = linear_back(text_flat, shared_back[2].T, grad_caption_pre)
    grad_modulation = (grad_six_spatial + grad_six_temporal).reshape(videos, 6 * D)
    grad_embed_act, grad_modulation_weight = linear_back(embed_act, shared_back[4], grad_modulation)
    grad_embedding = (
        jax.vjp(jax.nn.silu, embedding)[1](grad_embed_act)[0]
        + grad_shift_final[:, 0, 0]
        + grad_scale_final[:, 0, 0]
    )
    grad_hidden_act, grad_time_two = linear_back(hidden_act, shared_back[3], grad_embedding)
    grad_hidden_pre = jax.vjp(jax.nn.silu, hidden_pre)[1](grad_hidden_act)[0]
    unused_feat, grad_time_one = linear_back(features, shared_back[1].T, grad_hidden_pre)
    shared_share = reduce_one(
        jnp.concatenate(
            [
                grad_patch_weight.T,
                grad_time_one.T,
                grad_caption_weight.T,
                grad_time_two,
                grad_modulation_weight,
                grad_final_weight,
            ],
            axis=1,
        )
    )
    final_table_grad = jnp.stack(
        [jnp.sum(grad_shift_final[:, 0, 0], axis=0), jnp.sum(grad_scale_final[:, 0, 0], axis=0)],
        axis=1,
    )
    tables_share = reduce_one(
        jnp.concatenate(
            [
                jnp.sum(grad_six_spatial, axis=0).T,
                jnp.sum(grad_six_temporal, axis=0).T,
                final_table_grad,
            ],
            axis=1,
        )
    )
    grads = (shared_share, spatial_share, temporal_share, tables_share)
    masters = (w_shared, w_spatial, w_temporal, shift_tables)
    grad_sq = matrix_squares(grads)
    weight_sq = matrix_squares(masters)
    grad_sq, weight_sq, loss_sum, weight_total = lax.psum(
        (grad_sq, weight_sq, loss_part, denom_part), ("fsdp", "frame")
    )
    grad_sq = grad_sq / lax.axis_size("frame")
    weight_sq = weight_sq / lax.axis_size("frame")
    grad_norm = jnp.sqrt(jnp.sum(grad_sq)) / weight_total
    factor = CLIP_NORM / jnp.maximum(grad_norm, CLIP_NORM)
    grad_scale = factor / weight_total
    firsts, seconds, updates = ([], [], [])
    for grad_one, first_old, second_old, master in zip(
        grads,
        (m_shared, m_spatial, m_temporal, m_tables),
        (v_shared, v_spatial, v_temporal, v_tables),
        masters,
    ):
        clipped = grad_one * grad_scale
        first_new = BETA_ONE * first_old + (1.0 - BETA_ONE) * clipped
        second_new = BETA_TWO * second_old + (1.0 - BETA_TWO) * clipped * clipped
        updates.append(
            first_new
            / (1.0 - BETA_ONE**STEP)
            / (jnp.sqrt(second_new / (1.0 - BETA_TWO**STEP)) + ADAM_EPS)
            + DECAY_RATE * master
        )
        firsts.append(first_new)
        seconds.append(second_new)
    update_sq = lax.psum(matrix_squares(updates), "fsdp")
    trust_ratio = jnp.sqrt(weight_sq) / jnp.sqrt(update_sq)
    column_trust = (
        spread_columns(trust_ratio[0:6], shared_widths())[None, :],
        spread_columns(trust_ratio[6:13], spatial_widths())[None, :],
        spread_columns(trust_ratio[13:17], temporal_widths())[None, :],
        trust_ratio[17],
    )
    new_values = [
        master - LEARN_RATE * trust_one * update
        for master, trust_one, update in zip(masters, column_trust, updates)
    ]
    matrix_norms = jnp.stack([jnp.sqrt(weight_sq), jnp.sqrt(update_sq)])
    clipped_norms = jnp.sqrt(grad_sq) * grad_scale
    return (
        loss_sum,
        weight_total,
        grad_norm,
        matrix_norms,
        clipped_norms,
        new_values[0],
        new_values[1],
        new_values[2],
        new_values[3],
        firsts[0],
        firsts[1],
        firsts[2],
        firsts[3],
        seconds[0],
        seconds[1],
        seconds[2],
        seconds[3],
        new_values[0].astype(jnp.bfloat16),
        new_values[1].astype(jnp.bfloat16),
        new_values[2].astype(jnp.bfloat16),
        new_values[3].astype(jnp.bfloat16),
    )


def solution(mesh):
    return jax.shard_map(
        local,
        mesh=mesh,
        in_specs=(
            P(None, "fsdp", "frame", None, None),
            P(None, "fsdp", "frame", None, None),
            P(None, "fsdp", None, None),
            P(None, "fsdp"),
            P(None, "fsdp"),
            P(None, "fsdp", None),
            P("fsdp", None),
            P("fsdp", None),
            P("fsdp", None),
            P("fsdp", None),
            P("fsdp", None),
            P("fsdp", None),
            P("fsdp", None),
            P("fsdp", None),
            P("fsdp", None),
            P("fsdp", None),
            P("fsdp", None),
            P("fsdp", None),
        ),
        out_specs=(
            P(),
            P(),
            P(),
            P(),
            P(),
            P("fsdp", None),
            P("fsdp", None),
            P("fsdp", None),
            P("fsdp", None),
            P("fsdp", None),
            P("fsdp", None),
            P("fsdp", None),
            P("fsdp", None),
            P("fsdp", None),
            P("fsdp", None),
            P("fsdp", None),
            P("fsdp", None),
            P("fsdp", None),
            P("fsdp", None),
            P("fsdp", None),
            P("fsdp", None),
        ),
        check_vma=False,
    )
```

profile of v0, /device:TPU:0, one launch (start us, length us, event | category | flops | bytes accessed | tf_op | source)
XLA Modules:
  0.0 6593.1 jit_solution(4766103855479948134)
XLA Ops:
  26.6 68.1 %all-gather = bf16[8,144,14]{1,2,0:T(8,128)(2,1)S(1)} all-gather(bf16[1,144,14]{1,2,0:T(8,128)(2,1)S(1)} %convert_bitcast_fusion.2), channel_id=1, replica_groups=mesh['fsdp'=8,'frame'=4] {'fsdp'}, dimensions={0}, use_global_device_ids=true | all-gather | bytes 36288 | tf_op jit(solution)/shard_map/all_gather | solution.py:332
  96.7 470.4 %all-gather.7.cloned.1.call-done = bf16[1152,12448]{1,0:T(8,128)(2,1)} async-done(((bf16[144,12448]{1,0:T(8,128)(2,1)}), bf16[1152,12448]{1,0:T(8,128)(2,1)}) %all-gather.7.cloned.1.call-update) | async-done | bytes 28680208 | tf_op jit(solution)/shard_map/all_gather | solution.py:329
  597.4 776.7 %all-gather.9.cloned.1.call-done = bf16[1152,18432]{1,0:T(8,128)(2,1)} async-done(((bf16[144,18432]{1,0:T(8,128)(2,1)}), bf16[1152,18432]{1,0:T(8,128)(2,1)}) %all-gather.9.cloned.1.call-update) | async-done | bytes 42467344 | tf_op jit(solution)/shard_map/all_gather | solution.py:330
  1455.4 16.9 fusion.242
  1472.7 509.3 %all-gather.11.cloned.1.call-done = bf16[1152,13824]{1,0:T(8,128)(2,1)} async-done(((bf16[144,13824]{1,0:T(8,128)(2,1)}), bf16[1152,13824]{1,0:T(8,128)(2,1)}) %all-gather.11.cloned.1.call-update) | async-done | bytes 31850512 | tf_op jit(solution)/shard_map/all_gather | solution.py:331
  2009.7 22.9 all-gather.15.cloned.1.call-done
  2117.3 17.6 fusion.240
  2143.1 17.2 fusion.28
  2211.7 18.6 multiply_convert_fusion.3
  2274.0 36.8 reduce-scatter.9.cloned.1.call-done
  2326.0 15.7 fusion.21
  2481.7 72.9 %concatenate.53 = f32[1152,12448]{1,0:T(8,128)} concatenate(f32[1152,16]{1,0:T(8,128)S(1)} %copy-done.40, f32[1152,256]{1,0:T(8,128)S(1)} %fusion.186, f32[1152,4096]{1,0:T(8,128)} %fusion.261, f32[1152,1152]{1,0:T(8,128)} %fusion.227, f32[1152,6912]{1,0:T(8,128)} %fusion.228, f32[1152,16]{1,0:T(8,128)S(1)} %copy-done.59), dimensions={1} | concatenate | bytes 114720768 | tf_op jit(solution)/shard_map/concatenate | solution.py:450
  2594.8 43.3 pad_maximum_fusion
  2693.1 758.6 %reduce-scatter.13.cloned.1.call-done = f32[144,12448]{1,0:T(8,128)} async-done(((f32[1152,12448]{1,0:T(8,128)}), f32[144,12448]{1,0:T(8,128)}) %reduce-scatter.13.cloned.1.call-update) | async-done | bytes 7170064 | tf_op jit(solution)/shard_map/reduce_scatter | solution.py:152
  3451.7 1006.4 %reduce-scatter.17.cloned.1.call-done = f32[144,13824]{1,0:T(8,128)} async-done(((f32[1152,13824]{1,0:T(8,128)}), f32[144,13824]{1,0:T(8,128)}) %reduce-scatter.17.cloned.1.call-update) | async-done | bytes 7962640 | tf_op jit(solution)/shard_map/reduce_scatter | solution.py:152
  4458.0 1312.5 %reduce-scatter.15.cloned.1.call-done = f32[144,18432]{1,0:T(8,128)} async-done(((f32[1152,18432]{1,0:T(8,128)}), f32[144,18432]{1,0:T(8,128)}) %reduce-scatter.15.cloned.1.call-update) | async-done | bytes 10616848 | tf_op jit(solution)/shard_map/reduce_scatter | solution.py:152
  5801.2 34.9 reduce-scatter.19.cloned.1.call-done
  5848.3 424.4 %all-reduce.5.cloned.1.call-done = (f32[144,12448]{1,0:T(8,128)}, f32[144,18432]{1,0:T(8,128)}, f32[144,13824]{1,0:T(8,128)}) async-done(((f32[144,12448]{1,0:T(8,128)}, f32[144,18432]{1,0:T(8,128)}, f32[144,13824]{1,0:T(8,128)}), (f32[144,12448]{1,0:T(8,128)}, f32[144,18432]{1,0:T(8,128)}, f32[144,13824]{1,0:T(8,128)})) %all-reduce.5.cloned.1.call-update) | async-done | bytes 25749520 | tf_op jit(solution)/shard_map/psum | solution.py:153
  6313.3 39.7 all-reduce.1
  6355.6 18.9 multiply_add_fusion.4
  6386.8 20.1 multiply_add_fusion.2
  6415.4 26.7 multiply_add_fusion
  6477.3 21.2 psum.71
  6498.6 36.9 all-reduce
  (631 shorter events, 784.5 us)
Async XLA Ops:
  7.2 582.1 %copy-start = (bf16[2,1,64,4096]{3,2,1,0:T(8,128)(2,1)S(1)}, bf16[2,1,64,4096]{3,2,1,0:T(8,128)(2,1)}, u32[]{:S(2)}) copy-start(bf16[2,1,64,4096]{3,2,1,0:T(8,128)(2,1)} %param.20) | copy-start | bytes 3145732
  7.2 559.9 %all-gather.7.cloned.1.call-start = ((), (), s32[]{:S(2)}) async-start(), calls=%async_computation.6 | async-start | bytes 32514048 | tf_op jit(solution)/shard_map/all_gather | solution.py:329
  12.6 1361.5 %all-gather.9.cloned.1.call-start = ((), (), s32[]{:S(2)}) async-start(), calls=%async_computation.7 | async-start | bytes 47775744 | tf_op jit(solution)/shard_map/all_gather | solution.py:330
  19.7 1962.3 %all-gather.11.cloned.1.call-start = ((), (), s32[]{:S(2)}) async-start(), calls=%async_computation.8 | async-start | bytes 35831808 | tf_op jit(solution)/shard_map/all_gather | solution.py:331
  25.9 2006.8 %all-gather.15.cloned.1.call-start = ((), (), s32[]{:S(2)}) async-start(), calls=%async_computation.10 | async-start | bytes 5898240 | tf_op jit(solution)/shard_map/all_gather | solution.py:168
  571.5 1429.4 %copy-start.71 = (f32[2,1152]{1,0:T(2,128)}, f32[2,1152]{1,0:T(2,128)S(1)}, u32[]{:S(2)}) copy-start(f32[2,1152]{1,0:T(2,128)S(1)} %fusion.79) | copy-start | bytes 27652
  583.8 1398.2 %copy-start.75 = (f32[2,1,1152]{2,0,1:T(2,128)}, f32[2,1,1152]{2,0,1:T(2,128)S(1)}, u32[]{:S(2)}) copy-start(f32[2,1,1152]{2,0,1:T(2,128)S(1)} %copy.481) | copy-start | bytes 27652
  583.9 852.7 %copy-start.63 = (f32[2,1,1152]{2,0,1:T(2,128)}, f32[2,1,1152]{2,0,1:T(2,128)S(1)}, u32[]{:S(2)}) copy-start(f32[2,1,1152]{2,0,1:T(2,128)S(1)} %copy.488) | copy-start | bytes 27652
  583.9 804.5 %copy-start.82 = (f32[2,1,1152]{2,0,1:T(2,128)}, f32[2,1,1152]{2,0,1:T(2,128)S(1)}, u32[]{:S(2)}) copy-start(f32[2,1,1152]{2,0,1:T(2,128)S(1)} %copy.487) | copy-start | bytes 27652
  588.0 848.6 %copy-start.2 = (f32[2,2,128,1152]{3,2,1,0:T(8,128)}, f32[2,2,128,1152]{3,2,1,0:T(8,128)S(1)}, u32[]{:S(2)}) copy-start(f32[2,2,128,1152]{3,2,1,0:T(8,128)S(1)} %get-tuple-element.166) | copy-start | bytes 7077892
  588.0 800.4 %copy-start.111 = (f32[2,2,128]{2,1,0:T(2,128)}, f32[2,2,128]{2,1,0:T(2,128)S(1)}, u32[]{:S(2)}) copy-start(f32[2,2,128]{2,1,0:T(2,128)S(1)} %broadcast_multiply_fusion.6) | copy-start | bytes 6148
  589.3 799.1 %copy-start.117 = (f32[2,2,128]{2,1,0:T(2,128)}, f32[2,2,128]{2,1,0:T(2,128)S(1)}, u32[]{:S(2)}) copy-start(f32[2,2,128]{2,1,0:T(2,128)S(1)} %fusion.198) | copy-start | bytes 6148
  1472.3 851.4 %copy-start.5 = (f32[2,2,128,1152]{3,2,1,0:T(8,128)}, f32[2,2,128,1152]{3,2,1,0:T(8,128)S(1)}, u32[]{:S(2)}) copy-start(f32[2,2,128,1152]{3,2,1,0:T(8,128)S(1)} %get-tuple-element.109) | copy-start | bytes 7077892
  1472.3 518.4 %copy-start.60 = (f32[2,2,128]{2,1,0:T(2,128)}, f32[2,2,128]{2,1,0:T(2,128)S(1)}, u32[]{:S(2)}) copy-start(f32[2,2,128]{2,1,0:T(2,128)S(1)} %broadcast_multiply_fusion.4) | copy-start | bytes 6148
  1472.7 518.0 %copy-start.126 = (f32[2,2,128]{2,1,0:T(2,128)}, f32[2,2,128]{2,1,0:T(2,128)S(1)}, u32[]{:S(2)}) copy-start(f32[2,2,128]{2,1,0:T(2,128)S(1)} %multiply_reduce_fusion.23) | copy-start | bytes 6148
  1472.7 518.0 %copy-start.66 = (f32[2,2,128]{2,1,0:T(2,128)}, f32[2,2,128]{2,1,0:T(2,128)S(1)}, u32[]{:S(2)}) copy-start(f32[2,2,128]{2,1,0:T(2,128)S(1)} %fusion.200) | copy-start | bytes 6148
  1995.0 77.1 %all-gather.13.cloned.1.call-start = ((), (), s32[]{:S(2)}) async-start(), calls=%async_computation.9 | async-start | bytes 5898240 | tf_op jit(solution)/shard_map/all_gather | solution.py:171
  1997.5 273.9 %reduce-scatter.11.cloned.1.call-start = ((), (), s32[]{:S(2)}) async-start(), calls=%async_computation.12 | async-start | bytes 5898240 | tf_op jit(solution)/shard_map/reduce_scatter | solution.py:280
  2211.7 99.1 %reduce-scatter.9.cloned.1.call-start = ((), (), s32[]{:S(2)}) async-start(), calls=%async_computation.11 | async-start | bytes 5898240 | tf_op jit(solution)/shard_map/reduce_scatter | solution.py:277
  2251.0 1200.7 %reduce-scatter.13.cloned.1.call-start = ((), (), s32[]{:S(2)}) async-start(), calls=%async_computation.13 | async-start | bytes 65028096 | tf_op jit(solution)/shard_map/reduce_scatter | solution.py:152
  2554.7 1903.4 %reduce-scatter.17.cloned.1.call-start = ((), (), s32[]{:S(2)}) async-start(), calls=%async_computation.15 | async-start | bytes 71663616 | tf_op jit(solution)/shard_map/reduce_scatter | solution.py:152
  2638.2 3132.4 %reduce-scatter.15.cloned.1.call-start = ((), (), s32[]{:S(2)}) async-start(), calls=%async_computation.14 | async-start | bytes 95551488 | tf_op jit(solution)/shard_map/reduce_scatter | solution.py:152
  2690.9 3145.2 %reduce-scatter.19.cloned.1.call-start = ((), (), s32[]{:S(2)}) async-start(), calls=%async_computation.16 | async-start | bytes 663552
  2692.8 3579.9 %all-reduce.5.cloned.1.call-start = ((), (), s32[]{:S(2)}) async-start(), calls=%async_computation.17 | async-start | bytes 51609600 | tf_op jit(solution)/shard_map/psum | solution.py:153
  (157 other events, 4604.7 us)
Sparse Core Ops, SparseCore 0:
  12.7 554.3 all-gather.6
  569.3 804.8 all-gather.8
  1376.2 605.7 all-gather.10
  1995.2 37.4 all-gather.14
  2034.6 37.4 all-gather.12
  2211.8 47.8 reduce-scatter.10
  2262.9 47.8 reduce-scatter.8
  2554.8 896.8 reduce-scatter.12
  3455.6 1002.4 reduce-scatter.16
  4461.8 1308.7 reduce-scatter.14
  5774.7 61.3 reduce-scatter.18
  5838.9 433.7 all-reduce.4
where the time goes:
time: 6610 us; the launch traced here: 6590 us
  waiting for transfers between devices  5360 us (81%)
  matrix products  480 us (7%)
  other arithmetic  291 us (4%)
  local copies, waits for them, and re-layouts  266 us (4%)
  blocking collectives  176 us (3%)
    reduce_scatter x3, waiting for transfers between devices, reduce_one(): share = lax.psum_scatter(grad_full, 'fsdp', scatter_dimension=0, tiled=True)  3080 us
    all_gather x1, waiting for transfers between devices, local(): lax.all_gather(w_spatial.astype(jnp.bfloat16), 'fsdp', axis=0, tiled=True)  777 us
    all_gather x1, waiting for transfers between devices, local(): lax.all_gather(w_temporal.astype(jnp.bfloat16), 'fsdp', axis=0, tiled=True)  509 us
    all_gather x1, waiting for transfers between devices, local(): lax.all_gather(w_shared.astype(jnp.bfloat16), 'fsdp', axis=0, tiled=True)  470 us
    psum x1, waiting for transfers between devices, reduce_one(): return lax.psum(share, 'frame')  424 us
  transfers between devices with their start and end apart: 12, of which 11 were waited for; matrix products, arithmetic and copies ran while one was open for 6% of the time, Pallas kernels for 0%

commit v1 on v0

v1 whole, which is shorter than its diff:
```python
import math

import jax
import jax.numpy as jnp
import numpy as np
from jax import lax
from jax.experimental import pallas as pl
from jax.experimental.pallas import tpu as pltpu
from jax.sharding import PartitionSpec as P

D = 1152
HEADS = 16
HEAD_DIM = 72
FF = 4608
TXT_D = 4096
FREQ = 256
PCH = 16
STEP = 10

CLIP_NORM = 0.01
LEARN_RATE = 0.3
BETA_ONE = 0.9
BETA_TWO = 0.999
ADAM_EPS = 1e-06
DECAY_RATE = 0.01
SNR_GAMMA = 5.0
NORM_EPS = 1e-06

F32 = jnp.float32
BF16 = jnp.bfloat16


def few(axis):
    return lax.axis_size(axis) <= 8


def swap(values, axis, mask):
    return lax.ppermute(values, axis, [(n, n ^ mask) for n in range(lax.axis_size(axis))])


def order_of(axis):
    return jnp.arange(lax.axis_size(axis), dtype=jnp.int32) ^ lax.axis_index(axis)


def to_relative(stacked, axis):
    return jnp.take(stacked, order_of(axis), axis=0)


def masks(axis):
    return [m for m in (2, 4, 1) if m < lax.axis_size(axis)] if axis == "fsdp" else [1, 2]


def gate(values, after):
    return lax.optimization_barrier((values, after))[0]


def sum_over(values, axis):
    if not few(axis):
        return lax.psum(values, axis)
    for mask in masks(axis):
        values = values + swap(values, axis, mask)
    return values


def sum_over_frame_low(values):
    for mask in (1, 2):
        low = values.astype(BF16)
        values = low.astype(F32) + swap(low, "frame", mask).astype(F32)
    return values


def collect(values, axis):
    if not few(axis):
        return to_relative(lax.all_gather(values, axis, axis=0), axis)
    blocks = values[None]
    for mask in masks(axis):
        blocks = jnp.concatenate([blocks, swap(blocks, axis, mask)])
    if axis == "frame":
        return blocks
    size = lax.axis_size(axis)
    return jnp.swapaxes(blocks.reshape((2, size // 2) + values.shape), 0, 1).reshape(blocks.shape)


def collect_along(values):
    if not few("fsdp"):
        return values
    size = lax.axis_size("fsdp")
    return jnp.stack([values] + [swap(values, "fsdp", mask) for mask in range(2, size, 2)])


def collect_beside(along):
    if not few("fsdp"):
        return collect(along, "fsdp")
    both = jnp.stack([along, swap(along, "fsdp", 1)], axis=1)
    return both.reshape((-1,) + along.shape[1:])


def deliver_beside(blocks):
    if not few("fsdp"):
        return blocks
    pairs = blocks.reshape((-1, 2) + blocks.shape[1:])
    return pairs[:, 0] + swap(pairs[:, 1], "fsdp", 1)


def deliver_along(half):
    if not few("fsdp"):
        return deliver(half, "fsdp")
    total = half[0]
    for k in range(1, half.shape[0]):
        total = total + swap(half[k], "fsdp", 2 * k)
    return total


def fence(values):
    flat = values.reshape(-1, values.shape[-1])
    return swap(flat[:8, :128], "frame", 1)


def deliver(blocks, axis):
    size = lax.axis_size(axis)
    if not few(axis):
        return lax.psum_scatter(to_relative(blocks, axis), axis, scatter_dimension=0).astype(F32)
    kind = blocks.dtype
    held = list(range(size))
    for mask in masks(axis)[::-1]:
        keep = [k for k in held if not k & mask]
        low = blocks.astype(kind)
        received = swap(jnp.stack([low[held.index(k ^ mask)] for k in keep]), axis, mask)
        blocks = jnp.stack([blocks[held.index(k)] for k in keep]).astype(F32)
        blocks = blocks + received.astype(F32)
        held = keep
    return blocks[0]


def sum_relative(blocks, axis):
    size = lax.axis_size(axis)
    if not few(axis):
        return to_relative(lax.psum(to_relative(blocks, axis), axis), axis)
    for mask in masks(axis):
        received = swap(blocks, axis, mask)
        blocks = blocks + jnp.stack([received[k ^ mask] for k in range(size)])
    return blocks


def layer_norm(values):
    centered = values - jnp.mean(values, axis=-1, keepdims=True)
    return centered * lax.rsqrt(jnp.mean(centered * centered, axis=-1, keepdims=True) + NORM_EPS)


def modulate(residual, shift_by, scale_by):
    return layer_norm(residual) * (1.0 + scale_by) + shift_by


def gelu_tanh(values):
    return jax.nn.gelu(values, approximate=True)


def shared_widths():
    return (PCH, FREQ, TXT_D, D, 6 * D, PCH)


def spatial_widths():
    return (3 * D, D, D, 2 * D, D, FF, FF)


def temporal_widths():
    return (3 * D, D, FF, FF)


def split_columns(weight, widths):
    pieces = []
    offset = 0
    for column_count in widths:
        pieces.append(weight[:, offset : offset + column_count])
        offset += column_count
    return pieces


def dot(left, right):
    return lax.dot_general(
        left,
        right,
        (((left.ndim - 1,), (0,)), ((), ())),
        preferred_element_type=F32,
    )


def dot_t(left, right):
    return lax.dot_general(
        left,
        right,
        (((left.ndim - 1,), (1,)), ((), ())),
        preferred_element_type=F32,
    )


def outer(left, right):
    return lax.dot_general(
        left.reshape(-1, left.shape[-1]),
        right.reshape(-1, right.shape[-1]),
        (((0,), (0,)), ((), ())),
        preferred_element_type=F32,
    )


def modulate_back(residual, shift_by, scale_by, grad):
    grad_residual, grad_shift, grad_scale = jax.vjp(modulate, residual, shift_by, scale_by)[1](grad)
    return grad_residual, grad_shift[:, 0], grad_scale[:, 0]


LINES = 4
QUERIES = 128
BLOCK = D // (2 * LINES)
VMEM_LIMIT = 58 * 2**20
SCALE = 1.0 / math.sqrt(HEAD_DIM)


def nn(left, right):
    return lax.dot_general(left, right, (((1,), (0,)), ((), ())), preferred_element_type=F32)


def nt(left, right):
    return lax.dot_general(left, right, (((1,), (1,)), ((), ())), preferred_element_type=F32)


def tn(left, right):
    return lax.dot_general(left, right, (((0,), (0,)), ((), ())), preferred_element_type=F32)


class Pieces:
    def __init__(self, plan, place, refs, dest, sems, indices):
        z, y = place[0], place[1]
        self.copies = []
        for n, index in enumerate(indices):
            for k in range(LINES):
                for m, column in enumerate((y, 1 - y)):
                    ref, entry = plan[2 * n + m]
                    row = pl.multiple_of((jnp.bitwise_xor(z, k) * 2 + column) * BLOCK, BLOCK)
                    self.copies.append(
                        pltpu.make_async_copy(
                            refs[ref].at[entry, k],
                            dest.at[index, pl.ds(row, BLOCK)],
                            sems.at[n, 2 * k + m],
                        )
                    )

    def start(self):
        @pl.when(pl.program_id(0) == 0)
        def _():
            for copy in self.copies:
                copy.start()

    def wait(self, first, count):
        @pl.when(pl.program_id(0) == 0)
        def _():
            for copy in self.copies[2 * LINES * first : 2 * LINES * (first + count)]:
                copy.wait()


def windows():
    for head in range(HEADS):
        first = head * HEAD_DIM
        start = first // 128 * 128
        yield first - start, start, (256 if first - start + HEAD_DIM > 128 else 128)


def head_mask(offset, width):
    lane = lax.broadcasted_iota(jnp.int32, (1, width), 1)
    return jnp.where((lane >= offset) & (lane < offset + HEAD_DIM), 1.0, 0.0).astype(BF16)


def soft_columns(scores, allowed):
    scores = scores * SCALE
    if allowed is not None:
        scores = jnp.where(allowed > 0.5, scores, -1e30)
    grown = jnp.exp(scores - jnp.max(scores, axis=0, keepdims=True))
    return grown / jnp.sum(grown, axis=0, keepdims=True)


def attend_rows(query, key, value, out, allowed):
    for offset, start, width in windows():
        mask = head_mask(offset, width)
        lanes = slice(start, start + width)
        soft = soft_columns(nt(key[:, lanes], query[:, lanes] * mask), allowed)
        out[:, lanes] += tn(soft.astype(BF16), value[:, lanes] * mask)


def attend_rows_back(query, key, value, grad, grad_query, grad_key, grad_value, allowed):
    for offset, start, width in windows():
        mask = head_mask(offset, width)
        lanes = slice(start, start + width)
        query_head = query[:, lanes] * mask
        key_head = key[:, lanes] * mask
        grad_head = grad[:, lanes] * mask
        soft = soft_columns(nt(key_head, query_head), allowed)
        grad_soft = nt(value[:, lanes], grad_head)
        grad_value[:, lanes] += nn(soft.astype(BF16), grad_head)
        grad_scores = soft * (grad_soft - jnp.sum(soft * grad_soft, axis=0, keepdims=True))
        grad_scores = (grad_scores * SCALE).astype(BF16)
        grad_key[:, lanes] += nn(grad_scores, query_head)
        grad_query[:, lanes] += tn(grad_scores, key_head)


def normal(values):
    centered = values - jnp.mean(values, axis=-1, keepdims=True)
    scale = lax.rsqrt(jnp.mean(centered * centered, axis=-1, keepdims=True) + NORM_EPS)
    return centered * scale, scale


def normal_back(normed, scale, grad):
    return scale * (
        grad
        - jnp.mean(grad, axis=-1, keepdims=True)
        - normed * jnp.mean(grad * normed, axis=-1, keepdims=True)
    )


def gelu_parts(values):
    root = math.sqrt(2.0 / math.pi)
    square = values * values
    bent = jnp.tanh(root * (values + 0.044715 * (values * square)))
    half = 0.5 * (1.0 + bent)
    slope = half + 0.5 * values * (1.0 - bent * bent) * (root * (1.0 + 3 * 0.044715 * square))
    return values * half, slope


def attention_kernel(cross, plan, place, rows6, x, allowed, *refs):
    if cross:
        pair, refs = refs[0], refs[1:]
    count = max(ref for ref, _ in plan) + 1
    weights, refs = refs[:count], refs[count:]
    if cross:
        (middle, packed, projected, lefts, cross_query) = refs[:5]
        refs = refs[5:]
        after_low, cross_mixed = lefts.at[:, :, 2 * D : 3 * D], lefts.at[:, :, 3 * D : 4 * D]
    else:
        (middle, packed, projected, lefts) = refs[:4]
        refs = refs[4:]
    normed, mixed = lefts.at[:, :, 0:D], lefts.at[:, :, D : 2 * D]
    dest, sems, total = refs
    j = place[2]
    indices = [jnp.bitwise_xor(j, k) for k in range(4)]
    if cross:
        c = jnp.bitwise_and(j, 1)
        indices += [4 + c, 5 - c]
    pieces = Pieces(plan, place, weights, dest, sems, indices)
    pieces.start()
    row = [rows6[0, n : n + 1] for n in range(6)]
    inputs = x[0]
    normed[0] = (normal(inputs)[0] * (1.0 + row[1]) + row[0]).astype(BF16)
    pieces.wait(0, 4)
    for n in range(3):
        packed[0, :, n * D : (n + 1) * D] = nn(normed[0], dest[n]).astype(BF16)
    size = allowed.shape[1]
    blocks = x.shape[1] // size
    total[...] = jnp.zeros_like(total)

    @pl.loop(0, blocks)
    def _(r):
        rows = pl.ds(pl.multiple_of(r * size, size), size)
        own = packed.at[0, rows]
        attend_rows(
            own.at[:, 0:D],
            own.at[:, D : 2 * D],
            own.at[:, 2 * D : 3 * D],
            total.at[rows],
            allowed[0],
        )

    mixed[0] = total[...].astype(BF16)
    out = nn(mixed[0], dest[3])
    projected[0] = out
    after = x[0] + row[2] * out
    if not cross:
        middle[0] = after
        return
    middle[0] = after
    after_low[0] = after.astype(BF16)
    pieces.wait(4, 2)
    cross_query[0] = nn(after_low[0], dest[4]).astype(BF16)
    total[...] = jnp.zeros_like(total)

    @pl.loop(0, blocks)
    def _(r):
        rows = pl.ds(pl.multiple_of(r * size, size), size)
        attend_rows(
            cross_query.at[0, rows],
            pair.at[0, :, 0:D],
            pair.at[0, :, D : 2 * D],
            total.at[rows],
            None,
        )

    cross_mixed[0] = total[...].astype(BF16)
    middle[0] += nn(cross_mixed[0], dest[5])


def per_video(shape):
    return pl.BlockSpec((1,) + shape[1:], lambda v: (v,) + (0,) * (len(shape) - 1))


def block_call(kernel, name, place, values, weights, outs, scratch, flops):
    any_spec = pl.BlockSpec(memory_space=pl.ANY)
    moved = sum(v.size * v.dtype.itemsize for v in list(values) + list(weights) + list(outs))
    return pl.pallas_call(
        kernel,
        grid=(values[0].shape[0],),
        out_shape=outs,
        in_specs=[pl.BlockSpec(memory_space=pltpu.SMEM)]
        + [per_video(v.shape) for v in values]
        + [any_spec] * len(weights),
        out_specs=[per_video(v.shape) for v in outs],
        scratch_shapes=scratch,
        compiler_params=pltpu.CompilerParams(
            dimension_semantics=("arbitrary",), vmem_limit_bytes=VMEM_LIMIT
        ),
        cost_estimate=pl.CostEstimate(flops=flops, bytes_accessed=moved, transcendentals=0),
        name=name,
    )(place, *values, *weights)


def weight_scratch(count):
    return [pltpu.VMEM((count, D, D), BF16), pltpu.SemaphoreType.DMA((count, 2 * LINES))]


def plan_of(pieces):
    arrays, plan = [], []
    for piece in pieces:
        for array, entry in piece:
            known = [n for n, one in enumerate(arrays) if one is array]
            if not known:
                arrays.append(array)
            plan.append((known[0] if known else len(arrays) - 1, entry))
    return arrays, plan


def attention_forward(place, rows6, x, allowed, pair, pieces):
    arrays, plan = plan_of(pieces)
    cross = pair is not None
    videos, rows, _ = x.shape

    def shape(width, dtype):
        return jax.ShapeDtypeStruct((videos, rows, width), dtype)

    outs = [shape(D, F32), shape(3 * D, BF16), shape(D, F32), shape((4 if cross else 2) * D, BF16)]
    if cross:
        outs += [shape(D, BF16)]
    values = [rows6, x, allowed] + ([pair] if cross else [])
    return block_call(
        lambda *refs: attention_kernel(cross, plan, *refs),
        "attention_forward",
        place,
        values,
        arrays,
        outs,
        weight_scratch(len(pieces)) + [pltpu.VMEM((rows, D), F32)],
        2 * videos * rows * D * (len(pieces) * D + 1024),
    )


def cross_back_kernel(plan, place, grad, pair, query, *refs):
    count = max(ref for ref, _ in plan) + 1
    weights, refs = refs[:count], refs[count:]
    grad_x, rights, grad_pair, dest, sems, grad_mixed, grad_q = refs
    c = jnp.bitwise_and(place[2], 1)
    pieces = Pieces(plan, place, weights, dest, sems, [c, 1 - c])
    pieces.start()
    size = QUERIES
    blocks = grad.shape[1] // size
    grad_query, grad_out = rights.at[:, :, 0:D], rights.at[:, :, D : 2 * D]
    grad_out[0] = grad[0].astype(BF16)
    pieces.wait(0, 2)
    grad_mixed[...] = nt(grad_out[0], dest[1]).astype(BF16)
    grad_q[...] = jnp.zeros_like(grad_q)
    grad_pair[...] = jnp.zeros_like(grad_pair)

    @pl.loop(0, blocks)
    def _(r):
        rows = pl.ds(pl.multiple_of(r * size, size), size)
        attend_rows_back(
            query.at[0, rows],
            pair.at[0, :, 0:D],
            pair.at[0, :, D : 2 * D],
            grad_mixed.at[rows],
            grad_q.at[rows],
            grad_pair.at[0, :, 0:D],
            grad_pair.at[0, :, D : 2 * D],
            None,
        )

    grad_query[0] = grad_q[...].astype(BF16)
    grad_x[0] = grad[0] + nt(grad_query[0], dest[0])


def cross_backward(place, grad, pair, query, pieces):
    arrays, plan = plan_of(pieces)
    videos, rows, _ = grad.shape
    return block_call(
        lambda *refs: cross_back_kernel(plan, *refs),
        "cross_backward",
        place,
        [grad, pair, query],
        arrays,
        [
            jax.ShapeDtypeStruct((videos, rows, D), F32),
            jax.ShapeDtypeStruct((videos, rows, 2 * D), BF16),
            jax.ShapeDtypeStruct(pair.shape, F32),
        ],
        weight_scratch(2) + [pltpu.VMEM((rows, D), BF16), pltpu.VMEM((rows, D), F32)],
        2 * videos * rows * D * (2 * D + 1024),
    )


def attention_back_kernel(plan, place, rows6, x, allowed, packed, projected, grad, *refs):
    count = max(ref for ref, _ in plan) + 1
    weights, refs = refs[:count], refs[count:]
    grad_x, rights, six, dest, sems, grad_mixed, grad_q, grad_k, grad_v = refs
    grad_packed, grad_proj = rights.at[:, :, 0 : 3 * D], rights.at[:, :, 3 * D : 4 * D]
    j = place[2]
    pieces = Pieces(
        plan, place, weights, dest, sems, [jnp.bitwise_xor(j, k) for k in range(4)]
    )
    pieces.start()
    row = [rows6[0, n : n + 1] for n in range(6)]
    size = allowed.shape[1]
    blocks = x.shape[1] // size
    six[0, 2:3] = jnp.sum(grad[0] * projected[0], axis=0, keepdims=True)
    grad_proj[0] = (grad[0] * row[2]).astype(BF16)
    pieces.wait(0, 4)
    grad_mixed[...] = nt(grad_proj[0], dest[3]).astype(BF16)
    for one in (grad_q, grad_k, grad_v):
        one[...] = jnp.zeros_like(one)

    @pl.loop(0, blocks)
    def _(r):
        rows = pl.ds(pl.multiple_of(r * size, size), size)
        own = packed.at[0, rows]
        attend_rows_back(
            own.at[:, 0:D],
            own.at[:, D : 2 * D],
            own.at[:, 2 * D : 3 * D],
            grad_mixed.at[rows],
            grad_q.at[rows],
            grad_k.at[rows],
            grad_v.at[rows],
            allowed[0],
        )

    for n, one in enumerate((grad_q, grad_k, grad_v)):
        grad_packed[0, :, n * D : (n + 1) * D] = one[...].astype(BF16)
    grad_q[...] = nt(grad_packed[0, :, 0:D], dest[0])
    grad_q[...] += nt(grad_packed[0, :, D : 2 * D], dest[1])
    grad_q[...] += nt(grad_packed[0, :, 2 * D : 3 * D], dest[2])
    normed, scale = normal(x[0])
    six[0, 0:1] = jnp.sum(grad_q[...], axis=0, keepdims=True)
    six[0, 1:2] = jnp.sum(grad_q[...] * normed, axis=0, keepdims=True)
    grad_x[0] = grad[0] + normal_back(normed, scale, grad_q[...] * (1.0 + row[1]))


def attention_backward(place, rows6, x, allowed, packed, projected, grad, pieces):
    arrays, plan = plan_of(pieces)
    videos, rows, _ = x.shape
    return block_call(
        lambda *refs: attention_back_kernel(plan, *refs),
        "attention_backward",
        place,
        [rows6, x, allowed, packed, projected, grad],
        arrays,
        [
            jax.ShapeDtypeStruct((videos, rows, D), F32),
            jax.ShapeDtypeStruct((videos, rows, 4 * D), BF16),
            jax.ShapeDtypeStruct((videos, 8, D), F32),
        ],
        weight_scratch(len(pieces))
        + [pltpu.VMEM((rows, D), BF16)]
        + [pltpu.VMEM((rows, D), F32)] * 3,
        2 * videos * rows * D * (len(pieces) * D + 2048),
    )


def mlp_kernel(plan, place, rows6, x, *refs):
    count = max(ref for ref, _ in plan) + 1
    weights, refs = refs[:count], refs[count:]
    hidden, normed, ups, active, lowered, dest, sems = refs
    pieces = Pieces(plan, place, weights, dest, sems, range(8))
    pieces.start()
    row = [rows6[0, n : n + 1] for n in range(6)]
    normed[0] = (normal(x[0])[0] * (1.0 + row[4]) + row[3]).astype(BF16)
    for n in range(4):
        lanes = slice(n * D, (n + 1) * D)
        pieces.wait(n, 1)
        pieces.wait(4 + n, 1)
        up = nn(normed[0], dest[n])
        ups[0, :, lanes] = up
        active[0, :, lanes] = gelu_parts(up)[0].astype(BF16)
        part = nt(active[0, :, lanes], dest[4 + n])
        if n == 0:
            lowered[0] = part
        else:
            lowered[0] += part
    hidden[0] = x[0] + row[5] * lowered[0]


def mlp_forward(place, rows6, x, up, down):
    arrays, plan = plan_of(up + down)
    videos, rows, _ = x.shape

    def shape(width, dtype):
        return jax.ShapeDtypeStruct((videos, rows, width), dtype)

    return block_call(
        lambda *refs: mlp_kernel(plan, *refs),
        "mlp_forward",
        place,
        [rows6, x],
        arrays,
        [shape(D, F32), shape(D, BF16), shape(FF, F32), shape(FF, BF16), shape(D, F32)],
        weight_scratch(8),
        4 * videos * rows * D * FF,
    )


def mlp_back_kernel(plan, place, rows6, x, ups, lowered, grad, *refs):
    count = max(ref for ref, _ in plan) + 1
    weights, refs = refs[:count], refs[count:]
    grad_x, grad_ups, six, dest, sems, total = refs
    pieces = Pieces(plan, place, weights, dest, sems, range(8))
    pieces.start()
    row = [rows6[0, n : n + 1] for n in range(6)]
    six[0, 5:6] = jnp.sum(grad[0] * lowered[0], axis=0, keepdims=True)
    grad_low = (grad[0] * row[5]).astype(BF16)
    for n in range(4):
        lanes = slice(n * D, (n + 1) * D)
        pieces.wait(n, 1)
        pieces.wait(4 + n, 1)
        grad_active = nn(grad_low, dest[4 + n])
        grad_ups[0, :, lanes] = (grad_active * gelu_parts(ups[0, :, lanes])[1]).astype(BF16)
        part = nt(grad_ups[0, :, lanes], dest[n])
        if n == 0:
            total[...] = part
        else:
            total[...] += part
    normed, scale = normal(x[0])
    six[0, 3:4] = jnp.sum(total[...], axis=0, keepdims=True)
    six[0, 4:5] = jnp.sum(total[...] * normed, axis=0, keepdims=True)
    grad_x[0] = grad[0] + normal_back(normed, scale, total[...] * (1.0 + row[4]))


def mlp_backward(place, rows6, x, ups, lowered, grad, up, down):
    arrays, plan = plan_of(up + down)
    videos, rows, _ = x.shape

    def shape(width, dtype):
        return jax.ShapeDtypeStruct((videos, rows, width), dtype)

    return block_call(
        lambda *refs: mlp_back_kernel(plan, *refs),
        "mlp_backward",
        place,
        [rows6, x, ups, lowered, grad],
        arrays,
        [
            shape(D, F32),
            shape(FF, BF16),
            jax.ShapeDtypeStruct((videos, 8, D), F32),
        ],
        weight_scratch(8) + [pltpu.VMEM((rows, D), F32)],
        4 * videos * rows * D * FF,
    )


def outer_kernel(received, lefts_at, rights_at, place, left, right, *refs):
    added, out = refs[:received], refs[received]
    z, y = place[0], place[1]
    total = tn(left[...], right[...])
    for row in range(LINES):
        for column in range(2):
            at = (row * 2 + column) * BLOCK
            block = total[at : at + BLOCK]
            where = (jnp.bitwise_xor(column, y), jnp.bitwise_xor(row, z))
            for one in added:
                block = block + one[0, where[0], where[1]].astype(F32)
            out[0, where[0], where[1]] = block.astype(BF16)


def outer_pieces(place, lefts, rights, which, added=()):
    lefts, rights = lefts.reshape(-1, lefts.shape[-1]), rights.reshape(-1, rights.shape[-1])
    count = len(which)
    rows = lefts.shape[0]
    tables = [
        jnp.stack([jnp.asarray(pick[n], jnp.int32) for pick in which]) for n in range(2)
    ]
    shape = (count, 2, LINES, BLOCK, D)
    piece = pl.BlockSpec((1,) + shape[1:], lambda n, *_: (n, 0, 0, 0, 0))
    return pl.pallas_call(
        lambda *refs: outer_kernel(len(added), *refs),
        grid_spec=pltpu.PrefetchScalarGridSpec(
            num_scalar_prefetch=3,
            grid=(count,),
            in_specs=[
                pl.BlockSpec((rows, D), lambda n, l, r, p: (0, l[n])),
                pl.BlockSpec((rows, D), lambda n, l, r, p: (0, r[n])),
            ]
            + [piece] * len(added),
            out_specs=piece,
        ),
        out_shape=jax.ShapeDtypeStruct(shape, BF16),
        compiler_params=pltpu.CompilerParams(
            dimension_semantics=("arbitrary",), vmem_limit_bytes=VMEM_LIMIT
        ),
        cost_estimate=pl.CostEstimate(
            flops=2 * count * rows * D * D,
            bytes_accessed=2 * count * D * (2 * rows + D * (1 + len(added))),
            transcendentals=0,
        ),
        name="outer_pieces",
    )(*tables, place, lefts, rights, *added)


def optimizer_step(grad, first_old, second_old, master):
    first = BETA_ONE * first_old + (1.0 - BETA_ONE) * grad
    second = BETA_TWO * second_old + (1.0 - BETA_TWO) * grad * grad
    update = (
        first
        / (1.0 - BETA_ONE**STEP)
        / (jnp.sqrt(second / (1.0 - BETA_TWO**STEP)) + ADAM_EPS)
        + DECAY_RATE * master
    )
    return first, second, update


def moments_kernel(ranges, order, scale, *refs):
    grads, refs = refs[: len(ranges)], refs[len(ranges) :]
    first_old, second_old, master, first, second, update, squares, grad = refs
    n = pl.program_id(0)
    for one, pieces in zip(grads, ranges):

        @pl.when((n >= pieces[0]) & (n <= pieces[-1]))
        def _(one=one, pieces=pieces):
            grad[...] = one[0].astype(F32)

    value = grad[...] * scale[0]
    first[...], second[...], step = optimizer_step(
        value, first_old[...], second_old[...], master[...]
    )
    update[...] = step.astype(BF16)
    squares[0, 0:1] = jnp.sum(step * step, axis=0, keepdims=True)
    squares[0, 1:2] = jnp.sum(master[...] * master[...], axis=0, keepdims=True)


def moments(groups, order, scale, first_old, second_old, master):
    rows, width = master.shape
    count = width // D
    column = pl.BlockSpec((rows, D), lambda n, *_: (0, n))
    whole = jax.ShapeDtypeStruct(master.shape, F32)

    def entry(low, high):
        return pl.BlockSpec(
            (1, rows, D), lambda n, order, s: (order[jnp.clip(n, low, high)], 0, 0)
        )

    return pl.pallas_call(
        lambda *refs: moments_kernel([(low, high) for low, high, _ in groups], *refs),
        grid_spec=pltpu.PrefetchScalarGridSpec(
            num_scalar_prefetch=2,
            grid=(count,),
            in_specs=[entry(low, high) for low, high, _ in groups] + [column] * 3,
            out_specs=[column] * 3 + [pl.BlockSpec((1, 2, D), lambda n, *_: (n, 0, 0))],
            scratch_shapes=[pltpu.VMEM((rows, D), F32)],
        ),
        out_shape=[
            whole,
            whole,
            jax.ShapeDtypeStruct(master.shape, BF16),
            jax.ShapeDtypeStruct((count, 2, D), F32),
        ],
        compiler_params=pltpu.CompilerParams(
            dimension_semantics=("arbitrary",), vmem_limit_bytes=VMEM_LIMIT
        ),
        cost_estimate=pl.CostEstimate(
            flops=20 * master.size, bytes_accessed=24 * master.size, transcendentals=0
        ),
        name="moments",
    )(order, scale, *[grads for _, _, grads in groups], first_old, second_old, master)


def row_moments_kernel(scale, grad, first_old, second_old, master, first, second, update, squares):
    grad = grad[...].astype(F32) * scale[0]
    first[...], second[...], step = optimizer_step(
        grad, first_old[...], second_old[...], master[...]
    )
    update[...] = step.astype(BF16)

    @pl.when(pl.program_id(0) == 0)
    def _():
        squares[...] = jnp.zeros_like(squares)

    squares[0:1] += jnp.sum(step * step, axis=0, keepdims=True)
    squares[1:2] += jnp.sum(master[...] * master[...], axis=0, keepdims=True)


def row_step(rows):
    return 16 if rows % 16 == 0 else rows


def row_moments(scale, grads, first_old, second_old, master):
    rows, width = master.shape
    step = row_step(rows)
    block = pl.BlockSpec((step, width), lambda n, *_: (n, 0))
    whole = jax.ShapeDtypeStruct(master.shape, F32)
    return pl.pallas_call(
        row_moments_kernel,
        grid_spec=pltpu.PrefetchScalarGridSpec(
            num_scalar_prefetch=1,
            grid=(rows // step,),
            in_specs=[block] * 4,
            out_specs=[block] * 3 + [pl.BlockSpec((2, width), lambda n, *_: (0, 0))],
        ),
        out_shape=[
            whole,
            whole,
            jax.ShapeDtypeStruct(master.shape, BF16),
            jax.ShapeDtypeStruct((2, width), F32),
        ],
        compiler_params=pltpu.CompilerParams(
            dimension_semantics=("arbitrary",), vmem_limit_bytes=VMEM_LIMIT
        ),
        cost_estimate=pl.CostEstimate(
            flops=20 * master.size, bytes_accessed=24 * master.size, transcendentals=0
        ),
        name="row_moments",
    )(scale, grads, first_old, second_old, master)


def apply_kernel(trust, master, update, new, copy):
    value = master[...] - trust[...] * update[...].astype(F32)
    new[...] = value
    copy[...] = value.astype(BF16)


def apply_pieces_kernel(trust, master, update, new, copy):
    value = master[...] - trust[pl.program_id(0)] * update[...].astype(F32)
    new[...] = value
    copy[...] = value.astype(BF16)


def apply_update(trust, master, update):
    rows, width = master.shape
    step = row_step(rows)
    outs = [
        jax.ShapeDtypeStruct(master.shape, F32),
        jax.ShapeDtypeStruct(master.shape, BF16),
    ]
    params = pltpu.CompilerParams(
        dimension_semantics=("arbitrary",), vmem_limit_bytes=VMEM_LIMIT
    )
    cost = pl.CostEstimate(
        flops=4 * master.size, bytes_accessed=12 * master.size, transcendentals=0
    )
    if trust.ndim == 1:
        block = pl.BlockSpec((rows, D), lambda n, *_: (0, n))
        return pl.pallas_call(
            apply_pieces_kernel,
            grid_spec=pltpu.PrefetchScalarGridSpec(
                num_scalar_prefetch=1,
                grid=(width // D,),
                in_specs=[block, block],
                out_specs=[block, block],
            ),
            out_shape=outs,
            compiler_params=params,
            cost_estimate=cost,
            name="apply_pieces",
        )(trust, master, update)
    block = pl.BlockSpec((step, width), lambda n: (n, 0))
    return pl.pallas_call(
        apply_kernel,
        grid=(rows // step,),
        in_specs=[pl.BlockSpec((1, width), lambda n: (0, 0)), block, block],
        out_specs=[block, block],
        out_shape=outs,
        compiler_params=params,
        cost_estimate=cost,
        name="apply_update",
    )(trust, master, update)


def own_piece(shard, index):
    return lax.dynamic_slice(shard, (0, index * D), (shard.shape[0], D)).astype(BF16)


def pick_kernel(count, spatial_at, temporal_at, spatial, temporal, out):
    n = pl.program_id(0)

    @pl.when(n < count)
    def _():
        out[0] = spatial[...].astype(BF16)

    @pl.when(n >= count)
    def _():
        out[0] = temporal[...].astype(BF16)


def own_pieces(spatial, temporal, spatial_at, temporal_at):
    rows = spatial.shape[0]
    count, total = len(spatial_at), len(spatial_at) + len(temporal_at)
    spatial_at = spatial_at + spatial_at[-1:] * len(temporal_at)
    temporal_at = temporal_at[:1] * count + temporal_at
    tables = [
        jnp.stack([jnp.asarray(one, jnp.int32) for one in at]) for at in (spatial_at, temporal_at)
    ]
    return pl.pallas_call(
        lambda *refs: pick_kernel(count, *refs),
        grid_spec=pltpu.PrefetchScalarGridSpec(
            num_scalar_prefetch=2,
            grid=(total,),
            in_specs=[
                pl.BlockSpec((rows, D), lambda n, s, t: (0, s[n])),
                pl.BlockSpec((rows, D), lambda n, s, t: (0, t[n])),
            ],
            out_specs=pl.BlockSpec((1, rows, D), lambda n, *_: (n, 0, 0)),
        ),
        out_shape=jax.ShapeDtypeStruct((total, rows, D), BF16),
        compiler_params=pltpu.CompilerParams(
            dimension_semantics=("arbitrary",), vmem_limit_bytes=VMEM_LIMIT
        ),
        name="own_pieces",
    )(*tables, spatial, temporal)


def gathered_piece(shard, index):
    rows = lax.all_gather(own_piece(shard, index), "fsdp", axis=0, tiled=True)
    blocks = jnp.swapaxes(rows.reshape(LINES, 2, BLOCK, D), 0, 1)
    return ((blocks, 0), (blocks, 1))


def plus(kept, received):
    return (kept.astype(F32) + received.astype(F32)).astype(BF16)


def scatter_whole(pieces):
    whole = jnp.swapaxes(pieces, 1, 2).reshape(pieces.shape[0], D, D)
    return lax.psum_scatter(whole, "fsdp", scatter_dimension=1, tiled=True)


class Scatter:
    def __init__(self, pieces):
        self.pieces = pieces
        self.explicit = few("fsdp")

    def along_y(self, after=()):
        if not self.explicit:
            return self.pieces
        self.half = swap(gate(self.pieces[:, 1], after), "fsdp", 1)
        return self.half

    def along_z(self, after=()):
        if not self.explicit:
            return self.pieces
        self.half = plus(self.pieces[:, 0], self.half)
        self.quarter = swap(gate(self.half[:, 2:], after), "fsdp", 4)
        return self.quarter

    def end(self, after=()):
        if not self.explicit:
            self.rows = scatter_whole(self.pieces)
            return self.rows
        quarter = plus(self.half[:, :2], self.quarter)
        self.rows = plus(quarter[:, 0], swap(gate(quarter[:, 1], after), "fsdp", 2))
        return self.rows


def share(total):
    total = plus(total, swap(total[::-1], "frame", 2))
    return total, swap(total, "frame", 1)


def exchange_parts(parts):
    sent = swap(jnp.stack([parts[1], parts[3]]), "frame", 1)
    crossed = swap(jnp.stack([parts[2], sent[1]]), "frame", 2)
    return [parts[0], sent[0], crossed[0], crossed[1]]


def to_tokens(values):
    j, size = lax.axis_index("frame"), lax.axis_size("frame")
    videos, frames, tokens, width = values.shape
    part = tokens // (size * frames)
    halves = tokens // (size * part)
    cut = values.reshape(videos, frames, size, halves, part, width)
    parts = exchange_parts(
        [lax.dynamic_index_in_dim(cut, j ^ k, 2, False) for k in range(size)]
    )
    received = [jnp.swapaxes(one, 1, 2) for one in parts]
    return jnp.stack(received, axis=2).reshape(videos, halves * tokens, width)


def from_tokens(values, frames):
    j, size = lax.axis_index("frame"), lax.axis_size("frame")
    videos, rows, width = values.shape
    tokens_part = rows // (size * frames)
    tokens = tokens_part * size
    part = tokens // (size * frames)
    halves = tokens_part // part
    cut = values.reshape(videos, halves, size, frames, part, width)
    whole = jnp.zeros((videos, frames, size, halves, part, width), values.dtype)
    for k, block in enumerate(exchange_parts([cut[:, :, k] for k in range(size)])):
        block = jnp.swapaxes(block, 1, 2)[:, :, None]
        whole = lax.dynamic_update_slice_in_dim(whole, block, j ^ k, axis=2)
    return whole.reshape(videos, frames, tokens, width)


def local(
    latents,
    added_noise,
    text_states,
    timesteps,
    token_counts,
    frame_counts,
    w_shared,
    w_spatial,
    w_temporal,
    shift_tables,
    m_shared,
    m_spatial,
    m_temporal,
    m_tables,
    v_shared,
    v_spatial,
    v_temporal,
    v_tables,
):
    i, j = lax.axis_index("fsdp"), lax.axis_index("frame")
    c = j % 2
    n_fsdp, n_frame = lax.axis_size("fsdp"), lax.axis_size("frame")
    rows_own = w_shared.shape[0]
    frames = latents.shape[2]
    frames_all = frames * n_frame
    videos = latents.shape[0] * latents.shape[1]
    tokens = latents.shape[3]
    texts = text_states.shape[2]

    explicit = few("fsdp")
    if explicit:
        mine = own_pieces(
            w_spatial,
            w_temporal,
            [j, jnp.where(c == 0, 4, 7), 8 + j, 12 + j],
            [j, 4 + j, 4 + (j ^ 2), 8 + j, 8 + (j ^ 2)],
        )
        first, rest = mine[:1], mine[1:]
        first_near = jnp.stack([first, swap(first, "fsdp", 2)], axis=1)

    shared_parts = split_columns(w_shared, shared_widths())
    if explicit:
        shared_parts = gate(shared_parts, [first])
    patch_own, time_one, caption_w, time_two, mod_w, final_own = shared_parts
    time_one, time_two, mod_w = [one.astype(BF16) for one in (time_one, time_two, mod_w)]
    pair_w = w_spatial[:, 5 * D : 7 * D].astype(BF16)
    steps_own = timesteps.reshape(videos)
    steps_two = jnp.concatenate([steps_own // 32, steps_own % 32]).astype(BF16)[:, None]
    small = jnp.concatenate(
        [
            patch_own.T.astype(BF16),
            final_own.T.astype(BF16),
            shift_tables.T.astype(BF16),
            jnp.broadcast_to(steps_two, (2 * videos, rows_own)),
        ]
    )
    small = jnp.pad(small, ((0, -small.shape[0] % 16), (0, 0)))
    small = collect(small, "fsdp")
    at = 2 * PCH + 14
    steps_all = small[:, at : at + 2 * videos, 0].astype(F32)
    steps_all = steps_all[:, :videos] * 32.0 + steps_all[:, videos:]
    small = jnp.swapaxes(to_relative(small, "fsdp"), 0, 1).reshape(small.shape[1], D)
    patch_w, final_w = small[:PCH], small[PCH : 2 * PCH]
    tables = small[2 * PCH : at].astype(F32)

    cond_index = jnp.where(few("fsdp"), i, 0)
    place = jnp.stack([cond_index // 2, cond_index % 2, j]).astype(jnp.int32)

    step_float = timesteps.reshape(videos).astype(F32)
    token_count = token_counts.reshape(videos)
    alpha_bar = jnp.cos((step_float / 1000.0 + 0.008) / 1.008 * (math.pi / 2)) ** 2
    snr_value = alpha_bar / (1.0 - alpha_bar)
    loss_weight = jnp.minimum(snr_value, SNR_GAMMA) / snr_value

    half_count = FREQ // 2
    frequency = jnp.exp(-math.log(10000.0) * jnp.arange(half_count, dtype=F32) / half_count)
    angles = steps_all.reshape(-1)[:, None] * frequency[None, :]
    features = jnp.concatenate([jnp.cos(angles), jnp.sin(angles)], axis=-1).astype(BF16)
    hidden_pre = dot_t(features, time_one)
    hidden_act = jax.nn.silu(hidden_pre).astype(BF16)
    embedding_all = sum_relative(dot(hidden_act, time_two).reshape(n_fsdp, videos, D), "fsdp")
    embedding = embedding_all[0]
    embedding_part = lax.dynamic_slice(
        embedding_all.reshape(-1, D), (0, i * rows_own), (n_fsdp * videos, rows_own)
    )
    embed_act = jax.nn.silu(embedding_part).astype(BF16)
    mod_half = dot(embed_act, lax.dynamic_slice(mod_w, (0, c * 3 * D), (rows_own, 3 * D)))
    mod_half = deliver(mod_half.reshape(n_fsdp, videos, 3 * D), "fsdp")
    mod_other = swap(mod_half, "frame", 1)
    modulation = jnp.concatenate(
        [jnp.where(c == 0, mod_half, mod_other), jnp.where(c == 0, mod_other, mod_half)], axis=1
    ).reshape(videos, 6, D)
    six_spatial = modulation + tables[None, 0:6]
    six_temporal = modulation + tables[None, 6:12]
    final_rows = embedding[:, None, :] + tables[None, 12:14]

    text_part = TXT_D // n_frame
    text_own = text_states.reshape(videos * texts, TXT_D)
    text_own = lax.dynamic_slice(text_own, (0, j * text_part), (videos * texts, text_part))
    text_all = collect(text_own, "fsdp").reshape(-1, text_part)
    caption_part = lax.dynamic_slice(caption_w, (0, j * text_part), (rows_own, text_part))
    caption_part = caption_part.astype(BF16)
    caption_pre = sum_over_frame_low(dot_t(text_all, caption_part))
    caption = gelu_tanh(caption_pre).astype(BF16)
    pair_part = 2 * D // n_frame
    pair_w_part = lax.dynamic_slice(pair_w, (0, j * pair_part), (rows_own, pair_part))
    pair = dot(caption, pair_w_part).astype(BF16).reshape(n_fsdp, videos * texts, pair_part)
    pair = collect(deliver(pair, "fsdp").astype(BF16), "frame")
    pair = jnp.swapaxes(to_relative(pair, "frame"), 0, 1).reshape(videos, texts, 2 * D)

    target = to_tokens(added_noise.reshape(videos, frames, tokens, PCH)).astype(F32)

    if explicit:

        def with_far(near, after):
            return jnp.concatenate([near, swap(gate(near, after), "fsdp", 4)], axis=1)

        def y(lines, after):
            return swap(gate(lines, after), "fsdp", 1)

        def x(lines, after):
            return swap(gate(lines, after), "frame", 2)

        def core(lines, after):
            return swap(gate(lines, after), "frame", 1)

        def joined(*arrays):
            return jnp.concatenate(arrays)

        done = [first_near]
        la = with_far(first_near, done)
        rest_near = jnp.stack([rest, swap(gate(rest, done), "fsdp", 2)], axis=1)
        done = [la, rest_near, text_all]
        lbc = with_far(rest_near[0:2], done)
        ya, xla = y(la, done), x(la, done)
        done = [lbc, ya, xla, caption_pre]
        lde = with_far(rest_near[2:4], done)
        ybc, x1 = y(lbc, done), x(joined(ya, lbc[1:]), done)
        k1 = core(joined(la, xla), done)
        done = [lde, ybc, x1, k1, pair, modulation]
        lf = with_far(rest_near[4:6], done)
        yde, x2 = y(lde, done), x(joined(ybc[1:], lde), done)
        k2 = core(joined(ya, x1[:1], lbc, ybc), done)
        done = [lf, yde, x2, k2]
        lg = with_far(rest_near[6:8], done)
        yf, xyde = y(lf, done), x(yde, done)
        k3 = core(joined(x1[1:], lde, x2, yde), done)
        spatial_attn = [
            ((la, 0), (ya, 0)),
            ((k1, 0), (k2, 0)),
            ((xla, 0), (x1, 0)),
            ((k1, 1), (k2, 1)),
        ]
        cross_attn = [((lbc, 0), (ybc, 0)), ((k2, 2), (k2, 4))]
    else:
        done = []
        spatial_attn = [gathered_piece(w_spatial, j ^ k) for k in range(4)]
        cross_attn = [
            gathered_piece(w_spatial, jnp.where(c == n, 4, 7)) for n in range(2)
        ]
        spatial_up, spatial_down = [
            [gathered_piece(w_spatial, base + (j ^ k)) for k in range(4)] for base in (8, 12)
        ]
        temporal_attn, temporal_up, temporal_down = [
            [gathered_piece(w_temporal, base + (j ^ k)) for k in range(4)] for base in (0, 4, 8)
        ]

    noise_own = added_noise.reshape(videos, frames * tokens, PCH)
    clean = latents.reshape(videos, frames * tokens, PCH).astype(F32)
    noisy = (
        jnp.sqrt(alpha_bar)[:, None, None] * clean
        + jnp.sqrt(1.0 - alpha_bar)[:, None, None] * noise_own.astype(F32)
    ).astype(BF16)
    start = gate(dot(noisy, patch_w), done)
    key_valid = (jnp.arange(tokens)[None, :] < token_count[:, None]).astype(F32)
    spatial_allowed = jnp.broadcast_to(key_valid[:, :, None], (videos, tokens, tokens))
    middle1, packed1, projected1, lefts1, cross_query = attention_forward(
        place, six_spatial, start, spatial_allowed, pair, spatial_attn + cross_attn
    )
    if explicit:
        done = [lg, yf, xyde, k3, middle1, fence(middle1)]
        yg = y(lg, done)
        k4 = core(xyde, done)
        k5 = core(joined(lf, yf), [k4])
        spatial_up = [
            ((lbc, 1), (ybc, 1)),
            ((k2, 3), (k2, 5)),
            ((x1, 1), (x2, 0)),
            ((k3, 0), (k3, 3)),
        ]
        spatial_down, temporal_attn = [
            [
                ((lde, n), (yde, n)),
                ((k3, 1 + n), (k3, 6 + n)),
                ((x2, 1 + n), (xyde, n)),
                ((k3, 4 + n), (k4, n)),
            ]
            for n in range(2)
        ]
        middle1 = gate(middle1, done)
    hidden1, normed1, ups1, active1, lowered1 = mlp_forward(
        place, six_spatial, middle1, spatial_up, spatial_down
    )

    hidden = to_tokens(hidden1.reshape(videos, frames, tokens, D))
    rows = hidden.shape[1]
    part = tokens // frames_all
    clip_ends = jnp.cumsum(frame_counts.reshape(videos, -1), axis=-1)
    block_row = jnp.arange(tokens, dtype=jnp.int32)
    frame_at = ((block_row // (frames * part)) ^ j) * frames + block_row // part % frames
    segment = jnp.sum(
        (frame_at[None, :, None] >= clip_ends[:, None, :]).astype(jnp.int32), axis=-1
    )
    same_token = (block_row % part)[:, None] == (block_row % part)[None, :]
    same = same_token[None] & (segment[:, :, None] == segment[:, None, :])
    temporal_allowed = same.astype(F32)
    token_at = (
        j * (tokens // n_frame)
        + jnp.arange(rows, dtype=jnp.int32) // tokens * part
        + jnp.arange(rows, dtype=jnp.int32) % part
    )
    if explicit:
        done = [yg, k5, hidden]
        k6 = core(joined(lg, yg), done)
        temporal_up, temporal_down = [
            [((l, 0), (b, 0)), ((k, 0), (k, 2)), ((l, 1), (b, 1)), ((k, 1), (k, 3))]
            for l, b, k in ((lf, yf, k5), (lg, yg, k6))
        ]
        hidden = gate(hidden, done)
    middle2, packed2, projected2, lefts2 = attention_forward(
        place, six_temporal, hidden, temporal_allowed, None, temporal_attn
    )
    hidden2, normed2, ups2, active2, lowered2 = mlp_forward(
        place, six_temporal, middle2, temporal_up, temporal_down
    )

    shift_final = final_rows[:, 0][:, None, :]
    scale_final = final_rows[:, 1][:, None, :]
    normed_final = modulate(hidden2, shift_final, scale_final).astype(BF16)
    predicted = dot_t(normed_final, final_w)
    pred_error = predicted - target
    keep_weight = (token_at[None, :] < token_count[:, None]).astype(F32) * loss_weight[:, None]
    keep_weight = keep_weight[:, :, None]
    loss_part = jnp.sum(keep_weight * pred_error * pred_error) / PCH
    weight_part = jnp.sum(loss_weight * token_count.astype(F32)) * frames_all

    grad_pred = (keep_weight * pred_error * (2.0 / PCH)).astype(BF16)
    grad_final_w = outer(grad_pred, normed_final)
    grad_hidden2, grad_shift_final, grad_scale_final = modulate_back(
        hidden2, shift_final, scale_final, dot(grad_pred, final_w)
    )
    slots = [(0, k) for k in range(4)]
    low2 = (grad_hidden2 * six_temporal[:, 5][:, None, :]).astype(BF16)

    def pieces_of(lefts, rights, which, after=(), added=()):
        return outer_pieces(place, gate(lefts, after), rights, which, added)

    other1 = pieces_of(low2, active2, [slots[3], slots[1]])
    core1 = swap(other1, "frame", 1)
    grad_middle2, grad_ups2, six_mlp2 = mlp_backward(
        place,
        six_temporal,
        middle2,
        ups2,
        lowered2,
        gate(grad_hidden2, [other1]),
        temporal_up,
        temporal_down,
    )
    done = [core1, grad_middle2, fence(grad_middle2)]
    second1 = pieces_of(low2, active2, [slots[2]], done, (core1[:1],))
    x1 = swap(second1, "frame", 2)
    other2 = pieces_of(normed2, grad_ups2, [slots[1], slots[3]], [second1])
    core2 = swap(other2, "frame", 1)
    grad_hidden, rights2, six_attn2 = attention_backward(
        place,
        six_temporal,
        hidden,
        temporal_allowed,
        packed2,
        projected2,
        gate(grad_middle2, [other2]),
        temporal_attn,
    )
    done = [core2, grad_hidden, fence(grad_hidden)]
    sum2 = Scatter(pieces_of(normed2, grad_ups2, [slots[0], slots[2]], done, (core2,)))
    y2 = sum2.along_y()
    grad_hidden1 = from_tokens(gate(grad_hidden, [sum2.pieces]), frames)
    grad_hidden1 = grad_hidden1.reshape(videos, frames * tokens, D)
    which2 = [((j ^ k) // 3, j ^ k) for k in range(4)]
    other3 = pieces_of(lefts2, rights2, [which2[3], which2[1]], [sum2.pieces])
    core3 = swap(other3, "frame", 1)
    sum1 = Scatter(pieces_of(low2, active2, [slots[0]], [other3], (core1[1:], x1)))
    y1 = sum1.along_y()
    second3 = pieces_of(lefts2, rights2, [which2[2]], [sum1.pieces], (core3[:1],))
    done = [grad_hidden1, sum1.pieces, second3, y2]
    x3 = swap(gate(second3, done), "frame", 2)
    low1 = (gate(grad_hidden1, done) * six_spatial[:, 5][:, None, :]).astype(BF16)
    other4 = pieces_of(low1, active1, [slots[3], slots[1]])
    core4 = swap(other4, "frame", 1)
    z2 = sum2.along_z(done)
    grad_middle1, grad_ups1, six_mlp1 = mlp_backward(
        place,
        six_spatial,
        middle1,
        ups1,
        lowered1,
        gate(grad_hidden1, [other4]),
        spatial_up,
        spatial_down,
    )
    done = [core4, grad_middle1, fence(grad_middle1), y1]
    second4 = pieces_of(low1, active1, [slots[2]], done, (core4[:1],))
    x4 = swap(second4, "frame", 2)
    z1 = sum1.along_z(done)
    other5 = pieces_of(normed1, grad_ups1, [slots[1], slots[3]], [second4])
    core5 = swap(other5, "frame", 1)
    grad_after1, rights7, grad_pair = cross_backward(
        place, gate(grad_middle1, [other5]), pair, cross_query, cross_attn
    )
    sum3 = Scatter(pieces_of(lefts2, rights2, [which2[0]], [grad_after1], (core3[1:], x3)))
    y3 = sum3.along_y()
    rows2 = sum2.end([sum3.pieces])
    done = [core5, sum3.pieces, z1, z2]
    sum5 = Scatter(pieces_of(normed1, grad_ups1, [slots[0], slots[2]], done, (core5,)))
    y5 = sum5.along_y()
    other7 = pieces_of(lefts1, rights7, [(3 - c, 1 - c)], [sum5.pieces])
    core7 = swap(other7, "frame", 1)
    grad_pair = grad_pair.astype(BF16).reshape(videos * texts, n_frame, pair_part)
    grad_pair = to_relative(jnp.swapaxes(grad_pair, 0, 1), "frame")
    grad_pair = deliver(grad_pair, "frame").astype(BF16)
    rows1 = sum1.end([other7])
    grad_start, rights1, six_attn1 = attention_backward(
        place,
        six_spatial,
        start,
        spatial_allowed,
        packed1,
        projected1,
        gate(grad_after1, [other7]),
        spatial_attn,
    )
    sum4 = Scatter(pieces_of(low1, active1, [slots[0]], [grad_start], (core4[1:], x4)))
    done = [grad_start, core7, y3, sum4.pieces, grad_pair, rows1, rows2]

    along_pair = collect_along(gate(grad_pair, done))
    six_s, six_t = [
        jnp.concatenate([attn[:, 0:3], mlp[:, 3:6]], axis=1)
        for attn, mlp in ((gate(six_attn1, done), six_mlp1), (six_attn2, six_mlp2))
    ]
    grad_final = jnp.stack([grad_shift_final, grad_scale_final], axis=1)
    grad_patch_w = outer(noisy, grad_start.astype(BF16))
    cond = jnp.concatenate(
        [
            grad_patch_w,
            grad_final_w,
            jnp.sum(jnp.concatenate([six_s, six_t, grad_final], axis=1), axis=0),
            jnp.concatenate([six_s + six_t, grad_final], axis=1).reshape(-1, D),
        ]
    )
    cond = sum_over(cond, "frame")

    y4, z3 = sum4.along_y([along_pair]), sum3.along_z([along_pair])
    which1 = [((j ^ k) // 3, j ^ k) for k in range(4)]
    other6 = pieces_of(lefts1, rights1, [which1[1], which1[3]], done)
    core6 = swap(other6, "frame", 1)
    sum7 = Scatter(pieces_of(lefts1, rights7, [(2 + c, c)], [other6], (core7,)))
    y7 = sum7.along_y()
    pair6 = pieces_of(lefts1, rights1, [which1[0], which1[2]], [sum7.pieces], (core6,))
    sum6, sum8 = Scatter(pair6[:1]), Scatter(pair6[1:])
    done = [pair6, y4, z3, y5, along_pair, cond]
    grad_pair = collect_beside(gate(along_pair, done)).reshape(-1, pair_part)
    small_grad = jnp.swapaxes(cond[: 2 * PCH + 14].reshape(-1, n_fsdp, rows_own), 0, 1)
    small_grad = deliver_beside(gate(to_relative(small_grad, "fsdp"), done))
    along_cond = collect_along(
        gate(cond[2 * PCH + 14 :].astype(BF16).reshape(videos, 8, D), done)
    )
    first_sent = [grad_pair, small_grad, along_cond]
    y6 = sum6.along_y(first_sent)
    y8 = sum8.along_y([y7] + first_sent)
    z4, z5 = sum4.along_z(first_sent), sum5.along_z(first_sent)
    rows3 = sum3.end(done)
    done = [y7, z4, z5, rows3] + first_sent
    pair_w_grad = outer(caption, gate(grad_pair, done))
    grad_caption = sum_over_frame_low(dot_t(grad_pair, pair_w_part))
    small_grad = deliver_along(gate(small_grad, done)).T
    cond = collect_beside(gate(along_cond, done)).reshape(n_fsdp * videos, 8, D)
    first_sent = [cond, small_grad]
    z7 = sum7.along_z(first_sent)
    z6 = sum6.along_z([y6] + first_sent)
    rows4, rows5 = sum4.end(done), sum5.end(done)
    done = [y8, z7, rows4, rows5, grad_caption] + first_sent
    grad_caption = jax.vjp(gelu_tanh, caption_pre)[1](gate(grad_caption, done))[0].astype(BF16)
    both = jnp.concatenate([outer(grad_caption, text_all), pair_w_grad], axis=1).astype(BF16)
    both = collect(both, "frame")
    grad_mod = gate(cond, done)[:, :6].reshape(-1, 6 * D)
    mod_grad = outer(embed_act, grad_mod)
    final_part = lax.dynamic_slice(
        cond[:, 6].astype(F32) + cond[:, 7].astype(F32), (0, i * rows_own), embedding_part.shape
    )
    grad_embed = (
        jax.vjp(jax.nn.silu, embedding_part)[1](dot_t(grad_mod, mod_w))[0] + final_part
    ).astype(BF16)
    along_embed = collect_along(grad_embed.reshape(n_fsdp, videos, rows_own))
    z8 = sum8.along_z([along_embed, y8])
    rows7 = sum7.end([along_embed])
    quads = jnp.stack([rows1, rows3, rows4], axis=1)
    slots_two = jnp.stack([rows2, rows5], axis=1)
    crossed = swap(jnp.concatenate([slots_two[1], slots_two[0], quads[0]]), "frame", 2)
    totals = jnp.concatenate([plus(slots_two.reshape(4, rows_own, D), crossed[:4]), quads[0], crossed[4:]])
    done = [z6, z8, rows7, along_embed, totals, both]
    received = collect_beside(gate(along_embed, done))
    rows6, rows8 = sum6.end([received]), sum8.end([received])
    totals_other = swap(gate(totals, done), "frame", 1)
    crossed7 = swap(gate(rows7, done), "frame", 2)
    done = [rows6, rows8, totals_other, crossed7, received]
    last = jnp.concatenate([rows6, rows8])
    crossed = swap(gate(last[::-1], done), "frame", 2)
    last = jnp.concatenate([plus(last, crossed), plus(rows7, crossed7)])
    last_other = swap(last, "frame", 1)

    def in_order(total, other):
        return jnp.stack([total, other], axis=1).reshape((-1,) + total.shape[1:])

    up_grads2, up_grads1, down_grads2, attn_grads2, down_grads1 = [
        in_order(jnp.stack([totals[m], totals[n]]), jnp.stack([totals_other[m], totals_other[n]]))
        for m, n in ((0, 2), (1, 3), (4, 7), (5, 8), (6, 9))
    ]
    attn_grads1 = in_order(last[:2], last_other[:2])
    cross_grads = jnp.concatenate([last[2:], last_other[2:]])
    both = to_relative(both, "frame")
    caption_grad, pair_w_grad = [
        jnp.swapaxes(one, 0, 1).reshape(rows_own, -1)
        for one in (both[:, :, :text_part], both[:, :, text_part:])
    ]
    step = np.arange(n_fsdp)
    grad_embed = received[step[:, None], step[:, None] ^ step[None, :]]
    grad_embed = jnp.transpose(to_relative(grad_embed, "fsdp"), (1, 2, 0, 3)).reshape(-1, D)
    time_two_grad = outer(hidden_act, grad_embed)
    grad_hidden = dot_t(grad_embed, time_two)
    grad_hidden = jax.vjp(jax.nn.silu, hidden_pre)[1](grad_hidden)[0].astype(BF16)
    time_one_grad = outer(grad_hidden, features)
    shared_grads = jnp.concatenate(
        [
            small_grad[:, :PCH].astype(BF16),
            time_one_grad.astype(BF16),
            caption_grad,
            time_two_grad.astype(BF16),
            mod_grad.astype(BF16),
            small_grad[:, PCH : 2 * PCH].astype(BF16),
        ],
        axis=1,
    )

    pair_pieces = jnp.stack([pair_w_grad[:, :D], pair_w_grad[:, D:]])
    tables_grad = small_grad[:, 2 * PCH :]
    relative = jnp.arange(4, dtype=jnp.int32) ^ j
    spatial_order = jnp.concatenate(
        [
            relative,
            jnp.stack([c, 0 * c, 1 + 0 * c, 1 - c]).astype(jnp.int32),
            relative,
            relative,
        ]
    )
    temporal_order = jnp.concatenate([relative, relative, relative])
    spatial_groups = [
        (0, 3, attn_grads1),
        (4, 4, cross_grads),
        (5, 6, pair_pieces),
        (7, 7, cross_grads),
        (8, 11, up_grads1),
        (12, 15, down_grads1),
    ]
    temporal_groups = [(0, 3, attn_grads2), (4, 7, up_grads2), (8, 11, down_grads2)]

    def squares(values, axes=None):
        values = values.astype(F32)
        return jnp.sum(values * values, axis=axes)

    def group_squares(groups, order):
        return jnp.concatenate(
            [
                squares(grads, (1, 2))[order[low : high + 1]]
                for low, high, grads in groups
            ]
        )

    def rows_of(widths, first):
        which = np.repeat(np.arange(len(widths)) + first, widths)
        return jnp.asarray(which)[None, :] == jnp.arange(18)[:, None]

    shared_rows = rows_of(shared_widths(), 0)
    spatial_rows = rows_of([width // D for width in spatial_widths()], 6)
    temporal_rows = rows_of([width // D for width in temporal_widths()], 13)

    def matrix_sums(shared, spatial, temporal, table):
        totals = jnp.where(jnp.arange(18) == 17, table, 0.0)
        for marks, values in (
            (shared_rows, shared),
            (spatial_rows, spatial),
            (temporal_rows, temporal),
        ):
            totals = totals + jnp.sum(jnp.where(marks, values[None, :], 0.0), axis=1)
        return totals

    def spread(marks, values):
        return jnp.sum(jnp.where(marks, values[:, None], 0.0), axis=0)

    grad_part_sq = matrix_sums(
        squares(shared_grads, 0),
        group_squares(spatial_groups, spatial_order),
        group_squares(temporal_groups, temporal_order),
        squares(tables_grad),
    )
    loss_all = sum_over(loss_part[None], "frame")
    numbers = sum_over(jnp.concatenate([grad_part_sq, loss_all, weight_part[None]]), "fsdp")
    grad_sq, loss_sum, weight_total = numbers[:18], numbers[18], numbers[19]
    grad_norm = jnp.sqrt(jnp.sum(grad_sq)) / weight_total
    factor = CLIP_NORM / jnp.maximum(grad_norm, CLIP_NORM)
    grad_scale = factor / weight_total
    scale = grad_scale[None]
    shared_new = row_moments(scale, shared_grads, m_shared, v_shared, w_shared)
    spatial_new = moments(spatial_groups, spatial_order, scale, m_spatial, v_spatial, w_spatial)
    temporal_new = moments(
        temporal_groups, temporal_order, scale, m_temporal, v_temporal, w_temporal
    )
    tables_new = optimizer_step(tables_grad * grad_scale, m_tables, v_tables, shift_tables)
    spatial_sq = jnp.sum(spatial_new[3], axis=2)
    temporal_sq = jnp.sum(temporal_new[3], axis=2)
    numbers = [
        matrix_sums(shared_new[3][n], spatial_sq[:, n], temporal_sq[:, n], squares(table))
        for n, table in enumerate((tables_new[2], shift_tables))
    ]
    numbers = sum_over(jnp.concatenate(numbers), "fsdp")
    update_sq, weight_sq = numbers[:18], numbers[18:]
    trust = LEARN_RATE * jnp.sqrt(weight_sq) / jnp.sqrt(update_sq)
    new_shared, copy_shared = apply_update(
        spread(shared_rows, trust)[None], w_shared, shared_new[2]
    )
    new_spatial, copy_spatial = apply_update(
        spread(spatial_rows, trust), w_spatial, spatial_new[2]
    )
    new_temporal, copy_temporal = apply_update(
        spread(temporal_rows, trust), w_temporal, temporal_new[2]
    )
    new_tables = shift_tables - trust[17] * tables_new[2]
    return (
        loss_sum,
        weight_total,
        grad_norm,
        jnp.stack([jnp.sqrt(weight_sq), jnp.sqrt(update_sq)]),
        jnp.sqrt(grad_sq) * grad_scale,
        new_shared,
        new_spatial,
        new_temporal,
        new_tables,
        shared_new[0],
        spatial_new[0],
        temporal_new[0],
        tables_new[0],
        shared_new[1],
        spatial_new[1],
        temporal_new[1],
        tables_new[1],
        copy_shared,
        copy_spatial,
        copy_temporal,
        new_tables.astype(BF16),
    )


def solution(mesh):
    rows = P("fsdp", None)
    return jax.shard_map(
        local,
        mesh=mesh,
        in_specs=(
            P(None, "fsdp", "frame", None, None),
            P(None, "fsdp", "frame", None, None),
            P(None, "fsdp", None, None),
            P(None, "fsdp"),
            P(None, "fsdp"),
            P(None, "fsdp", None),
        )
        + (rows,) * 12,
        out_specs=(P(),) * 5 + (rows,) * 16,
        check_vma=False,
    )
```

time: 6610 us -> 1670 us (0.25)
  waiting for transfers between devices: 5360 us -> 651 us
  Pallas kernels: 0 us -> 526 us
  matrix products: 480 us -> 17.7 us
  blocking collectives: 176 us -> 0 us
  other arithmetic: 291 us -> 150 us
  starting transfers between devices: 0.67 us -> 123 us
  local copies, waits for them, and re-layouts: 266 us -> 179 us
    reduce_scatter x5 -> x0, waiting for transfers between devices: 3110 us -> none  [the longest x3 3080 us: reduce_one(): share = lax.psum_scatter(grad_full, 'fsdp', scatter_dimension=0, tiled=True)]
    all_gather x5 -> x0, waiting for transfers between devices: 1780 us -> none  [the longest x1 777 us: local(): lax.all_gather(w_spatial.astype(jnp.bfloat16), 'fsdp', axis=0, tiled=True)]
    ppermute x0 -> x121, waiting for transfers between devices: none -> 651 us  [swap(): lax.ppermute(values, axis, [(n, n ^ mask) for n in range(lax.axis_size(ax...]
    pallas_call x0 -> x33, Pallas kernels: none -> 526 us  [the longest x9 283 us: block_call(): pl.pallas_call(kernel, grid=(values[0].shape[0],), out_shape=outs, in_spe...]
    psum x1 -> x0, waiting for transfers between devices: 424 us -> none  [reduce_one(): return lax.psum(share, 'frame')]
    dot_general x61 -> x17, matrix products: 437 us -> 17.7 us  [the longest x7 6.59 us: outer(): lax.dot_general(left.reshape(-1, left.shape[-1]), right.reshape(-1, right...]
    ppermute x0 -> x121, starting transfers between devices: none -> 123 us  [swap(): lax.ppermute(values, axis, [(n, n ^ mask) for n in range(lax.axis_size(ax...]
    psum x4 -> x0, blocking collectives: 108 us -> none  [the longest x2 76.6 us: local(): lax.psum((grad_sq, weight_sq, loss_part, denom_part), ('fsdp', 'frame'))]
  transfers between devices with their start and end apart: 12 -> 121, of which waited for: 11 -> 45; matrix products, arithmetic and copies ran while one was open for 6% -> 17% of each run, Pallas kernels for 0% -> 20%
where the time goes in v1:
time: 1670 us; the launch traced here: 1660 us
  waiting for transfers between devices  651 us (39%)
  Pallas kernels  526 us (31%)
  local copies, waits for them, and re-layouts  179 us (11%)
  other arithmetic  150 us (9%)
  starting transfers between devices  123 us (7%)
  matrix products  17.7 us (1%)
    ppermute x121, waiting for transfers between devices, swap(): lax.ppermute(values, axis, [(n, n ^ mask) for n in range(lax.axis_size(ax...  651 us
    pallas_call x9, Pallas kernels, block_call(): pl.pallas_call(kernel, grid=(values[0].shape[0],), out_shape=outs, in_spe...  283 us
    pallas_call x17, Pallas kernels, outer_pieces(): pl.pallas_call(lambda *refs: outer_kernel(len(added), *refs), grid_spec=p...  125 us
    ppermute x121, starting transfers between devices, swap(): lax.ppermute(values, axis, [(n, n ^ mask) for n in range(lax.axis_size(ax...  123 us
    pallas_call x2, Pallas kernels, moments(): pl.pallas_call(lambda *refs: moments_kernel([(low, high) for low, high, _...  47.5 us
  transfers between devices with their start and end apart: 121, of which 45 were waited for; matrix products, arithmetic and copies ran while one was open for 17% of the time, Pallas kernels for 20%

profile of v1, /device:TPU:0, one launch (start us, length us, event | category | flops | bytes accessed | tf_op | source)
XLA Modules:
  0.0 1658.0 jit_solution(16674664284089037588)
XLA Ops:
  82.0 22.3 %collective-permute-done.15 = bf16[4,128,1024]{2,1,0:T(8,128)(2,1)S(1)} collective-permute-done((bf16[4,128,1024]{2,1,0:T(8,128)(2,1)S(1)}, bf16[4,128,1024]{2,1,0:T(8,128)(2,1)S(1)}, u32[]{:S(2)}, u32[]{:S(2)}) %collective-permute-start.15) | collective-permute-done | bytes 1048608 | tf_op jit(solution)/shard_map/ppermute | solution.py:38
  111.2 25.1 %collective-permute-done.7 = f32[2,2,3456]{2,1,0:T(2,128)S(1)} collective-permute-done((f32[2,2,3456]{2,1,0:T(2,128)S(1)}, f32[2,2,3456]{2,1,0:T(2,128)S(1)}, u32[]{:S(2)}, u32[]{:S(2)}) %collective-permute-start.7) | collective-permute-done | bytes 55328 | tf_op jit(solution)/shard_map/ppermute | solution.py:38
  157.7 56.7 %collective-permute-done.26 = bf16[2,128,576]{1,2,0:T(8,128)(2,1)S(1)} collective-permute-done((bf16[2,128,576]{1,2,0:T(8,128)(2,1)S(1)}, bf16[2,128,576]{1,2,0:T(8,128)(2,1)S(1)}, u32[]{:S(2)}, u32[]{:S(2)}) %collective-permute-start.26) | collective-permute-done | bytes 294944 | tf_op jit(solution)/shard_map/ppermute | solution.py:38
  230.9 59.4 %collective-permute-done.29 = bf16[2,128,576]{1,2,0:T(8,128)(2,1)S(1)} collective-permute-done((bf16[2,128,576]{1,2,0:T(8,128)(2,1)S(1)}, bf16[2,128,576]{1,2,0:T(8,128)(2,1)S(1)}, u32[]{:S(2)}, u32[]{:S(2)}) %collective-permute-start.29) | collective-permute-done | bytes 294944 | tf_op jit(solution)/shard_map/ppermute | solution.py:38
  316.0 57.2 %collective-permute-done.30 = bf16[2,2,144,1152]{3,2,1,0:T(8,128)(2,1)S(1)} collective-permute-done((bf16[2,2,144,1152]{3,2,1,0:T(8,128)(2,1)S(1)}, bf16[2,2,144,1152]{3,2,1,0:T(8,128)(2,1)S(1)}, u32[]{:S(2)}, u32[]{:S(2)}) %collective-permute-start.30) | collective-permute-done | bytes 1327136 | tf_op jit(solution)/shard_map/ppermute | solution.py:38
  375.1 23.2 %collective-permute-done.32.refs_7_.refs_10_ = bf16[3,4,144,1152]{3,2,1,0:T(8,128)(2,1)S(1)} collective-permute-done((bf16[3,4,144,1152]{3,2,1,0:T(8,128)(2,1)S(1)}, bf16[3,4,144,1152]{3,2,1,0:T(8,128)(2,1)S(1)}, u32[]{:S(2)}, u32[]{:S(2)}) %collective-permute-start.32) | collective-permute-done | bytes 3981344 | tf_op jit(solution)/shard_map/ppermute | solution.py:38
  421.9 47.0 %attention_forward.2 = (f32[2,256,1152]{2,1,0:T(8,128)}, bf16[2,256,3456]{2,1,0:T(8,128)(2,1)}, f32[2,256,1152]{2,1,0:T(8,128)}, bf16[2,256,4608]{2,1,0:T(8,128)(2,1)}, bf16[2,256,1152]{2,1,0:T(8,128)(2,1)}) custom-call(s32[3]{0:T(128)} %pad_add_fusion.refs_0_.refs_2_, f32[2,6,1152]{2,1,0:T(8,128)} %get-tuple-element.584.refs_1_, ...), custom_call_target="tpu_custom_call" | custom-call | flops 9361686528 | bytes 39852032 | tf_op jit(solution)/shard_map/attention_forward/pallas_call | solution.py:405
  487.1 26.3 %mlp_forward.2 = (f32[2,256,1152]{2,1,0:T(8,128)}, bf16[2,256,1152]{2,1,0:T(8,128)(2,1)}, f32[2,256,4608]{2,1,0:T(8,128)}, bf16[2,256,4608]{2,1,0:T(8,128)(2,1)}, f32[2,256,1152]{2,1,0:T(8,128)}) custom-call(s32[3]{0:T(128)} %pad_add_fusion.refs_0_.refs_2_, f32[2,6,1152]{2,1,0:T(8,128)} %get-tuple-element.584.refs_1_, ...), custom_call_target="tpu_custom_call" | custom-call | flops 10871635968 | bytes 63608832 | tf_op jit(solution)/shard_map/mlp_forward/pallas_call | solution.py:405
  519.5 26.9 %collective-permute-done.42.refs_7_.refs_10_ = bf16[2,4,144,1152]{3,2,1,0:T(8,128)(2,1)} collective-permute-done((bf16[2,4,144,1152]{3,2,1,0:T(8,128)(2,1)S(1)}, bf16[2,4,144,1152]{3,2,1,0:T(8,128)(2,1)}, u32[]{:S(2)}, u32[]{:S(2)}) %collective-permute-start.42) | collective-permute-done | bytes 2654240 | tf_op jit(solution)/shard_map/ppermute | solution.py:38
  567.6 26.9 %attention_forward.3 = (f32[2,256,1152]{2,1,0:T(8,128)}, bf16[2,256,3456]{2,1,0:T(8,128)(2,1)}, f32[2,256,1152]{2,1,0:T(8,128)}, bf16[2,256,2304]{2,1,0:T(8,128)(2,1)}) custom-call(s32[3]{0:T(128)} %pad_add_fusion.refs_0_.refs_2_, f32[2,6,1152]{2,1,0:T(8,128)} %copy-done.74, f32[2,256,1152]{2,1,0:T(8,128)} %bitcast.572, ...), custom_call_target="tpu_custom_call" | custom-call | flops 6643777536 | bytes 38377472 | tf_op jit(solution)/shard_map/attention_forward/pallas_call | solution.py:405
  594.6 26.7 %mlp_forward.3 = (f32[2,256,1152]{2,1,0:T(8,128)}, bf16[2,256,1152]{2,1,0:T(8,128)(2,1)}, f32[2,256,4608]{2,1,0:T(8,128)}, bf16[2,256,4608]{2,1,0:T(8,128)(2,1)}, f32[2,256,1152]{2,1,0:T(8,128)}) custom-call(s32[3]{0:T(128)} %pad_add_fusion.refs_0_.refs_2_, f32[2,6,1152]{2,1,0:T(8,128)} %copy-done.74, f32[2,256,1152]{2,1,0:T(8,128)} %get-tuple-element.195.refs_2_, ...), custom_call_target="tpu_custom_call" | custom-call | flops 10871635968 | bytes 43702272 | tf_op jit(solution)/shard_map/mlp_forward/pallas_call | solution.py:405
  638.0 29.5 %mlp_backward.2 = (f32[2,256,1152]{2,1,0:T(8,128)}, bf16[2,256,4608]{2,1,0:T(8,128)(2,1)}, f32[2,8,1152]{2,1,0:T(8,128)}) custom-call(s32[3]{0:T(128)} %pad_add_fusion.refs_0_.refs_2_, f32[2,6,1152]{2,1,0:T(8,128)} %copy-done.74, f32[2,256,1152]{2,1,0:T(8,128)} %get-tuple-element.195.refs_2_, f32[2,256,4608]{2,1,0:T(8,128)} %get-tuple-element.197.refs_3_, ...), custom_call_target="tpu_custom_call" | custom-call | flops 10871635968 | bytes 44955648 | tf_op jit(solution)/shard_map/mlp_backward/pallas_call | solution.py:405
  688.3 35.0 %attention_backward.2 = (f32[2,256,1152]{2,1,0:T(8,128)}, bf16[2,256,4608]{2,1,0:T(8,128)(2,1)}, f32[2,8,1152]{2,1,0:T(8,128)}) custom-call(s32[3]{0:T(128)} %pad_add_fusion.refs_0_.refs_2_, f32[2,6,1152]{2,1,0:T(8,128)} %copy-done.74, f32[2,256,1152]{2,1,0:T(8,128)} %bitcast.573, f32[2,128,128]{2,1,0:T(8,128)} %and_convert_fusion.refs_3_, ...), custom_call_target="tpu_custom_call" | custom-call | flops 7851737088 | bytes 43169792 | tf_op jit(solution)/shard_map/attention_backward/pallas_call | solution.py:405
  760.4 42.5 %collective-permute-done.51.refs_6_ = bf16[1,2,4,144,1152]{4,3,2,1,0:T(8,128)(2,1)} collective-permute-done((bf16[1,2,4,144,1152]{4,3,2,1,0:T(8,128)(2,1)}, bf16[1,2,4,144,1152]{4,3,2,1,0:T(8,128)(2,1)}, u32[]{:S(2)}, u32[]{:S(2)}) %collective-permute-start.51) | collective-permute-done | bytes 2654240 | tf_op jit(solution)/shard_map/ppermute | solution.py:38
  876.0 29.7 %mlp_backward.3 = (f32[2,256,1152]{2,1,0:T(8,128)}, bf16[2,256,4608]{2,1,0:T(8,128)(2,1)}, f32[2,8,1152]{2,1,0:T(8,128)}) custom-call(s32[3]{0:T(128)} %pad_add_fusion.refs_0_.refs_2_, f32[2,6,1152]{2,1,0:T(8,128)} %get-tuple-element.584.refs_1_, f32[2,256,1152]{2,1,0:T(8,128)} %get-tuple-element.185.refs_2_, f32[2,256,4608]{2,1,0:T(8,128)} %get-tuple-element.187.refs_3_, ...), custom_call_target="tpu_custom_call" | custom-call | flops 10871635968 | bytes 64862208 | tf_op jit(solution)/shard_map/mlp_backward/pallas_call | solution.py:405
  936.9 26.4 %cross_backward.1 = (f32[2,256,1152]{2,1,0:T(8,128)}, bf16[2,256,2304]{2,1,0:T(8,128)(2,1)}, f32[2,64,2304]{2,1,0:T(8,128)}) custom-call(s32[3]{0:T(128)} %pad_add_fusion.refs_0_.refs_2_, f32[2,256,1152]{2,1,0:T(8,128)} %get-tuple-element.224.refs_1_, bf16[2,64,2304]{2,1,0:T(8,128)(2,1)} %reshape.819.refs_4_.refs_2_, ...), custom_call_target="tpu_custom_call" | custom-call | flops 3925868544 | bytes 23298048 | tf_op jit(solution)/shard_map/cross_backward/pallas_call | solution.py:405
  1038.2 35.2 %attention_backward.3 = (f32[2,256,1152]{2,1,0:T(8,128)}, bf16[2,256,4608]{2,1,0:T(8,128)(2,1)}, f32[2,8,1152]{2,1,0:T(8,128)}) custom-call(s32[3]{0:T(128)} %pad_add_fusion.refs_0_.refs_2_, f32[2,6,1152]{2,1,0:T(8,128)} %get-tuple-element.584.refs_1_, f32[2,256,1152]{2,1,0:T(8,128)} %fusion.154.refs_2_, f32[2,128,128]{2,1,0:T(8,128)} %broadcast_in_dim.292.refs_3_, ...), custom_call_target="tpu_custom_call" | custom-call | flops 7851737088 | bytes 35207168 | tf_op jit(solution)/shard_map/attention_backward/pallas_call | solution.py:405
  1120.0 27.5 %collective-permute-done.75 = bf16[1,2,144,1152]{3,2,1,0:T(8,128)(2,1)} collective-permute-done((bf16[1,2,144,1152]{3,2,1,0:T(8,128)(2,1)}, bf16[1,2,144,1152]{3,2,1,0:T(8,128)(2,1)}, u32[]{:S(2)}, u32[]{:S(2)}) %collective-permute-start.75) | collective-permute-done | bytes 663584 | tf_op jit(solution)/shard_map/ppermute | solution.py:38
  1152.6 20.0 %collective-permute-done.74 = bf16[1,4,144,1152]{3,2,1,0:T(8,128)(2,1)} collective-permute-done((bf16[1,4,144,1152]{3,2,1,0:T(8,128)(2,1)}, bf16[1,4,144,1152]{3,2,1,0:T(8,128)(2,1)}, u32[]{:S(2)}, u32[]{:S(2)}) %collective-permute-start.74) | collective-permute-done | bytes 1327136 | tf_op jit(solution)/shard_map/ppermute | solution.py:38
  1227.4 76.2 %collective-permute-done.83 = bf16[1,2,144,1152]{3,2,1,0:T(8,128)(2,1)S(1)} collective-permute-done((bf16[1,2,144,1152]{3,2,1,0:T(8,128)(2,1)}, bf16[1,2,144,1152]{3,2,1,0:T(8,128)(2,1)S(1)}, u32[]{:S(2)}, u32[]{:S(2)}) %collective-permute-start.83) | collective-permute-done | bytes 663584 | tf_op jit(solution)/shard_map/ppermute | solution.py:38
  1320.9 27.5 %collective-permute-done.92 = bf16[1,144,1152]{2,1,0:T(8,128)(2,1)S(1)} collective-permute-done((bf16[1,144,1152]{2,1,0:T(8,128)(2,1)S(1)}, bf16[1,144,1152]{2,1,0:T(8,128)(2,1)S(1)}, u32[]{:S(2)}, u32[]{:S(2)}) %collective-permute-start.92) | collective-permute-done | bytes 331808 | tf_op jit(solution)/shard_map/ppermute | solution.py:38
  1522.4 20.1 %row_moments.1 = (f32[144,12448]{1,0:T(8,128)}, f32[144,12448]{1,0:T(8,128)}, bf16[144,12448]{1,0:T(8,128)(2,1)}, f32[2,12448]{1,0:T(2,128)}) custom-call(f32[1]{0:T(128)} %bitcast.252.scale.refs_1_, bf16[144,12448]{1,0:T(8,128)(2,1)} %concatenate.208.grad, f32[144,12448]{1,0:T(8,128)} %first_old.1, f32[144,12448]{1,0:T(8,128)} %second_old.1, ...), custom_call_target="tpu_custom_call" | custom-call | flops 35850240 | bytes 43020288 | tf_op jit(solution)/shard_map/row_moments/pallas_call | solution.py:811
  1543.8 27.1 %moments.2 = (f32[144,18432]{1,0:T(8,128)}, f32[144,18432]{1,0:T(8,128)}, bf16[144,18432]{1,0:T(8,128)(2,1)}, f32[16,2,1152]{2,1,0:T(2,128)}) custom-call(s32[16]{0:T(128)} %concatenate.215.refs_0_, f32[1]{0:T(128)} %bitcast.252.scale.refs_1_, bf16[4,144,1152]{2,1,0:T(8,128)(2,1)} %bitcast.603, bf16[2,144,1152]{2,1,0:T(8,128)(2,1)} %pad_maximum_fusion.34.refs_3_.refs_5_, ...), custom_call_target="tpu_custom_call" | custom-call | flops 53084160 | bytes 63700992 | tf_op jit(solution)/shard_map/moments/pallas_call | solution.py:762
  1572.1 20.4 %moments.3 = (f32[144,13824]{1,0:T(8,128)}, f32[144,13824]{1,0:T(8,128)}, bf16[144,13824]{1,0:T(8,128)(2,1)}, f32[12,2,1152]{2,1,0:T(2,128)}) custom-call(s32[12]{0:T(128)} %pad_add_fusion.7.refs_0_, f32[1]{0:T(128)} %bitcast.252.scale.refs_1_, bf16[4,144,1152]{2,1,0:T(8,128)(2,1)} %bitcast.606, bf16[4,144,1152]{2,1,0:T(8,128)(2,1)} %bitcast.605, ...), custom_call_target="tpu_custom_call" | custom-call | flops 39813120 | bytes 47775744 | tf_op jit(solution)/shard_map/moments/pallas_call | solution.py:762
  (987 shorter events, 833.0 us)
Async XLA Ops:
  65.7 78.2 %collective-permute-start.11 = (bf16[8,144,1152]{2,1,0:T(8,128)(2,1)}, bf16[8,144,1152]{2,1,0:T(8,128)(2,1)}, u32[]{:S(2)}, u32[]{:S(2)}) collective-permute-start(bf16[8,144,1152]{2,1,0:T(8,128)(2,1)} %get-tuple-element.164), channel_id=1, source_target_pairs={{0,8},{4,12},{8,0},{12,4},{16,24},{20,28},{24,16},{28,20},{1,9},{5... | collective-permute-start | bytes 7962632 | tf_op jit(solution)/shard_map/ppermute | solution.py:38
  66.3 72.1 %collective-permute-start.12 = (bf16[1,2,144,1152]{3,2,1,0:T(8,128)(2,1)}, bf16[1,2,144,1152]{3,2,1,0:T(8,128)(2,1)}, u32[]{:S(2)}, u32[]{:S(2)}) collective-permute-start(bf16[1,2,144,1152]{3,2,1,0:T(8,128)(2,1)} %pad_maximum_fusion.32), channel_id=1, source_target_pairs={{0,16},{4,20},{8,24},{12,28},{16,0},{20,4},{24,8},{28,12},{1,17},{... | collective-permute-start | bytes 1990664 | tf_op jit(solution)/shard_map/ppermute | solution.py:38
  147.2 72.6 %collective-permute-start.16 = (bf16[2,2,144,1152]{3,2,1,0:T(8,128)(2,1)S(1)}, bf16[2,2,144,1152]{3,2,1,0:T(8,128)(2,1)S(1)}, u32[]{:S(2)}, u32[]{:S(2)}) collective-permute-start(bf16[2,2,144,1152]{3,2,1,0:T(8,128)(2,1)S(1)} %get-tuple-element.166), channel_id=1, source_target_pairs={{0,16},{4,20},{8,24},{12,28},{16,0},{20,4},{24,8},{28,12},{1,17},{... | collective-permute-start | bytes 3981320 | tf_op jit(solution)/shard_map/ppermute | solution.py:38
  154.9 70.0 %collective-permute-start.9 = (f32[2,3456]{1,0:T(2,128)S(1)}, f32[2,3456]{1,0:T(2,128)S(1)}, u32[]{:S(2)}, u32[]{:S(2)}) collective-permute-start(f32[2,3456]{1,0:T(2,128)S(1)} %fusion.66), channel_id=1, source_target_pairs={{0,1},{1,0},{2,3},{3,2},{4,5},{5,4},{6,7},{7,6},{8,9},{9,8},{10,11... | collective-permute-start | bytes 82952 | tf_op jit(solution)/shard_map/ppermute | solution.py:38
  156.2 67.5 %collective-permute-start.18 = (bf16[1,4,144,1152]{3,2,1,0:T(8,128)(2,1)S(1)}, bf16[1,4,144,1152]{3,2,1,0:T(8,128)(2,1)S(1)}, u32[]{:S(2)}, u32[]{:S(2)}) collective-permute-start(bf16[1,4,144,1152]{3,2,1,0:T(8,128)(2,1)S(1)} %pad_maximum_fusion.17.refs_5_.refs_7_), channel_id=1, source_target_pairs={{0,2},{1,3},{2,0},{3,1},{4,6},{5,7},{6,4},{7,5},{8,10},{9,11},{10,... | collective-permute-start | bytes 3981320 | tf_op jit(solution)/shard_map/ppermute | solution.py:38
  223.7 75.1 %collective-permute-start.23 = (bf16[2,4,144,1152]{3,2,1,0:T(8,128)(2,1)}, bf16[2,4,144,1152]{3,2,1,0:T(8,128)(2,1)}, u32[]{:S(2)}, u32[]{:S(2)}) collective-permute-start(bf16[2,4,144,1152]{3,2,1,0:T(8,128)(2,1)} %pad_maximum_fusion.8), channel_id=1, source_target_pairs={{0,2},{1,3},{2,0},{3,1},{4,6},{5,7},{6,4},{7,5},{8,10},{9,11},{10,... | collective-permute-start | bytes 7962632 | tf_op jit(solution)/shard_map/ppermute | solution.py:38
  224.9 76.8 %collective-permute-start.22 = (bf16[2,4,144,1152]{3,2,1,0:T(8,128)(2,1)}, bf16[2,4,144,1152]{3,2,1,0:T(8,128)(2,1)}, u32[]{:S(2)}, u32[]{:S(2)}) collective-permute-start(bf16[2,4,144,1152]{3,2,1,0:T(8,128)(2,1)} %pad_maximum_fusion.6.refs_11_.refs_3_.refs_6_.refs_4_), channel_id=1, source_target_pairs={{0,4},{4,0},{8,12},{12,8},{16,20},{20,16},{24,28},{28,24},{1,5},{5... | collective-permute-start | bytes 7962632 | tf_op jit(solution)/shard_map/ppermute | solution.py:38
  227.2 69.5 %collective-permute-start.21 = (bf16[2,2,144,1152]{3,2,1,0:T(8,128)(2,1)}, bf16[2,2,144,1152]{3,2,1,0:T(8,128)(2,1)}, u32[]{:S(2)}, u32[]{:S(2)}) collective-permute-start(bf16[2,2,144,1152]{3,2,1,0:T(8,128)(2,1)} %get-tuple-element.169), channel_id=1, source_target_pairs={{0,16},{4,20},{8,24},{12,28},{16,0},{20,4},{24,8},{28,12},{1,17},{... | collective-permute-start | bytes 3981320 | tf_op jit(solution)/shard_map/ppermute | solution.py:38
  306.2 100.2 %collective-permute-start.33 = (bf16[6,4,144,1152]{3,2,1,0:T(8,128)(2,1)S(1)}, bf16[6,4,144,1152]{3,2,1,0:T(8,128)(2,1)S(1)}, u32[]{:S(2)}, u32[]{:S(2)}) collective-permute-start(bf16[6,4,144,1152]{3,2,1,0:T(8,128)(2,1)S(1)} %pad_maximum_fusion.2), channel_id=1, source_target_pairs={{0,1},{1,0},{2,3},{3,2},{4,5},{5,4},{6,7},{7,6},{8,9},{9,8},{10,11... | collective-permute-start | bytes 23887880 | tf_op jit(solution)/shard_map/ppermute | solution.py:38
  310.3 88.0 %collective-permute-start.32 = (bf16[3,4,144,1152]{3,2,1,0:T(8,128)(2,1)S(1)}, bf16[3,4,144,1152]{3,2,1,0:T(8,128)(2,1)S(1)}, u32[]{:S(2)}, u32[]{:S(2)}) collective-permute-start(bf16[3,4,144,1152]{3,2,1,0:T(8,128)(2,1)S(1)} %maximum_maximum_fusion), channel_id=1, source_target_pairs={{0,2},{1,3},{2,0},{3,1},{4,6},{5,7},{6,4},{7,5},{8,10},{9,11},{10,... | collective-permute-start | bytes 11943944 | tf_op jit(solution)/shard_map/ppermute | solution.py:38
  409.6 70.6 %collective-permute-start.37 = (bf16[8,4,144,1152]{3,2,1,0:T(8,128)(2,1)}, bf16[8,4,144,1152]{3,2,1,0:T(8,128)(2,1)}, u32[]{:S(2)}, u32[]{:S(2)}) collective-permute-start(bf16[8,4,144,1152]{3,2,1,0:T(8,128)(2,1)} %pad_maximum_fusion), channel_id=1, source_target_pairs={{0,1},{1,0},{2,3},{3,2},{4,5},{5,4},{6,7},{7,6},{8,9},{9,8},{10,11... | collective-permute-start | bytes 31850504 | tf_op jit(solution)/shard_map/ppermute | solution.py:38
  412.4 67.8 %collective-permute-start.36 = (bf16[2,4,144,1152]{3,2,1,0:T(8,128)(2,1)}, bf16[2,4,144,1152]{3,2,1,0:T(8,128)(2,1)}, u32[]{:S(2)}, u32[]{:S(2)}) collective-permute-start(bf16[2,4,144,1152]{3,2,1,0:T(8,128)(2,1)} %copy-done.6), channel_id=1, source_target_pairs={{0,2},{1,3},{2,0},{3,1},{4,6},{5,7},{6,4},{7,5},{8,10},{9,11},{10,... | collective-permute-start | bytes 7962632 | tf_op jit(solution)/shard_map/ppermute | solution.py:38
  739.5 90.1 %collective-permute-start.52 = (bf16[2,2,4,144,1152]{4,3,2,1,0:T(8,128)(2,1)}, bf16[2,2,4,144,1152]{4,3,2,1,0:T(8,128)(2,1)}, u32[]{:S(2)}, u32[]{:S(2)}) collective-permute-start(bf16[2,2,4,144,1152]{4,3,2,1,0:T(8,128)(2,1)} %outer_pieces.21), channel_id=1, source_target_pairs={{0,1},{1,0},{2,3},{3,2},{4,5},{5,4},{6,7},{7,6},{8,9},{9,8},{10,11... | collective-permute-start | bytes 15925256 | tf_op jit(solution)/shard_map/ppermute | solution.py:38
  752.5 74.8 %collective-permute-start.50 = (f32[2,2,2,2,16,1152]{5,4,2,3,1,0:T(8,128)}, f32[2,2,2,2,16,1152]{5,4,2,3,1,0:T(8,128)}, u32[]{:S(2)}, u32[]{:S(2)}) collective-permute-start(f32[2,2,2,2,16,1152]{5,4,2,3,1,0:T(8,128)} %pad_maximum_fusion.27), channel_id=1, source_target_pairs={{0,2},{1,3},{2,0},{3,1},{4,6},{5,7},{6,4},{7,5},{8,10},{9,11},{10,... | collective-permute-start | bytes 3538952 | tf_op jit(solution)/shard_map/ppermute | solution.py:38
  759.3 83.0 %collective-permute-start.53 = (bf16[2,4,144,1152]{3,2,0,1:T(8,128)(2,1)}, bf16[2,4,144,1152]{3,2,0,1:T(8,128)(2,1)}, u32[]{:S(2)}, u32[]{:S(2)}) collective-permute-start(bf16[2,4,144,1152]{3,2,0,1:T(8,128)(2,1)} %bitcast.546), channel_id=1, source_target_pairs={{0,4},{4,0},{8,12},{12,8},{16,20},{20,16},{24,28},{28,24},{1,5},{5... | collective-permute-start | bytes 7962632 | tf_op jit(solution)/shard_map/ppermute | solution.py:38
  875.1 96.2 %collective-permute-start.58 = (bf16[1,2,4,144,1152]{4,3,2,1,0:T(8,128)(2,1)}, bf16[1,2,4,144,1152]{4,3,2,1,0:T(8,128)(2,1)}, u32[]{:S(2)}, u32[]{:S(2)}) collective-permute-start(bf16[1,2,4,144,1152]{4,3,2,1,0:T(8,128)(2,1)} %outer_pieces.23), channel_id=1, source_target_pairs={{0,2},{1,3},{2,0},{3,1},{4,6},{5,7},{6,4},{7,5},{8,10},{9,11},{10,... | collective-permute-start | bytes 7962632 | tf_op jit(solution)/shard_map/ppermute | solution.py:38
  926.0 89.7 %collective-permute-start.57 = (bf16[2,2,4,144,1152]{4,3,2,1,0:T(8,128)(2,1)}, bf16[2,2,4,144,1152]{4,3,2,1,0:T(8,128)(2,1)}, u32[]{:S(2)}, u32[]{:S(2)}) collective-permute-start(bf16[2,2,4,144,1152]{4,3,2,1,0:T(8,128)(2,1)} %outer_pieces.26), channel_id=1, source_target_pairs={{0,1},{1,0},{2,3},{3,2},{4,5},{5,4},{6,7},{7,6},{8,9},{9,8},{10,11... | collective-permute-start | bytes 15925256 | tf_op jit(solution)/shard_map/ppermute | solution.py:38
  970.1 103.3 %collective-permute-start.63 = (bf16[1,2,4,144,1152]{4,3,2,1,0:T(8,128)(2,1)S(1)}, bf16[1,2,4,144,1152]{4,3,2,1,0:T(8,128)(2,1)}, u32[]{:S(2)}, u32[]{:S(2)}) collective-permute-start(bf16[1,2,4,144,1152]{4,3,2,1,0:T(8,128)(2,1)S(1)} %copy-done.56), channel_id=1, source_target_pairs={{0,2},{1,3},{2,0},{3,1},{4,6},{5,7},{6,4},{7,5},{8,10},{9,11},{10,... | collective-permute-start | bytes 7962632 | tf_op jit(solution)/shard_map/ppermute | solution.py:38
  1098.0 78.2 %collective-permute-start.70 = (bf16[2,2,4,144,1152]{4,3,2,1,0:T(8,128)(2,1)}, bf16[2,2,4,144,1152]{4,3,2,1,0:T(8,128)(2,1)}, u32[]{:S(2)}, u32[]{:S(2)}) collective-permute-start(bf16[2,2,4,144,1152]{4,3,2,1,0:T(8,128)(2,1)} %outer_pieces.31), channel_id=1, source_target_pairs={{0,1},{1,0},{2,3},{3,2},{4,5},{5,4},{6,7},{7,6},{8,9},{9,8},{10,11... | collective-permute-start | bytes 15925256 | tf_op jit(solution)/shard_map/ppermute | solution.py:38
  1214.7 89.2 %collective-permute-start.84 = (bf16[2,2,144,1152]{3,2,0,1:T(8,128)(2,1)}, bf16[2,2,144,1152]{3,2,0,1:T(8,128)(2,1)S(1)}, u32[]{:S(2)}, u32[]{:S(2)}) collective-permute-start(bf16[2,2,144,1152]{3,2,0,1:T(8,128)(2,1)} %slice.1078), channel_id=1, source_target_pairs={{0,16},{4,20},{8,24},{12,28},{16,0},{20,4},{24,8},{28,12},{1,17},{... | collective-permute-start | bytes 3981320 | tf_op jit(solution)/shard_map/ppermute | solution.py:38
  1215.5 88.1 %collective-permute-start.83 = (bf16[1,2,144,1152]{3,2,1,0:T(8,128)(2,1)}, bf16[1,2,144,1152]{3,2,1,0:T(8,128)(2,1)S(1)}, u32[]{:S(2)}, u32[]{:S(2)}) collective-permute-start(bf16[1,2,144,1152]{3,2,1,0:T(8,128)(2,1)} %slice.1075), channel_id=1, source_target_pairs={{0,16},{4,20},{8,24},{12,28},{16,0},{20,4},{24,8},{28,12},{1,17},{... | collective-permute-start | bytes 1990664 | tf_op jit(solution)/shard_map/ppermute | solution.py:38
  1220.0 88.7 %collective-permute-start.90 = (bf16[1,4,144,1152]{3,2,1,0:T(8,128)(2,1)}, bf16[1,4,144,1152]{3,2,1,0:T(8,128)(2,1)S(1)}, u32[]{:S(2)}, u32[]{:S(2)}) collective-permute-start(bf16[1,4,144,1152]{3,2,1,0:T(8,128)(2,1)} %get-tuple-element.261), channel_id=1, source_target_pairs={{0,4},{4,0},{8,12},{12,8},{16,20},{20,16},{24,28},{28,24},{1,5},{5... | collective-permute-start | bytes 3981320 | tf_op jit(solution)/shard_map/ppermute | solution.py:38
  1221.6 88.4 %collective-permute-start.99 = (bf16[1,4,144,1152]{3,2,1,0:T(8,128)(2,1)}, bf16[1,4,144,1152]{3,2,1,0:T(8,128)(2,1)S(1)}, u32[]{:S(2)}, u32[]{:S(2)}) collective-permute-start(bf16[1,4,144,1152]{3,2,1,0:T(8,128)(2,1)} %get-tuple-element.266), channel_id=1, source_target_pairs={{0,4},{4,0},{8,12},{12,8},{16,20},{20,16},{24,28},{28,24},{1,5},{5... | collective-permute-start | bytes 3981320 | tf_op jit(solution)/shard_map/ppermute | solution.py:38
  1350.9 89.9 %collective-permute-start.103 = (bf16[7,144,1152]{2,1,0:T(8,128)(2,1)}, bf16[7,144,1152]{2,1,0:T(8,128)(2,1)}, u32[]{:S(2)}, u32[]{:S(2)}) collective-permute-start(bf16[7,144,1152]{2,1,0:T(8,128)(2,1)} %pad_maximum_fusion.13), channel_id=1, source_target_pairs={{0,2},{1,3},{2,0},{3,1},{4,6},{5,7},{6,4},{7,5},{8,10},{9,11},{10,... | collective-permute-start | bytes 6967304 | tf_op jit(solution)/shard_map/ppermute | solution.py:38
  (238 other events, 5056.0 us)

commit v2 on v1

--- a/solution.py
+++ b/solution.py
@@ -81,34 +81,48 @@
     return jnp.swapaxes(blocks.reshape((2, size // 2) + values.shape), 0, 1).reshape(blocks.shape)
 
 
-def collect_along(values):
-    if not few("fsdp"):
-        return values
-    size = lax.axis_size("fsdp")
-    return jnp.stack([values] + [swap(values, "fsdp", mask) for mask in range(2, size, 2)])
-
-
-def collect_beside(along):
-    if not few("fsdp"):
-        return collect(along, "fsdp")
-    both = jnp.stack([along, swap(along, "fsdp", 1)], axis=1)
-    return both.reshape((-1,) + along.shape[1:])
-
-
-def deliver_beside(blocks):
-    if not few("fsdp"):
-        return blocks
-    pairs = blocks.reshape((-1, 2) + blocks.shape[1:])
-    return pairs[:, 0] + swap(pairs[:, 1], "fsdp", 1)
-
-
-def deliver_along(half):
-    if not few("fsdp"):
-        return deliver(half, "fsdp")
-    total = half[0]
-    for k in range(1, half.shape[0]):
-        total = total + swap(half[k], "fsdp", 2 * k)
-    return total
+class Collect:
+    def __init__(self, values):
+        self.values = values
+        self.explicit = few("fsdp")
+        if self.explicit:
+            size = lax.axis_size("fsdp")
+            self.sent = [swap(values, "fsdp", mask) for mask in range(2, size, 2)]
+
+    def beside(self, after=()):
+        if self.explicit:
+            self.values = jnp.stack([self.values] + gate(self.sent, after))
+            self.sent = swap(self.values, "fsdp", 1)
+
+    def all(self, after=()):
+        if not self.explicit:
+            return collect(self.values, "fsdp")
+        both = jnp.stack([self.values, gate(self.sent, after)], axis=1)
+        return both.reshape((-1,) + self.values.shape[1:])
+
+
+class Deliver:
+    def __init__(self, blocks):
+        self.blocks = blocks
+        self.explicit = few("fsdp")
+        if self.explicit:
+            self.pairs = blocks.reshape((-1, 2) + blocks.shape[1:])
+            self.sent = [
+                swap(self.pairs[k], "fsdp", 2 * k) for k in range(1, self.pairs.shape[0])
+            ]
+
+    def beside(self, after=()):
+        if self.explicit:
+            sent = gate(self.sent, after)
+            self.half = self.pairs[0]
+            for one in sent:
+                self.half = self.half + one
+            self.sent = swap(self.half[1], "fsdp", 1)
+
+    def total(self, after=()):
+        if not self.explicit:
+            return deliver(self.blocks, "fsdp")
+        return self.half[0] + gate(self.sent, after)
 
 
 def fence(values):
@@ -212,6 +226,7 @@
 QUERIES = 128
 BLOCK = D // (2 * LINES)
 VMEM_LIMIT = 58 * 2**20
+SHORT = pl.CostEstimate(flops=1000, bytes_accessed=1000, transcendentals=0)
 SCALE = 1.0 / math.sqrt(HEAD_DIM)
 
 
@@ -414,7 +429,7 @@
         compiler_params=pltpu.CompilerParams(
             dimension_semantics=("arbitrary",), vmem_limit_bytes=VMEM_LIMIT
         ),
-        cost_estimate=pl.CostEstimate(flops=flops, bytes_accessed=moved, transcendentals=0),
+        cost_estimate=SHORT,
         name=name,
     )(place, *values, *weights)
 
@@ -669,21 +684,29 @@
     )
 
 
-def outer_kernel(received, lefts_at, rights_at, place, left, right, *refs):
-    added, out = refs[:received], refs[received]
+def outer_kernel(received, split, lefts_at, rights_at, place, left, right, *refs):
+    added, outs = refs[:received], refs[received:]
     z, y = place[0], place[1]
     total = tn(left[...], right[...])
-    for row in range(LINES):
-        for column in range(2):
-            at = (row * 2 + column) * BLOCK
-            block = total[at : at + BLOCK]
-            where = (jnp.bitwise_xor(column, y), jnp.bitwise_xor(row, z))
-            for one in added:
-                block = block + one[0, where[0], where[1]].astype(F32)
-            out[0, where[0], where[1]] = block.astype(BF16)
-
-
-def outer_pieces(place, lefts, rights, which, added=()):
+
+    def store(own):
+        for row in range(LINES):
+            for column in range(2):
+                at = (row * 2 + column) * BLOCK
+                block = total[at : at + BLOCK]
+                beside, along = column ^ own, jnp.bitwise_xor(row, z)
+                for one in added:
+                    block = block + one[0, beside, along].astype(F32)
+                if split:
+                    outs[beside][0, along] = block.astype(BF16)
+                else:
+                    outs[0][0, beside, along] = block.astype(BF16)
+
+    for own in range(2):
+        pl.when(y == own)(lambda own=own: store(own))
+
+
+def outer_pieces(place, lefts, rights, which, added=(), split=False):
     lefts, rights = lefts.reshape(-1, lefts.shape[-1]), rights.reshape(-1, rights.shape[-1])
     count = len(which)
     rows = lefts.shape[0]
@@ -692,8 +715,10 @@
     ]
     shape = (count, 2, LINES, BLOCK, D)
     piece = pl.BlockSpec((1,) + shape[1:], lambda n, *_: (n, 0, 0, 0, 0))
+    half = (count, LINES, BLOCK, D)
+    half_piece = pl.BlockSpec((1,) + half[1:], lambda n, *_: (n, 0, 0, 0))
     return pl.pallas_call(
-        lambda *refs: outer_kernel(len(added), *refs),
+        lambda *refs: outer_kernel(len(added), split, *refs),
         grid_spec=pltpu.PrefetchScalarGridSpec(
             num_scalar_prefetch=3,
             grid=(count,),
@@ -702,17 +727,15 @@
                 pl.BlockSpec((rows, D), lambda n, l, r, p: (0, r[n])),
             ]
             + [piece] * len(added),
-            out_specs=piece,
+            out_specs=[half_piece] * 2 if split else piece,
         ),
-        out_shape=jax.ShapeDtypeStruct(shape, BF16),
+        out_shape=[jax.ShapeDtypeStruct(half, BF16)] * 2
+        if split
+        else jax.ShapeDtypeStruct(shape, BF16),
         compiler_params=pltpu.CompilerParams(
             dimension_semantics=("arbitrary",), vmem_limit_bytes=VMEM_LIMIT
         ),
-        cost_estimate=pl.CostEstimate(
-            flops=2 * count * rows * D * D,
-            bytes_accessed=2 * count * D * (2 * rows + D * (1 + len(added))),
-            transcendentals=0,
-        ),
+        cost_estimate=SHORT,
         name="outer_pieces",
     )(*tables, place, lefts, rights, *added)
 
@@ -721,22 +744,21 @@
     first = BETA_ONE * first_old + (1.0 - BETA_ONE) * grad
     second = BETA_TWO * second_old + (1.0 - BETA_TWO) * grad * grad
     update = (
-        first
-        / (1.0 - BETA_ONE**STEP)
-        / (jnp.sqrt(second / (1.0 - BETA_TWO**STEP)) + ADAM_EPS)
+        (first * (1.0 / (1.0 - BETA_ONE**STEP)))
+        / (jnp.sqrt(second * (1.0 / (1.0 - BETA_TWO**STEP))) + ADAM_EPS)
         + DECAY_RATE * master
     )
     return first, second, update
 
 
-def moments_kernel(ranges, order, scale, *refs):
-    grads, refs = refs[: len(ranges)], refs[len(ranges) :]
+def moments_kernel(arrays, source, entry, scale, *refs):
+    grads, refs = refs[:arrays], refs[arrays:]
     first_old, second_old, master, first, second, update, squares, grad = refs
     n = pl.program_id(0)
-    for one, pieces in zip(grads, ranges):
-
-        @pl.when((n >= pieces[0]) & (n <= pieces[-1]))
-        def _(one=one, pieces=pieces):
+    for number, one in enumerate(grads):
+
+        @pl.when(source[n] == number)
+        def _(one=one):
             grad[...] = one[0].astype(F32)
 
     value = grad[...] * scale[0]
@@ -748,23 +770,24 @@
     squares[0, 1:2] = jnp.sum(master[...] * master[...], axis=0, keepdims=True)
 
 
-def moments(groups, order, scale, first_old, second_old, master):
+def moments(arrays, source, entry, scale, first_old, second_old, master):
     rows, width = master.shape
     count = width // D
     column = pl.BlockSpec((rows, D), lambda n, *_: (0, n))
     whole = jax.ShapeDtypeStruct(master.shape, F32)
 
-    def entry(low, high):
+    def block(number):
         return pl.BlockSpec(
-            (1, rows, D), lambda n, order, s: (order[jnp.clip(n, low, high)], 0, 0)
+            (1, rows, D),
+            lambda n, source, entry, _: (jnp.where(source[n] == number, entry[n], 0), 0, 0),
         )
 
     return pl.pallas_call(
-        lambda *refs: moments_kernel([(low, high) for low, high, _ in groups], *refs),
+        lambda *refs: moments_kernel(len(arrays), *refs),
         grid_spec=pltpu.PrefetchScalarGridSpec(
-            num_scalar_prefetch=2,
+            num_scalar_prefetch=3,
             grid=(count,),
-            in_specs=[entry(low, high) for low, high, _ in groups] + [column] * 3,
+            in_specs=[block(number) for number in range(len(arrays))] + [column] * 3,
             out_specs=[column] * 3 + [pl.BlockSpec((1, 2, D), lambda n, *_: (n, 0, 0))],
             scratch_shapes=[pltpu.VMEM((rows, D), F32)],
         ),
@@ -777,11 +800,9 @@
         compiler_params=pltpu.CompilerParams(
             dimension_semantics=("arbitrary",), vmem_limit_bytes=VMEM_LIMIT
         ),
-        cost_estimate=pl.CostEstimate(
-            flops=20 * master.size, bytes_accessed=24 * master.size, transcendentals=0
-        ),
+        cost_estimate=SHORT,
         name="moments",
-    )(order, scale, *[grads for _, _, grads in groups], first_old, second_old, master)
+    )(source, entry, scale, *arrays, first_old, second_old, master)
 
 
 def row_moments_kernel(scale, grad, first_old, second_old, master, first, second, update, squares):
@@ -825,9 +846,7 @@
         compiler_params=pltpu.CompilerParams(
             dimension_semantics=("arbitrary",), vmem_limit_bytes=VMEM_LIMIT
         ),
-        cost_estimate=pl.CostEstimate(
-            flops=20 * master.size, bytes_accessed=24 * master.size, transcendentals=0
-        ),
+        cost_estimate=SHORT,
         name="row_moments",
     )(scale, grads, first_old, second_old, master)
 
@@ -853,9 +872,6 @@
     ]
     params = pltpu.CompilerParams(
         dimension_semantics=("arbitrary",), vmem_limit_bytes=VMEM_LIMIT
-    )
-    cost = pl.CostEstimate(
-        flops=4 * master.size, bytes_accessed=12 * master.size, transcendentals=0
     )
     if trust.ndim == 1:
         block = pl.BlockSpec((rows, D), lambda n, *_: (0, n))
@@ -869,7 +885,7 @@
             ),
             out_shape=outs,
             compiler_params=params,
-            cost_estimate=cost,
+            cost_estimate=SHORT,
             name="apply_pieces",
         )(trust, master, update)
     block = pl.BlockSpec((step, width), lambda n: (n, 0))
@@ -880,7 +896,7 @@
         out_specs=[block, block],
         out_shape=outs,
         compiler_params=params,
-        cost_estimate=cost,
+        cost_estimate=SHORT,
         name="apply_update",
     )(trust, master, update)
 
@@ -938,63 +954,61 @@
     return (kept.astype(F32) + received.astype(F32)).astype(BF16)
 
 
-def scatter_whole(pieces):
-    whole = jnp.swapaxes(pieces, 1, 2).reshape(pieces.shape[0], D, D)
+def scatter_whole(keep, send):
+    whole = jnp.stack([keep, send], axis=2).reshape(keep.shape[0], D, D)
     return lax.psum_scatter(whole, "fsdp", scatter_dimension=1, tiled=True)
 
 
 class Scatter:
     def __init__(self, pieces):
-        self.pieces = pieces
+        self.pieces, self.sent = pieces
         self.explicit = few("fsdp")
 
     def along_y(self, after=()):
-        if not self.explicit:
-            return self.pieces
-        self.half = swap(gate(self.pieces[:, 1], after), "fsdp", 1)
-        return self.half
+        self.sent = gate(self.sent, after)
+        if self.explicit:
+            self.sent = swap(self.sent, "fsdp", 1)
 
     def along_z(self, after=()):
         if not self.explicit:
             return self.pieces
-        self.half = plus(self.pieces[:, 0], self.half)
-        self.quarter = swap(gate(self.half[:, 2:], after), "fsdp", 4)
-        return self.quarter
-
-    def end(self, after=()):
+        half = plus(gate(self.pieces, after), self.sent)
+        self.half, self.sent = half, swap(half[:, 2:], "fsdp", 4)
+        return half
+
+    def end_z(self, after=()):
         if not self.explicit:
-            self.rows = scatter_whole(self.pieces)
-            return self.rows
-        quarter = plus(self.half[:, :2], self.quarter)
-        self.rows = plus(quarter[:, 0], swap(gate(quarter[:, 1], after), "fsdp", 2))
-        return self.rows
-
-
-def share(total):
-    total = plus(total, swap(total[::-1], "frame", 2))
-    return total, swap(total, "frame", 1)
-
-
-def exchange_parts(parts):
-    sent = swap(jnp.stack([parts[1], parts[3]]), "frame", 1)
-    crossed = swap(jnp.stack([parts[2], sent[1]]), "frame", 2)
+            return self.pieces
+        quarter = plus(gate(self.half[:, :2], after), self.sent)
+        self.half, self.sent = quarter, swap(quarter[:, 1], "fsdp", 2)
+        return quarter
+
+    def rows(self, after=()):
+        if not self.explicit:
+            return scatter_whole(self.pieces, self.sent)
+        return plus(gate(self.half[:, 0], after), self.sent)
+
+
+def exchange_parts(parts, between=(), after=()):
+    sent = gate(swap(jnp.stack([parts[1], parts[3]]), "frame", 1), between)
+    crossed = gate(swap(jnp.stack([parts[2], sent[1]]), "frame", 2), after)
     return [parts[0], sent[0], crossed[0], crossed[1]]
 
 
-def to_tokens(values):
+def to_tokens(values, between=()):
     j, size = lax.axis_index("frame"), lax.axis_size("frame")
     videos, frames, tokens, width = values.shape
     part = tokens // (size * frames)
     halves = tokens // (size * part)
     cut = values.reshape(videos, frames, size, halves, part, width)
     parts = exchange_parts(
-        [lax.dynamic_index_in_dim(cut, j ^ k, 2, False) for k in range(size)]
+        [lax.dynamic_index_in_dim(cut, j ^ k, 2, False) for k in range(size)], between
     )
     received = [jnp.swapaxes(one, 1, 2) for one in parts]
     return jnp.stack(received, axis=2).reshape(videos, halves * tokens, width)
 
 
-def from_tokens(values, frames):
+def from_tokens(values, frames, between=(), after=()):
     j, size = lax.axis_index("frame"), lax.axis_size("frame")
     videos, rows, width = values.shape
     tokens_part = rows // (size * frames)
@@ -1003,7 +1017,9 @@
     halves = tokens_part // part
     cut = values.reshape(videos, halves, size, frames, part, width)
     whole = jnp.zeros((videos, frames, size, halves, part, width), values.dtype)
-    for k, block in enumerate(exchange_parts([cut[:, :, k] for k in range(size)])):
+    for k, block in enumerate(
+        exchange_parts([cut[:, :, k] for k in range(size)], between, after)
+    ):
         block = jnp.swapaxes(block, 1, 2)[:, :, None]
         whole = lax.dynamic_update_slice_in_dim(whole, block, j ^ k, axis=2)
     return whole.reshape(videos, frames, tokens, width)
@@ -1052,7 +1068,8 @@
 
     shared_parts = split_columns(w_shared, shared_widths())
     if explicit:
-        shared_parts = gate(shared_parts, [first])
+        shared_parts = gate(shared_parts, [first_near])
+        text_states = gate(text_states, [first_near])
     patch_own, time_one, caption_w, time_two, mod_w, final_own = shared_parts
     time_one, time_two, mod_w = [one.astype(BF16) for one in (time_one, time_two, mod_w)]
     pair_w = w_spatial[:, 5 * D : 7 * D].astype(BF16)
@@ -1141,21 +1158,22 @@
 
         done = [first_near]
         la = with_far(first_near, done)
-        rest_near = jnp.stack([rest, swap(gate(rest, done), "fsdp", 2)], axis=1)
-        done = [la, rest_near, text_all]
-        lbc = with_far(rest_near[0:2], done)
+        near_bc = jnp.stack([rest[:2], swap(gate(rest[:2], done), "fsdp", 2)], axis=1)
+        done = [la, near_bc]
+        lbc = with_far(near_bc, done)
+        near = jnp.stack([rest[2:], swap(gate(rest[2:], done), "fsdp", 2)], axis=1)
         ya, xla = y(la, done), x(la, done)
-        done = [lbc, ya, xla, caption_pre]
-        lde = with_far(rest_near[2:4], done)
+        done = [lbc, ya, xla, near, text_all]
+        lde = with_far(near[0:2], done)
         ybc, x1 = y(lbc, done), x(joined(ya, lbc[1:]), done)
         k1 = core(joined(la, xla), done)
-        done = [lde, ybc, x1, k1, pair, modulation]
-        lf = with_far(rest_near[4:6], done)
-        yde, x2 = y(lde, done), x(joined(ybc[1:], lde), done)
+        done = [lde, ybc, x1, k1, caption_pre, target]
+        lf = with_far(near[2:4], done)
+        yde, x2 = y(lde, done), x(joined(ybc[1:], lde[:1]), done)
         k2 = core(joined(ya, x1[:1], lbc, ybc), done)
-        done = [lf, yde, x2, k2]
-        lg = with_far(rest_near[6:8], done)
-        yf, xyde = y(lf, done), x(yde, done)
+        done = [lf, yde, x2, k2, pair, modulation]
+        lg = with_far(near[4:6], done)
+        yf, x3 = y(lf, done), x(joined(lde[1:], yde[:1]), done)
         k3 = core(joined(x1[1:], lde, x2, yde), done)
         spatial_attn = [
             ((la, 0), (ya, 0)),
@@ -1190,9 +1208,10 @@
         place, six_spatial, start, spatial_allowed, pair, spatial_attn + cross_attn
     )
     if explicit:
-        done = [lg, yf, xyde, k3, middle1, fence(middle1)]
+        done = [lg, yf, x3, k3, middle1, fence(middle1)]
+        k4 = core(x3, done)
+        x4 = x(yde[1:], done)
         yg = y(lg, done)
-        k4 = core(xyde, done)
         k5 = core(joined(lf, yf), [k4])
         spatial_up = [
             ((lbc, 1), (ybc, 1)),
@@ -1200,21 +1219,20 @@
             ((x1, 1), (x2, 0)),
             ((k3, 0), (k3, 3)),
         ]
-        spatial_down, temporal_attn = [
-            [
-                ((lde, n), (yde, n)),
-                ((k3, 1 + n), (k3, 6 + n)),
-                ((x2, 1 + n), (xyde, n)),
-                ((k3, 4 + n), (k4, n)),
-            ]
-            for n in range(2)
+        spatial_down = [
+            ((lde, 0), (yde, 0)),
+            ((k3, 1), (k3, 5)),
+            ((x2, 1), (x3, 1)),
+            ((k3, 4), (k4, 1)),
         ]
         middle1 = gate(middle1, done)
     hidden1, normed1, ups1, active1, lowered1 = mlp_forward(
         place, six_spatial, middle1, spatial_up, spatial_down
     )
 
-    hidden = to_tokens(hidden1.reshape(videos, frames, tokens, D))
+    hidden = to_tokens(
+        hidden1.reshape(videos, frames, tokens, D), [x4] if explicit else []
+    )
     rows = hidden.shape[1]
     part = tokens // frames_all
     clip_ends = jnp.cumsum(frame_counts.reshape(videos, -1), axis=-1)
@@ -1232,8 +1250,15 @@
         + jnp.arange(rows, dtype=jnp.int32) % part
     )
     if explicit:
-        done = [yg, k5, hidden]
-        k6 = core(joined(lg, yg), done)
+        k7 = core(x4, [])
+        temporal_attn = [
+            ((lde, 1), (yde, 1)),
+            ((k3, 2), (k3, 6)),
+            ((x3, 0), (x4, 0)),
+            ((k4, 0), (k7, 0)),
+        ]
+        done = [k5, hidden, k7]
+        k6 = core(joined(lg, yg), [hidden, yg])
         temporal_up, temporal_down = [
             [((l, 0), (b, 0)), ((k, 0), (k, 2)), ((l, 1), (b, 1)), ((k, 1), (k, 3))]
             for l, b, k in ((lf, yf, k5), (lg, yg, k6))
@@ -1267,7 +1292,13 @@
     def pieces_of(lefts, rights, which, after=(), added=()):
         return outer_pieces(place, gate(lefts, after), rights, which, added)
 
-    other1 = pieces_of(low2, active2, [slots[3], slots[1]])
+    def own_pieces_of(lefts, rights, which, after, added):
+        return outer_pieces(place, gate(lefts, after), rights, which, (added,), True)
+
+    others, mine = [slots[1], slots[3]], [slots[0], slots[2]]
+    which = [((j ^ k) // 3, j ^ k) for k in range(4)]
+
+    other1 = pieces_of(low2, active2, others)
     core1 = swap(other1, "frame", 1)
     grad_middle2, grad_ups2, six_mlp2 = mlp_backward(
         place,
@@ -1279,10 +1310,10 @@
         temporal_up,
         temporal_down,
     )
-    done = [core1, grad_middle2, fence(grad_middle2)]
-    second1 = pieces_of(low2, active2, [slots[2]], done, (core1[:1],))
-    x1 = swap(second1, "frame", 2)
-    other2 = pieces_of(normed2, grad_ups2, [slots[1], slots[3]], [second1])
+    sum1 = Scatter(own_pieces_of(low2, active2, mine, [grad_middle2], core1))
+    other2 = pieces_of(normed2, grad_ups2, others, [sum1.pieces])
+    done = [other2]
+    sum1.along_y(done)
     core2 = swap(other2, "frame", 1)
     grad_hidden, rights2, six_attn2 = attention_backward(
         place,
@@ -1291,57 +1322,50 @@
         temporal_allowed,
         packed2,
         projected2,
-        gate(grad_middle2, [other2]),
+        gate(grad_middle2, done),
         temporal_attn,
     )
-    done = [core2, grad_hidden, fence(grad_hidden)]
-    sum2 = Scatter(pieces_of(normed2, grad_ups2, [slots[0], slots[2]], done, (core2,)))
-    y2 = sum2.along_y()
-    grad_hidden1 = from_tokens(gate(grad_hidden, [sum2.pieces]), frames)
+    sum2 = Scatter(own_pieces_of(normed2, grad_ups2, mine, [grad_hidden], core2))
+    other3 = pieces_of(lefts2, rights2, [which[1], which[3]], [sum2.pieces])
+    done = [sum1.sent, other3]
+    sum2.along_y(done)
+    half1 = sum1.along_z(done)
+    core3 = swap(gate(other3, done), "frame", 1)
+    grad_hidden1 = from_tokens(gate(grad_hidden, done), frames, [half1])
     grad_hidden1 = grad_hidden1.reshape(videos, frames * tokens, D)
-    which2 = [((j ^ k) // 3, j ^ k) for k in range(4)]
-    other3 = pieces_of(lefts2, rights2, [which2[3], which2[1]], [sum2.pieces])
-    core3 = swap(other3, "frame", 1)
-    sum1 = Scatter(pieces_of(low2, active2, [slots[0]], [other3], (core1[1:], x1)))
-    y1 = sum1.along_y()
-    second3 = pieces_of(lefts2, rights2, [which2[2]], [sum1.pieces], (core3[:1],))
-    done = [grad_hidden1, sum1.pieces, second3, y2]
-    x3 = swap(gate(second3, done), "frame", 2)
-    low1 = (gate(grad_hidden1, done) * six_spatial[:, 5][:, None, :]).astype(BF16)
-    other4 = pieces_of(low1, active1, [slots[3], slots[1]])
-    core4 = swap(other4, "frame", 1)
-    z2 = sum2.along_z(done)
+    sum3 = Scatter(own_pieces_of(lefts2, rights2, [which[0], which[2]], [half1], core3))
+    low1 = gate(grad_hidden1, [sum3.pieces]) * six_spatial[:, 5][:, None, :]
+    low1 = low1.astype(BF16)
+    other4 = pieces_of(low1, active1, others)
+    done = [sum2.sent, sum1.sent, other4]
+    sum3.along_y(done)
+    half2, quarter1 = sum2.along_z(done), sum1.end_z(done)
+    core4 = swap(gate(other4, done), "frame", 1)
     grad_middle1, grad_ups1, six_mlp1 = mlp_backward(
         place,
         six_spatial,
         middle1,
         ups1,
         lowered1,
-        gate(grad_hidden1, [other4]),
+        gate(grad_hidden1, [half2, quarter1]),
         spatial_up,
         spatial_down,
     )
-    done = [core4, grad_middle1, fence(grad_middle1), y1]
-    second4 = pieces_of(low1, active1, [slots[2]], done, (core4[:1],))
-    x4 = swap(second4, "frame", 2)
-    z1 = sum1.along_z(done)
-    other5 = pieces_of(normed1, grad_ups1, [slots[1], slots[3]], [second4])
-    core5 = swap(other5, "frame", 1)
+    sum4 = Scatter(own_pieces_of(low1, active1, mine, [grad_middle1], core4))
+    other5 = pieces_of(normed1, grad_ups1, others, [sum4.pieces])
+    done = [sum3.sent, sum2.sent, sum1.sent, other5]
+    sum4.along_y(done)
+    half3, quarter2, rows1 = sum3.along_z(done), sum2.end_z(done), sum1.rows(done)
+    core5 = swap(gate(other5, done), "frame", 1)
     grad_after1, rights7, grad_pair = cross_backward(
-        place, gate(grad_middle1, [other5]), pair, cross_query, cross_attn
-    )
-    sum3 = Scatter(pieces_of(lefts2, rights2, [which2[0]], [grad_after1], (core3[1:], x3)))
-    y3 = sum3.along_y()
-    rows2 = sum2.end([sum3.pieces])
-    done = [core5, sum3.pieces, z1, z2]
-    sum5 = Scatter(pieces_of(normed1, grad_ups1, [slots[0], slots[2]], done, (core5,)))
-    y5 = sum5.along_y()
+        place, gate(grad_middle1, [half3, quarter2]), pair, cross_query, cross_attn
+    )
+    sum5 = Scatter(own_pieces_of(normed1, grad_ups1, mine, [grad_after1], core5))
     other7 = pieces_of(lefts1, rights7, [(3 - c, 1 - c)], [sum5.pieces])
-    core7 = swap(other7, "frame", 1)
-    grad_pair = grad_pair.astype(BF16).reshape(videos * texts, n_frame, pair_part)
-    grad_pair = to_relative(jnp.swapaxes(grad_pair, 0, 1), "frame")
-    grad_pair = deliver(grad_pair, "frame").astype(BF16)
-    rows1 = sum1.end([other7])
+    done = [sum4.sent, sum3.sent, sum2.sent, other7]
+    sum5.along_y(done)
+    half4, quarter3, rows2 = sum4.along_z(done), sum3.end_z(done), sum2.rows(done)
+    core7 = swap(gate(other7, done), "frame", 1)
     grad_start, rights1, six_attn1 = attention_backward(
         place,
         six_spatial,
@@ -1349,19 +1373,25 @@
         spatial_allowed,
         packed1,
         projected1,
-        gate(grad_after1, [other7]),
+        gate(grad_after1, [half4, quarter3]),
         spatial_attn,
     )
-    sum4 = Scatter(pieces_of(low1, active1, [slots[0]], [grad_start], (core4[1:], x4)))
-    done = [grad_start, core7, y3, sum4.pieces, grad_pair, rows1, rows2]
-
-    along_pair = collect_along(gate(grad_pair, done))
+    other6 = pieces_of(lefts1, rights1, [which[1], which[3]], [grad_start])
+    sum7 = Scatter(own_pieces_of(lefts1, rights7, [(2 + c, c)], [other6], core7))
+    done = [sum5.sent, sum4.sent, sum3.sent, sum7.pieces]
+    sum7.along_y(done)
+    half5, quarter4, rows3 = sum5.along_z(done), sum4.end_z(done), sum3.rows(done)
+    core6 = swap(gate(other6, done), "frame", 1)
+
+    grad_pair = gate(grad_pair, [half5, quarter4]).astype(BF16)
+    grad_pair = grad_pair.reshape(videos * texts, n_frame, pair_part)
+    grad_pair = to_relative(jnp.swapaxes(grad_pair, 0, 1), "frame")
     six_s, six_t = [
         jnp.concatenate([attn[:, 0:3], mlp[:, 3:6]], axis=1)
-        for attn, mlp in ((gate(six_attn1, done), six_mlp1), (six_attn2, six_mlp2))
+        for attn, mlp in ((gate(six_attn1, [half5, quarter4]), six_mlp1), (six_attn2, six_mlp2))
     ]
     grad_final = jnp.stack([grad_shift_final, grad_scale_final], axis=1)
-    grad_patch_w = outer(noisy, grad_start.astype(BF16))
+    grad_patch_w = outer(noisy, gate(grad_start, [half5, quarter4]).astype(BF16))
     cond = jnp.concatenate(
         [
             grad_patch_w,
@@ -1370,42 +1400,49 @@
             jnp.concatenate([six_s + six_t, grad_final], axis=1).reshape(-1, D),
         ]
     )
-    cond = sum_over(cond, "frame")
-
-    y4, z3 = sum4.along_y([along_pair]), sum3.along_z([along_pair])
-    which1 = [((j ^ k) // 3, j ^ k) for k in range(4)]
-    other6 = pieces_of(lefts1, rights1, [which1[1], which1[3]], done)
-    core6 = swap(other6, "frame", 1)
-    sum7 = Scatter(pieces_of(lefts1, rights7, [(2 + c, c)], [other6], (core7,)))
-    y7 = sum7.along_y()
-    pair6 = pieces_of(lefts1, rights1, [which1[0], which1[2]], [sum7.pieces], (core6,))
-    sum6, sum8 = Scatter(pair6[:1]), Scatter(pair6[1:])
-    done = [pair6, y4, z3, y5, along_pair, cond]
-    grad_pair = collect_beside(gate(along_pair, done)).reshape(-1, pair_part)
+    pair_core = swap(jnp.stack([grad_pair[1], grad_pair[3]]), "frame", 1)
+    cond_core = swap(cond, "frame", 1)
+    sum6 = Scatter(
+        own_pieces_of(lefts1, rights1, [which[0], which[2]], [half5, quarter4], core6)
+    )
+    done = [sum6.pieces, sum7.sent, sum4.sent, pair_core, cond_core]
+    sum6.along_y(done)
+    half7, rows4 = sum7.along_z(done), sum4.rows(done)
+    pair_core, cond_core = gate((pair_core, cond_core), done)
+    pair_x = swap(plus(grad_pair[2], pair_core[1]), "frame", 2)
+    cond = cond + cond_core
+    cond_x = swap(cond, "frame", 2)
+    done = [pair_x, cond_x, half7]
+    pair_x, cond_x = gate((pair_x, cond_x), done)
+    grad_pair = plus(plus(grad_pair[0], pair_core[0]), pair_x)
+    cond = cond + cond_x
     small_grad = jnp.swapaxes(cond[: 2 * PCH + 14].reshape(-1, n_fsdp, rows_own), 0, 1)
-    small_grad = deliver_beside(gate(to_relative(small_grad, "fsdp"), done))
-    along_cond = collect_along(
-        gate(cond[2 * PCH + 14 :].astype(BF16).reshape(videos, 8, D), done)
-    )
-    first_sent = [grad_pair, small_grad, along_cond]
-    y6 = sum6.along_y(first_sent)
-    y8 = sum8.along_y([y7] + first_sent)
-    z4, z5 = sum4.along_z(first_sent), sum5.along_z(first_sent)
-    rows3 = sum3.end(done)
-    done = [y7, z4, z5, rows3] + first_sent
-    pair_w_grad = outer(caption, gate(grad_pair, done))
+    small_grad = Deliver(to_relative(small_grad, "fsdp"))
+    cond_rows = 8 * videos
+    sent = Collect(
+        jnp.concatenate([cond[2 * PCH + 14 :].astype(BF16), grad_pair.reshape(-1, D)])
+    )
+    early = jnp.concatenate([rows1, rows2, rows3])
+    crossed = swap(
+        gate(jnp.concatenate([rows1[::-1], rows2[::-1], rows3[::-1]]), [cond]), "frame", 2
+    )
+    small_sent = sent.sent + small_grad.sent if explicit else [cond]
+    done = small_sent + [sum6.sent, sum5.sent, crossed]
+    half6 = sum6.along_z(done)
+    sent.beside([half6])
+    small_grad.beside([half6])
+    quarter5 = sum5.end_z([half6])
+    early = plus(early, gate(crossed, [half6]))
+    early_other = swap(early, "frame", 1)
+    received = sent.all([quarter5, early])
+    small_grad = small_grad.total([quarter5, early]).T
+    quarter7, rows5 = sum7.end_z([received]), sum5.rows([received])
+    late = jnp.concatenate([rows4, rows5])
+    grad_pair = received[:, cond_rows:].reshape(-1, pair_part)
+    pair_w_grad = outer(caption, grad_pair)
     grad_caption = sum_over_frame_low(dot_t(grad_pair, pair_w_part))
-    small_grad = deliver_along(gate(small_grad, done)).T
-    cond = collect_beside(gate(along_cond, done)).reshape(n_fsdp * videos, 8, D)
-    first_sent = [cond, small_grad]
-    z7 = sum7.along_z(first_sent)
-    z6 = sum6.along_z([y6] + first_sent)
-    rows4, rows5 = sum4.end(done), sum5.end(done)
-    done = [y8, z7, rows4, rows5, grad_caption] + first_sent
-    grad_caption = jax.vjp(gelu_tanh, caption_pre)[1](gate(grad_caption, done))[0].astype(BF16)
-    both = jnp.concatenate([outer(grad_caption, text_all), pair_w_grad], axis=1).astype(BF16)
-    both = collect(both, "frame")
-    grad_mod = gate(cond, done)[:, :6].reshape(-1, 6 * D)
+    cond = received[:, :cond_rows].reshape(n_fsdp * videos, 8, D)
+    grad_mod = cond[:, :6].reshape(-1, 6 * D)
     mod_grad = outer(embed_act, grad_mod)
     final_part = lax.dynamic_slice(
         cond[:, 6].astype(F32) + cond[:, 7].astype(F32), (0, i * rows_own), embedding_part.shape
@@ -1413,33 +1450,27 @@
     grad_embed = (
         jax.vjp(jax.nn.silu, embedding_part)[1](dot_t(grad_mod, mod_w))[0] + final_part
     ).astype(BF16)
-    along_embed = collect_along(grad_embed.reshape(n_fsdp, videos, rows_own))
-    z8 = sum8.along_z([along_embed, y8])
-    rows7 = sum7.end([along_embed])
-    quads = jnp.stack([rows1, rows3, rows4], axis=1)
-    slots_two = jnp.stack([rows2, rows5], axis=1)
-    crossed = swap(jnp.concatenate([slots_two[1], slots_two[0], quads[0]]), "frame", 2)
-    totals = jnp.concatenate([plus(slots_two.reshape(4, rows_own, D), crossed[:4]), quads[0], crossed[4:]])
-    done = [z6, z8, rows7, along_embed, totals, both]
-    received = collect_beside(gate(along_embed, done))
-    rows6, rows8 = sum6.end([received]), sum8.end([received])
-    totals_other = swap(gate(totals, done), "frame", 1)
-    crossed7 = swap(gate(rows7, done), "frame", 2)
-    done = [rows6, rows8, totals_other, crossed7, received]
-    last = jnp.concatenate([rows6, rows8])
-    crossed = swap(gate(last[::-1], done), "frame", 2)
-    last = jnp.concatenate([plus(last, crossed), plus(rows7, crossed7)])
+    grad_embed = Collect(grad_embed.reshape(n_fsdp, videos, rows_own))
+    late_x = swap(
+        gate(jnp.concatenate([rows4[::-1], rows5[::-1]]), [grad_caption]), "frame", 2
+    )
+    quarter6 = sum6.end_z([grad_caption, quarter7])
+    grad_caption = gate(grad_caption, [quarter6])
+    grad_caption = jax.vjp(gelu_tanh, caption_pre)[1](grad_caption)[0].astype(BF16)
+    both = jnp.concatenate([outer(grad_caption, text_all), pair_w_grad], axis=1).astype(BF16)
+    late = plus(late, gate(late_x, [both]))
+    late_other = swap(late, "frame", 1)
+    both = jnp.stack([both, swap(both, "frame", 1)])
+    rows7 = sum7.rows([quarter6])
+    rows6 = sum6.rows([both])
+    last = plus(
+        jnp.concatenate([rows6, rows7]),
+        swap(jnp.concatenate([rows6[::-1], rows7]), "frame", 2),
+    )
+    both = jnp.concatenate([both, swap(gate(both, [rows6]), "frame", 2)])
+    grad_embed.beside([quarter6])
+    received = grad_embed.all([rows6])
     last_other = swap(last, "frame", 1)
-
-    def in_order(total, other):
-        return jnp.stack([total, other], axis=1).reshape((-1,) + total.shape[1:])
-
-    up_grads2, up_grads1, down_grads2, attn_grads2, down_grads1 = [
-        in_order(jnp.stack([totals[m], totals[n]]), jnp.stack([totals_other[m], totals_other[n]]))
-        for m, n in ((0, 2), (1, 3), (4, 7), (5, 8), (6, 9))
-    ]
-    attn_grads1 = in_order(last[:2], last_other[:2])
-    cross_grads = jnp.concatenate([last[2:], last_other[2:]])
     both = to_relative(both, "frame")
     caption_grad, pair_w_grad = [
         jnp.swapaxes(one, 0, 1).reshape(rows_own, -1)
@@ -1466,37 +1497,31 @@
 
     pair_pieces = jnp.stack([pair_w_grad[:, :D], pair_w_grad[:, D:]])
     tables_grad = small_grad[:, 2 * PCH :]
-    relative = jnp.arange(4, dtype=jnp.int32) ^ j
-    spatial_order = jnp.concatenate(
-        [
-            relative,
-            jnp.stack([c, 0 * c, 1 + 0 * c, 1 - c]).astype(jnp.int32),
-            relative,
-            relative,
-        ]
-    )
-    temporal_order = jnp.concatenate([relative, relative, relative])
-    spatial_groups = [
-        (0, 3, attn_grads1),
-        (4, 4, cross_grads),
-        (5, 6, pair_pieces),
-        (7, 7, cross_grads),
-        (8, 11, up_grads1),
-        (12, 15, down_grads1),
-    ]
-    temporal_groups = [(0, 3, attn_grads2), (4, 7, up_grads2), (8, 11, down_grads2)]
+    relative = np.arange(4) ^ j
+    odd, half = relative % 2, relative // 2
+    core_first = jnp.stack([c, 1 - c])
+    temporal_arrays = [early, early_other]
+    temporal_source = jnp.concatenate([odd, odd, odd]).astype(jnp.int32)
+    temporal_entry = jnp.concatenate([4 + half, 2 + half, half]).astype(jnp.int32)
+    spatial_arrays = [last, last_other, late, late_other, pair_pieces]
+    fours = jnp.array([4, 4], jnp.int32)
+    spatial_source = jnp.concatenate(
+        [odd, core_first[:1], fours, core_first[1:], 2 + odd, 2 + odd]
+    ).astype(jnp.int32)
+    spatial_entry = jnp.concatenate(
+        [half, fours[:1] // 2, fours // 4 - np.array([1, 0]), fours[:1] // 2, 2 + half, half]
+    ).astype(jnp.int32)
 
     def squares(values, axes=None):
         values = values.astype(F32)
         return jnp.sum(values * values, axis=axes)
 
-    def group_squares(groups, order):
-        return jnp.concatenate(
-            [
-                squares(grads, (1, 2))[order[low : high + 1]]
-                for low, high, grads in groups
-            ]
+    def piece_squares(arrays, source, entry):
+        most = max(one.shape[0] for one in arrays)
+        table = jnp.concatenate(
+            [jnp.pad(squares(one, (1, 2)), (0, most - one.shape[0])) for one in arrays]
         )
+        return table[source * most + entry]
 
     def rows_of(widths, first):
         which = np.repeat(np.arange(len(widths)) + first, widths)
@@ -1521,8 +1546,8 @@
 
     grad_part_sq = matrix_sums(
         squares(shared_grads, 0),
-        group_squares(spatial_groups, spatial_order),
-        group_squares(temporal_groups, temporal_order),
+        piece_squares(spatial_arrays, spatial_source, spatial_entry),
+        piece_squares(temporal_arrays, temporal_source, temporal_entry),
         squares(tables_grad),
     )
     loss_all = sum_over(loss_part[None], "frame")
@@ -1533,9 +1558,11 @@
     grad_scale = factor / weight_total
     scale = grad_scale[None]
     shared_new = row_moments(scale, shared_grads, m_shared, v_shared, w_shared)
-    spatial_new = moments(spatial_groups, spatial_order, scale, m_spatial, v_spatial, w_spatial)
+    spatial_new = moments(
+        spatial_arrays, spatial_source, spatial_entry, scale, m_spatial, v_spatial, w_spatial
+    )
     temporal_new = moments(
-        temporal_groups, temporal_order, scale, m_temporal, v_temporal, w_temporal
+        temporal_arrays, temporal_source, temporal_entry, scale, m_temporal, v_temporal, w_temporal
     )
     tables_new = optimizer_step(tables_grad * grad_scale, m_tables, v_tables, shift_tables)
     spatial_sq = jnp.sum(spatial_new[3], axis=2)

time: 1670 us -> 1450 us (0.87)
  waiting for transfers between devices: 651 us -> 463 us
  local copies, waits for them, and re-layouts: 179 us -> 140 us
  other arithmetic: 150 us -> 172 us
  starting transfers between devices: 123 us -> 106 us
    ppermute x121 -> x114, waiting for transfers between devices: 651 us -> 463 us  [swap(): lax.ppermute(values, axis, [(n, n ^ mask) for n in range(lax.axis_size(ax...]
    slice x23 -> x18, local copies, waits for them, and re-layouts: 47 us -> 24 us  [the longest x7 13.3 us: end_z(): quarter = plus(gate(self.half[:, :2], after), self.sent)]
    ppermute x121 -> x114, starting transfers between devices: 123 us -> 106 us  [swap(): lax.ppermute(values, axis, [(n, n ^ mask) for n in range(lax.axis_size(ax...]
    optimization_barrier x2 -> x8, local copies, waits for them, and re-layouts: 0.14 us -> 17 us  [gate(): return lax.optimization_barrier((values, after))[0]]
    convert_element_type x26 -> x23, other arithmetic: 28.5 us -> 38.4 us  [plus(): return (kept.astype(F32) + received.astype(F32)).astype(BF16)]
    pallas_call x19 -> x16, Pallas kernels: 173 us -> 167 us  [the longest x14 119 us: outer_pieces(): pl.pallas_call(lambda *refs: outer_kernel(len(added), split, *refs), grid...]
  transfers between devices with their start and end apart: 121 -> 114, of which waited for: 45 -> 50; matrix products, arithmetic and copies ran while one was open for 17% -> 20% of each run, Pallas kernels for 20% -> 24%
where the time goes in v2:
time: 1450 us; the launch traced here: 1430 us
  Pallas kernels  520 us (36%)
  waiting for transfers between devices  463 us (32%)
  other arithmetic  172 us (12%)
  local copies, waits for them, and re-layouts  140 us (10%)
  starting transfers between devices  106 us (7%)
  matrix products  20.3 us (1%)
    ppermute x114, waiting for transfers between devices, swap(): lax.ppermute(values, axis, [(n, n ^ mask) for n in range(lax.axis_size(ax...  463 us
    pallas_call x9, Pallas kernels, block_call(): pl.pallas_call(kernel, grid=(values[0].shape[0],), out_shape=outs, in_spe...  282 us
    pallas_call x14, Pallas kernels, outer_pieces(): pl.pallas_call(lambda *refs: outer_kernel(len(added), split, *refs), grid...  119 us
    ppermute x114, starting transfers between devices, swap(): lax.ppermute(values, axis, [(n, n ^ mask) for n in range(lax.axis_size(ax...  106 us
    pallas_call x2, Pallas kernels, moments(): pl.pallas_call(lambda *refs: moments_kernel(len(arrays), *refs), grid_spe...  48.6 us
    convert_element_type x23, other arithmetic, plus(): return (kept.astype(F32) + received.astype(F32)).astype(BF16)  38.4 us
    pallas_call x2, Pallas kernels, apply_update(): pl.pallas_call(apply_pieces_kernel, grid_spec=pltpu.PrefetchScalarGridSpe...  30.9 us
    concatenate x8, other arithmetic, joined(): return jnp.concatenate(arrays)  29.2 us
  transfers between devices with their start and end apart: 114, of which 50 were waited for; matrix products, arithmetic and copies ran while one was open for 20% of the time, Pallas kernels for 24%

profile of v2, /device:TPU:0, one launch (start us, length us, event | category | flops | bytes accessed | tf_op | source)
XLA Modules:
  0.0 1430.4 jit_solution(1710442598332833750)
XLA Ops:
  69.8 14.9 %collective-permute-done.17 = bf16[1,128,1024]{2,1,0:T(8,128)(2,1)S(1)} collective-permute-done((bf16[1,128,1024]{2,1,0:T(8,128)(2,1)}, bf16[1,128,1024]{2,1,0:T(8,128)(2,1)S(1)}, u32[]{:S(2)}, u32[]{:S(2)}) %collective-permute-start.17) | collective-permute-done | bytes 262176 | tf_op jit(solution)/shard_map/ppermute | solution.py:38
  104.1 15.9 %collective-permute-done.18 = bf16[2,128,1024]{2,1,0:T(8,128)(2,1)} collective-permute-done((bf16[2,128,1024]{2,1,0:T(8,128)(2,1)}, bf16[2,128,1024]{2,1,0:T(8,128)(2,1)}, u32[]{:S(2)}, u32[]{:S(2)}) %collective-permute-start.18) | collective-permute-done | bytes 524320 | tf_op jit(solution)/shard_map/ppermute | solution.py:38
  127.3 23.5 %collective-permute-done.7 = f32[4,2,3456]{2,1,0:T(2,128)S(1)} collective-permute-done((f32[4,2,3456]{2,1,0:T(2,128)S(1)}, f32[4,2,3456]{2,1,0:T(2,128)S(1)}, u32[]{:S(2)}, u32[]{:S(2)}) %collective-permute-start.7) | collective-permute-done | bytes 110624 | tf_op jit(solution)/shard_map/ppermute | solution.py:38
  153.4 23.4 %collective-permute-done.14 = bf16[2,2,144,1152]{3,2,1,0:T(8,128)(2,1)} collective-permute-done((bf16[2,2,144,1152]{3,2,1,0:T(8,128)(2,1)}, bf16[2,2,144,1152]{3,2,1,0:T(8,128)(2,1)}, u32[]{:S(2)}, u32[]{:S(2)}) %collective-permute-start.14) | collective-permute-done | bytes 1327136 | tf_op jit(solution)/shard_map/ppermute | solution.py:38
  193.6 52.8 %collective-permute-done.25 = bf16[1024,144]{0,1:T(8,128)(2,1)S(1)} collective-permute-done((bf16[1024,144]{0,1:T(8,128)(2,1)S(1)}, bf16[1024,144]{0,1:T(8,128)(2,1)S(1)}, u32[]{:S(2)}, u32[]{:S(2)}) %collective-permute-start.25) | collective-permute-done | bytes 294944 | tf_op jit(solution)/shard_map/ppermute | solution.py:38
  286.5 59.7 %collective-permute-done.36 = bf16[2,128,576]{1,2,0:T(8,128)(2,1)S(1)} collective-permute-done((bf16[2,128,576]{1,2,0:T(8,128)(2,1)S(1)}, bf16[2,128,576]{1,2,0:T(8,128)(2,1)S(1)}, u32[]{:S(2)}, u32[]{:S(2)}) %collective-permute-start.36) | collective-permute-done | bytes 294944 | tf_op jit(solution)/shard_map/ppermute | solution.py:38
  374.9 46.6 %attention_forward.2 = (f32[2,256,1152]{2,1,0:T(8,128)}, bf16[2,256,3456]{2,1,0:T(8,128)(2,1)}, f32[2,256,1152]{2,1,0:T(8,128)}, bf16[2,256,4608]{2,1,0:T(8,128)(2,1)}, bf16[2,256,1152]{2,1,0:T(8,128)(2,1)}) custom-call(s32[3]{0:T(128)} %pad_add_fusion.refs_0_.refs_2_, f32[2,6,1152]{2,1,0:T(8,128)} %get-tuple-element.652.refs_1_, ...), custom_call_target="tpu_custom_call" | custom-call | flops 1000 | bytes 1000 | tf_op jit(solution)/shard_map/attention_forward/pallas_call | solution.py:420
  439.2 26.7 %mlp_forward.2 = (f32[2,256,1152]{2,1,0:T(8,128)}, bf16[2,256,1152]{2,1,0:T(8,128)(2,1)}, f32[2,256,4608]{2,1,0:T(8,128)}, bf16[2,256,4608]{2,1,0:T(8,128)(2,1)}, f32[2,256,1152]{2,1,0:T(8,128)}) custom-call(s32[3]{0:T(128)} %pad_add_fusion.refs_0_.refs_2_, f32[2,6,1152]{2,1,0:T(8,128)} %get-tuple-element.652.refs_1_, ...), custom_call_target="tpu_custom_call" | custom-call | flops 1000 | bytes 1000 | tf_op jit(solution)/shard_map/mlp_forward/pallas_call | solution.py:420
  512.7 27.1 %attention_forward.3 = (f32[2,256,1152]{2,1,0:T(8,128)}, bf16[2,256,3456]{2,1,0:T(8,128)(2,1)}, f32[2,256,1152]{2,1,0:T(8,128)}, bf16[2,256,2304]{2,1,0:T(8,128)(2,1)}) custom-call(s32[3]{0:T(128)} %pad_add_fusion.refs_0_.refs_2_, f32[2,6,1152]{2,1,0:T(8,128)} %copy-done.69, f32[2,256,1152]{2,1,0:T(8,128)} %bitcast.437, ...), custom_call_target="tpu_custom_call" | custom-call | flops 1000 | bytes 1000 | tf_op jit(solution)/shard_map/attention_forward/pallas_call | solution.py:420
  539.8 26.5 %mlp_forward.3 = (f32[2,256,1152]{2,1,0:T(8,128)}, bf16[2,256,1152]{2,1,0:T(8,128)(2,1)}, f32[2,256,4608]{2,1,0:T(8,128)}, bf16[2,256,4608]{2,1,0:T(8,128)(2,1)}, f32[2,256,1152]{2,1,0:T(8,128)}) custom-call(s32[3]{0:T(128)} %pad_add_fusion.refs_0_.refs_2_, f32[2,6,1152]{2,1,0:T(8,128)} %copy-done.69, f32[2,256,1152]{2,1,0:T(8,128)} %get-tuple-element.238.refs_2_, ...), custom_call_target="tpu_custom_call" | custom-call | flops 1000 | bytes 1000 | tf_op jit(solution)/shard_map/mlp_forward/pallas_call | solution.py:420
  584.3 29.4 %mlp_backward.2 = (f32[2,256,1152]{2,1,0:T(8,128)}, bf16[2,256,4608]{2,1,0:T(8,128)(2,1)}, f32[2,8,1152]{2,1,0:T(8,128)}) custom-call(s32[3]{0:T(128)} %pad_add_fusion.refs_0_.refs_2_, f32[2,6,1152]{2,1,0:T(8,128)} %copy-done.69, f32[2,256,1152]{2,1,0:T(8,128)} %get-tuple-element.238.refs_2_, f32[2,256,4608]{2,1,0:T(8,128)} %get-tuple-element.241.refs_3_, ...), custom_call_target="tpu_custom_call" | custom-call | flops 1000 | bytes 1000 | tf_op jit(solution)/shard_map/mlp_backward/pallas_call | solution.py:420
  635.1 34.8 %attention_backward.2 = (f32[2,256,1152]{2,1,0:T(8,128)}, bf16[2,256,4608]{2,1,0:T(8,128)(2,1)}, f32[2,8,1152]{2,1,0:T(8,128)}) custom-call(s32[3]{0:T(128)} %pad_add_fusion.refs_0_.refs_2_, f32[2,6,1152]{2,1,0:T(8,128)} %copy-done.69, f32[2,256,1152]{2,1,0:T(8,128)} %bitcast.438, f32[2,128,128]{2,1,0:T(8,128)} %and_convert_fusion.refs_3_, ...), custom_call_target="tpu_custom_call" | custom-call | flops 1000 | bytes 1000 | tf_op jit(solution)/shard_map/attention_backward/pallas_call | solution.py:420
  712.1 23.0 %collective-permute-done.54 = f32[2,2,2,2,16,1152]{5,4,2,3,1,0:T(8,128)S(1)} collective-permute-done((f32[2,2,2,2,16,1152]{5,4,2,3,1,0:T(8,128)S(1)}, f32[2,2,2,2,16,1152]{5,4,2,3,1,0:T(8,128)S(1)}, u32[]{:S(2)}, u32[]{:S(2)}) %collective-permute-start.54) | collective-permute-done | bytes 1179680 | tf_op jit(solution)/shard_map/ppermute | solution.py:38
  753.8 15.8 %collective-permute-done.56 = bf16[2,2,144,1152]{3,2,0,1:T(8,128)(2,1)} collective-permute-done((bf16[2,2,144,1152]{3,2,0,1:T(8,128)(2,1)}, bf16[2,2,144,1152]{3,2,0,1:T(8,128)(2,1)}, u32[]{:S(2)}, u32[]{:S(2)}) %collective-permute-start.56) | collective-permute-done | bytes 1327136 | tf_op jit(solution)/shard_map/ppermute | solution.py:38
  782.8 29.4 %mlp_backward.3 = (f32[2,256,1152]{2,1,0:T(8,128)}, bf16[2,256,4608]{2,1,0:T(8,128)(2,1)}, f32[2,8,1152]{2,1,0:T(8,128)}) custom-call(s32[3]{0:T(128)} %pad_add_fusion.refs_0_.refs_2_, f32[2,6,1152]{2,1,0:T(8,128)} %get-tuple-element.652.refs_1_, f32[2,256,1152]{2,1,0:T(8,128)} %get-tuple-element.227.refs_2_, f32[2,256,4608]{2,1,0:T(8,128)} %get-tuple-element.229.refs_3_, ...), custom_call_target="tpu_custom_call" | custom-call | flops 1000 | bytes 1000 | tf_op jit(solution)/shard_map/mlp_backward/pallas_call | solution.py:420
  860.6 26.3 %cross_backward.1 = (f32[2,256,1152]{2,1,0:T(8,128)}, bf16[2,256,2304]{2,1,0:T(8,128)(2,1)}, f32[2,64,2304]{2,1,0:T(8,128)}) custom-call(s32[3]{0:T(128)} %pad_add_fusion.refs_0_.refs_2_, f32[2,256,1152]{2,1,0:T(8,128)} %get-tuple-element.285.refs_1_, bf16[2,64,2304]{2,1,0:T(8,128)(2,1)} %reshape.885.refs_4_.refs_2_, ...), custom_call_target="tpu_custom_call" | custom-call | flops 1000 | bytes 1000 | tf_op jit(solution)/shard_map/cross_backward/pallas_call | solution.py:420
  930.7 35.0 %attention_backward.3 = (f32[2,256,1152]{2,1,0:T(8,128)}, bf16[2,256,4608]{2,1,0:T(8,128)(2,1)}, f32[2,8,1152]{2,1,0:T(8,128)}) custom-call(s32[3]{0:T(128)} %pad_add_fusion.refs_0_.refs_2_, f32[2,6,1152]{2,1,0:T(8,128)} %get-tuple-element.652.refs_1_, f32[2,256,1152]{2,1,0:T(8,128)} %fusion.142.refs_2_, f32[2,128,128]{2,1,0:T(8,128)} %broadcast_in_dim.280.refs_3_, ...), custom_call_target="tpu_custom_call" | custom-call | flops 1000 | bytes 1000 | tf_op jit(solution)/shard_map/attention_backward/pallas_call | solution.py:420
  1042.5 27.8 %collective-permute-done.84 = bf16[2,2,144,1152]{3,2,0,1:T(8,128)(2,1)} collective-permute-done((bf16[2,2,144,1152]{3,2,0,1:T(8,128)(2,1)}, bf16[2,2,144,1152]{3,2,0,1:T(8,128)(2,1)}, u32[]{:S(2)}, u32[]{:S(2)}) %collective-permute-start.84) | collective-permute-done | bytes 1327136 | tf_op jit(solution)/shard_map/ppermute | solution.py:38
  1086.2 19.5 %collective-permute-done.81 = bf16[80,1152]{1,0:T(8,128)(2,1)S(1)} collective-permute-done((bf16[80,1152]{1,0:T(8,128)(2,1)S(1)}, bf16[80,1152]{1,0:T(8,128)(2,1)S(1)}, u32[]{:S(2)}, u32[]{:S(2)}) %collective-permute-start.81) | collective-permute-done | bytes 184352 | tf_op jit(solution)/shard_map/ppermute | solution.py:38
  1225.9 17.3 %collective-permute-done.98 = bf16[2,144,1600]{2,1,0:T(8,128)(2,1)} collective-permute-done((bf16[2,144,1600]{2,1,0:T(8,128)(2,1)}, bf16[2,144,1600]{2,1,0:T(8,128)(2,1)}, u32[]{:S(2)}, u32[]{:S(2)}) %collective-permute-start.98) | collective-permute-done | bytes 921632 | tf_op jit(solution)/shard_map/ppermute | solution.py:38
  1293.8 20.1 %row_moments.1 = (f32[144,12448]{1,0:T(8,128)}, f32[144,12448]{1,0:T(8,128)}, bf16[144,12448]{1,0:T(8,128)(2,1)}, f32[2,12448]{1,0:T(2,128)}) custom-call(f32[1]{0:T(128)} %bitcast.211.scale.refs_2_, bf16[144,12448]{1,0:T(8,128)(2,1)} %concatenate.279.grad, f32[144,12448]{1,0:T(8,128)} %first_old.1, f32[144,12448]{1,0:T(8,128)} %second_old.1, ...), custom_call_target="tpu_custom_call" | custom-call | flops 1000 | bytes 1000 | tf_op jit(solution)/shard_map/row_moments/pallas_call | solution.py:832
  1315.2 27.6 %moments.2 = (f32[144,18432]{1,0:T(8,128)}, f32[144,18432]{1,0:T(8,128)}, bf16[144,18432]{1,0:T(8,128)(2,1)}, f32[16,2,1152]{2,1,0:T(2,128)}) custom-call(s32[16]{0:T(128)} %concatenate.301.refs_0_, s32[16]{0:T(128)} %concatenate.302.refs_1_, f32[1]{0:T(128)} %bitcast.211.scale.refs_2_, bf16[3,144,1152]{2,1,0:T(8,128)(2,1)} %get-tuple-element.549.refs_3_, ...), custom_call_target="tpu_custom_call" | custom-call | flops 1000 | bytes 1000 | tf_op jit(solution)/shard_map/moments/pallas_call | solution.py:785
  1344.1 21.0 %moments.3 = (f32[144,13824]{1,0:T(8,128)}, f32[144,13824]{1,0:T(8,128)}, bf16[144,13824]{1,0:T(8,128)(2,1)}, f32[12,2,1152]{2,1,0:T(2,128)}) custom-call(s32[12]{0:T(128)} %pad_add_fusion.5.refs_0_, s32[12]{0:T(128)} %pad_add_fusion.6.refs_1_, f32[1]{0:T(128)} %bitcast.211.scale.refs_2_, bf16[6,144,1152]{2,1,0:T(8,128)(2,1)} %copy-done.19, ...), custom_call_target="tpu_custom_call" | custom-call | flops 1000 | bytes 1000 | tf_op jit(solution)/shard_map/moments/pallas_call | solution.py:785
  1399.3 17.5 %apply_pieces.2 = (f32[144,18432]{1,0:T(8,128)}, bf16[144,18432]{1,0:T(8,128)(2,1)}) custom-call(f32[16]{0:T(128)} %select_reduce_fusion.5.trust, f32[144,18432]{1,0:T(8,128)} %master.6, bf16[144,18432]{1,0:T(8,128)(2,1)} %get-tuple-element.363.update), custom_call_target="tpu_custom_call" | custom-call | flops 1000 | bytes 1000 | tf_op jit(solution)/shard_map/apply_pieces/pallas_call | solution.py:878
  (949 shorter events, 759.1 us)
Async XLA Ops:
  100.9 83.5 %collective-permute-start.13 = (bf16[6,144,1152]{2,1,0:T(8,128)(2,1)}, bf16[6,144,1152]{2,1,0:T(8,128)(2,1)}, u32[]{:S(2)}, u32[]{:S(2)}) collective-permute-start(bf16[6,144,1152]{2,1,0:T(8,128)(2,1)} %get-tuple-element.206), channel_id=1, source_target_pairs={{0,8},{4,12},{8,0},{12,4},{16,24},{20,28},{24,16},{28,20},{1,9},{5... | collective-permute-start | bytes 5971976 | tf_op jit(solution)/shard_map/ppermute | solution.py:38
  102.6 74.2 %collective-permute-start.14 = (bf16[2,2,144,1152]{3,2,1,0:T(8,128)(2,1)}, bf16[2,2,144,1152]{3,2,1,0:T(8,128)(2,1)}, u32[]{:S(2)}, u32[]{:S(2)}) collective-permute-start(bf16[2,2,144,1152]{3,2,1,0:T(8,128)(2,1)} %pad_maximum_fusion.19), channel_id=1, source_target_pairs={{0,16},{4,20},{8,24},{12,28},{16,0},{20,4},{24,8},{28,12},{1,17},{... | collective-permute-start | bytes 3981320 | tf_op jit(solution)/shard_map/ppermute | solution.py:38
  151.4 109.6 %collective-permute-start.8 = (f32[2,2,3456]{2,1,0:T(2,128)S(1)}, f32[2,2,3456]{2,1,0:T(2,128)S(1)}, u32[]{:S(2)}, u32[]{:S(2)}) collective-permute-start(f32[2,2,3456]{2,1,0:T(2,128)S(1)} %stack.413), channel_id=1, source_target_pairs={{0,16},{4,20},{8,24},{12,28},{16,0},{20,4},{24,8},{28,12},{1,17},{... | collective-permute-start | bytes 165896 | tf_op jit(solution)/shard_map/ppermute | solution.py:38
  184.5 68.2 %collective-permute-start.22 = (bf16[2,4,144,1152]{3,2,1,0:T(8,128)(2,1)S(1)}, bf16[2,4,144,1152]{3,2,1,0:T(8,128)(2,1)S(1)}, u32[]{:S(2)}, u32[]{:S(2)}) collective-permute-start(bf16[2,4,144,1152]{3,2,1,0:T(8,128)(2,1)S(1)} %pad_maximum_fusion.7), channel_id=1, source_target_pairs={{0,2},{1,3},{2,0},{3,1},{4,6},{5,7},{6,4},{7,5},{8,10},{9,11},{10,... | collective-permute-start | bytes 7962632 | tf_op jit(solution)/shard_map/ppermute | solution.py:38
  186.6 68.0 %collective-permute-start.21 = (bf16[2,4,144,1152]{3,2,1,0:T(8,128)(2,1)S(1)}, bf16[2,4,144,1152]{3,2,1,0:T(8,128)(2,1)S(1)}, u32[]{:S(2)}, u32[]{:S(2)}) collective-permute-start(bf16[2,4,144,1152]{3,2,1,0:T(8,128)(2,1)S(1)} %pad_maximum_fusion.6.refs_11_.refs_3_.refs_6_.refs_4_), channel_id=1, source_target_pairs={{0,4},{4,0},{8,12},{12,8},{16,20},{20,16},{24,28},{28,24},{1,5},{5... | collective-permute-start | bytes 7962632 | tf_op jit(solution)/shard_map/ppermute | solution.py:38
  260.4 99.7 %collective-permute-start.31 = (bf16[6,4,144,1152]{3,2,1,0:T(8,128)(2,1)}, bf16[6,4,144,1152]{3,2,1,0:T(8,128)(2,1)}, u32[]{:S(2)}, u32[]{:S(2)}) collective-permute-start(bf16[6,4,144,1152]{3,2,1,0:T(8,128)(2,1)} %pad_maximum_fusion.1), channel_id=1, source_target_pairs={{0,1},{1,0},{2,3},{3,2},{4,5},{5,4},{6,7},{7,6},{8,9},{9,8},{10,11... | collective-permute-start | bytes 23887880 | tf_op jit(solution)/shard_map/ppermute | solution.py:38
  280.9 71.9 %collective-permute-start.30 = (bf16[2,4,144,1152]{3,2,1,0:T(8,128)(2,1)}, bf16[2,4,144,1152]{3,2,1,0:T(8,128)(2,1)}, u32[]{:S(2)}, u32[]{:S(2)}) collective-permute-start(bf16[2,4,144,1152]{3,2,1,0:T(8,128)(2,1)} %pad_maximum_fusion.10), channel_id=1, source_target_pairs={{0,2},{1,3},{2,0},{3,1},{4,6},{5,7},{6,4},{7,5},{8,10},{9,11},{10,... | collective-permute-start | bytes 7962632 | tf_op jit(solution)/shard_map/ppermute | solution.py:38
  281.7 71.2 %collective-permute-start.29 = (bf16[2,4,144,1152]{3,2,1,0:T(8,128)(2,1)}, bf16[2,4,144,1152]{3,2,1,0:T(8,128)(2,1)}, u32[]{:S(2)}, u32[]{:S(2)}) collective-permute-start(bf16[2,4,144,1152]{3,2,1,0:T(8,128)(2,1)} %pad_maximum_fusion.5.refs_9_.refs_4_.refs_7_.refs_12_), channel_id=1, source_target_pairs={{0,4},{4,0},{8,12},{12,8},{16,20},{20,16},{24,28},{28,24},{1,5},{5... | collective-permute-start | bytes 7962632 | tf_op jit(solution)/shard_map/ppermute | solution.py:38
  283.1 66.1 %collective-permute-start.28 = (bf16[2,2,144,1152]{3,2,1,0:T(8,128)(2,1)}, bf16[2,2,144,1152]{3,2,1,0:T(8,128)(2,1)}, u32[]{:S(2)}, u32[]{:S(2)}) collective-permute-start(bf16[2,2,144,1152]{3,2,1,0:T(8,128)(2,1)} %get-tuple-element.215), channel_id=1, source_target_pairs={{0,16},{4,20},{8,24},{12,28},{16,0},{20,4},{24,8},{28,12},{1,17},{... | collective-permute-start | bytes 3981320 | tf_op jit(solution)/shard_map/ppermute | solution.py:38
  360.1 72.4 %collective-permute-start.40 = (bf16[7,4,144,1152]{3,2,1,0:T(8,128)(2,1)}, bf16[7,4,144,1152]{3,2,1,0:T(8,128)(2,1)}, u32[]{:S(2)}, u32[]{:S(2)}) collective-permute-start(bf16[7,4,144,1152]{3,2,1,0:T(8,128)(2,1)} %pad_maximum_fusion), channel_id=1, source_target_pairs={{0,1},{1,0},{2,3},{3,2},{4,5},{5,4},{6,7},{7,6},{8,9},{9,8},{10,11... | collective-permute-start | bytes 27869192 | tf_op jit(solution)/shard_map/ppermute | solution.py:38
  365.9 66.6 %collective-permute-start.39 = (bf16[2,4,144,1152]{3,2,1,0:T(8,128)(2,1)}, bf16[2,4,144,1152]{3,2,1,0:T(8,128)(2,1)}, u32[]{:S(2)}, u32[]{:S(2)}) collective-permute-start(bf16[2,4,144,1152]{3,2,1,0:T(8,128)(2,1)} %pad_maximum_fusion.12), channel_id=1, source_target_pairs={{0,2},{1,3},{2,0},{3,1},{4,6},{5,7},{6,4},{7,5},{8,10},{9,11},{10,... | collective-permute-start | bytes 7962632 | tf_op jit(solution)/shard_map/ppermute | solution.py:38
  366.4 66.1 %collective-permute-start.38 = (bf16[2,4,144,1152]{3,2,1,0:T(8,128)(2,1)}, bf16[2,4,144,1152]{3,2,1,0:T(8,128)(2,1)}, u32[]{:S(2)}, u32[]{:S(2)}) collective-permute-start(bf16[2,4,144,1152]{3,2,1,0:T(8,128)(2,1)} %pad_maximum_fusion.9.refs_3_.refs_6_), channel_id=1, source_target_pairs={{0,4},{4,0},{8,12},{12,8},{16,20},{20,16},{24,28},{28,24},{1,5},{5... | collective-permute-start | bytes 7962632 | tf_op jit(solution)/shard_map/ppermute | solution.py:38
  702.9 66.8 %collective-permute-start.55 = (bf16[2,4,144,1152]{3,2,0,1:T(8,128)(2,1)}, bf16[2,4,144,1152]{3,2,0,1:T(8,128)(2,1)}, u32[]{:S(2)}, u32[]{:S(2)}) collective-permute-start(bf16[2,4,144,1152]{3,2,0,1:T(8,128)(2,1)} %copy.491), channel_id=1, source_target_pairs={{0,4},{4,0},{8,12},{12,8},{16,20},{20,16},{24,28},{28,24},{1,5},{5... | collective-permute-start | bytes 7962632 | tf_op jit(solution)/shard_map/ppermute | solution.py:38
  771.8 65.8 %collective-permute-start.58 = (bf16[2,4,144,1152]{3,2,0,1:T(8,128)(2,1)S(1)}, bf16[2,4,144,1152]{3,2,0,1:T(8,128)(2,1)}, u32[]{:S(2)}, u32[]{:S(2)}) collective-permute-start(bf16[2,4,144,1152]{3,2,0,1:T(8,128)(2,1)S(1)} %copy.493), channel_id=1, source_target_pairs={{0,4},{4,0},{8,12},{12,8},{16,20},{20,16},{24,28},{28,24},{1,5},{5... | collective-permute-start | bytes 7962632 | tf_op jit(solution)/shard_map/ppermute | solution.py:38
  846.5 64.9 %collective-permute-start.62 = (bf16[2,4,144,1152]{3,2,0,1:T(8,128)(2,1)}, bf16[2,4,144,1152]{3,2,0,1:T(8,128)(2,1)}, u32[]{:S(2)}, u32[]{:S(2)}) collective-permute-start(bf16[2,4,144,1152]{3,2,0,1:T(8,128)(2,1)} %copy.495), channel_id=1, source_target_pairs={{0,4},{4,0},{8,12},{12,8},{16,20},{20,16},{24,28},{28,24},{1,5},{5... | collective-permute-start | bytes 7962632 | tf_op jit(solution)/shard_map/ppermute | solution.py:38
  859.6 65.0 %collective-permute-start.106 = (f32[1]{0:T(128)}, f32[1]{0:T(128)}, u32[]{:S(2)}, u32[]{:S(2)}) collective-permute-start(f32[1]{0:T(128)} %bitcast.207), channel_id=1, source_target_pairs={{0,1},{1,0},{2,3},{3,2},{4,5},{5,4},{6,7},{7,6},{8,9},{9,8},{10,11... | collective-permute-start | bytes 20 | tf_op jit(solution)/shard_map/ppermute | solution.py:38
  913.1 67.9 %collective-permute-start.66 = (bf16[2,4,144,1152]{3,2,0,1:T(8,128)(2,1)}, bf16[2,4,144,1152]{3,2,0,1:T(8,128)(2,1)}, u32[]{:S(2)}, u32[]{:S(2)}) collective-permute-start(bf16[2,4,144,1152]{3,2,0,1:T(8,128)(2,1)} %copy.497), channel_id=1, source_target_pairs={{0,4},{4,0},{8,12},{12,8},{16,20},{20,16},{24,28},{28,24},{1,5},{5... | collective-permute-start | bytes 7962632 | tf_op jit(solution)/shard_map/ppermute | solution.py:38
  918.3 62.7 %collective-permute-start.67 = (bf16[2,2,144,1152]{3,2,0,1:T(8,128)(2,1)}, bf16[2,2,144,1152]{3,2,0,1:T(8,128)(2,1)}, u32[]{:S(2)}, u32[]{:S(2)}) collective-permute-start(bf16[2,2,144,1152]{3,2,0,1:T(8,128)(2,1)} %get-tuple-element.574), channel_id=1, source_target_pairs={{0,16},{4,20},{8,24},{12,28},{16,0},{20,4},{24,8},{28,12},{1,17},{... | collective-permute-start | bytes 3981320 | tf_op jit(solution)/shard_map/ppermute | solution.py:38
  1005.4 64.9 %collective-permute-start.84 = (bf16[2,2,144,1152]{3,2,0,1:T(8,128)(2,1)}, bf16[2,2,144,1152]{3,2,0,1:T(8,128)(2,1)}, u32[]{:S(2)}, u32[]{:S(2)}) collective-permute-start(bf16[2,2,144,1152]{3,2,0,1:T(8,128)(2,1)} %get-tuple-element.572), channel_id=1, source_target_pairs={{0,16},{4,20},{8,24},{12,28},{16,0},{20,4},{24,8},{28,12},{1,17},{... | collective-permute-start | bytes 3981320 | tf_op jit(solution)/shard_map/ppermute | solution.py:38
  1029.3 76.5 %collective-permute-start.83 = (bf16[2,4,144,1152]{3,2,0,1:T(8,128)(2,1)}, bf16[2,4,144,1152]{3,2,0,1:T(8,128)(2,1)}, u32[]{:S(2)}, u32[]{:S(2)}) collective-permute-start(bf16[2,4,144,1152]{3,2,0,1:T(8,128)(2,1)} %copy.503), channel_id=1, source_target_pairs={{0,4},{4,0},{8,12},{12,8},{16,20},{20,16},{24,28},{28,24},{1,5},{5... | collective-permute-start | bytes 7962632 | tf_op jit(solution)/shard_map/ppermute | solution.py:38
  1034.9 70.8 %collective-permute-start.85 = (bf16[6,144,1152]{2,1,0:T(8,128)(2,1)}, bf16[6,144,1152]{2,1,0:T(8,128)(2,1)}, u32[]{:S(2)}, u32[]{:S(2)}) collective-permute-start(bf16[6,144,1152]{2,1,0:T(8,128)(2,1)} %pad_maximum_fusion.15), channel_id=1, source_target_pairs={{0,2},{1,3},{2,0},{3,1},{4,6},{5,7},{6,4},{7,5},{8,10},{9,11},{10,... | collective-permute-start | bytes 5971976 | tf_op jit(solution)/shard_map/ppermute | solution.py:38
  1082.6 69.9 %collective-permute-start.93 = (bf16[1,2,144,1152]{3,2,1,0:T(8,128)(2,1)}, bf16[1,2,144,1152]{3,2,1,0:T(8,128)(2,1)}, u32[]{:S(2)}, u32[]{:S(2)}) collective-permute-start(bf16[1,2,144,1152]{3,2,1,0:T(8,128)(2,1)} %get-tuple-element.602), channel_id=1, source_target_pairs={{0,16},{4,20},{8,24},{12,28},{16,0},{20,4},{24,8},{28,12},{1,17},{... | collective-permute-start | bytes 1990664 | tf_op jit(solution)/shard_map/ppermute | solution.py:38
  1115.2 65.2 %collective-permute-start.94 = (bf16[2,2,144,1152]{3,2,0,1:T(8,128)(2,1)}, bf16[2,2,144,1152]{3,2,0,1:T(8,128)(2,1)}, u32[]{:S(2)}, u32[]{:S(2)}) collective-permute-start(bf16[2,2,144,1152]{3,2,0,1:T(8,128)(2,1)} %get-tuple-element.570), channel_id=1, source_target_pairs={{0,16},{4,20},{8,24},{12,28},{16,0},{20,4},{24,8},{28,12},{1,17},{... | collective-permute-start | bytes 3981320 | tf_op jit(solution)/shard_map/ppermute | solution.py:38
  1129.1 84.2 %collective-permute-start.105 = (bf16[6,144,1152]{2,1,0:T(8,128)(2,1)S(1)}, bf16[6,144,1152]{2,1,0:T(8,128)(2,1)}, u32[]{:S(2)}, u32[]{:S(2)}) collective-permute-start(bf16[6,144,1152]{2,1,0:T(8,128)(2,1)S(1)} %get-tuple-element.551.refs_3_), channel_id=1, source_target_pairs={{0,1},{1,0},{2,3},{3,2},{4,5},{5,4},{6,7},{7,6},{8,9},{9,8},{10,11... | collective-permute-start | bytes 5971976 | tf_op jit(solution)/shard_map/ppermute | solution.py:38
  (240 other events, 4571.6 us)
